TPU v7x, 128 devices: a whole 4x4x4 slice. The times are simulated.
128 devices in a mesh: tm: 16 (over x, y), ha: 8 (over z, core).
Axes of the slice: x: 4, y: 4, z: 4, core: 2. Of those that a mesh axis runs over, the one named last changes fastest.
Arguments:
- tokens: bfloat16 [32, 8, 16, 16, 1536], P('tm', 'ha'), may hold values from -12 to 12
- projection: bfloat16 [1536, 2304], replicated, may hold values from -0.15309311 to 0.15309311
- norm_gain: float32 [2, 768], replicated, may hold values from 0.4 to 6.25, as said below
- modulation: float32 [50, 2, 1536], replicated, may hold values from -3 to 3
- levels: int32 [32], P('tm'), may hold values from 0 to 49
- frame_order: int32 [32], replicated, may hold values from 0 to 31, each once
Outputs:
- attended: bfloat16 [32, 8, 16, 16, 768], P('tm', 'ha')
Inputs may be any that keep to these rules, and one draw needn't show every extreme that they name: `norm_gain`: positive gains. `frame_order`: each number of 0 to 31 once.
All inputs are finite; a program needn't handle non-finite values.
Results may differ from a plain program's by a relative error of at most 0.0059.
Values may be sent and summed in bfloat16 or wider, within the bound.
No kernel may reach another device: no remote copies, remote signals or barrier semaphores. Data moves between devices by JAX's collectives and lax.ppermute only.
A program may use at most 192 MiB of HBM per device.

v0:
```python
import math

import jax
import jax.numpy as jnp
import numpy as np
from jax import lax
from jax.sharding import PartitionSpec as P

D = 1536
HEADS = 6
HD = 128
TILE = 16
PAD = 2
TROWS = 2
LEVELS = 50


LOWEST = -1e30
OFFSETS = ((-1, -1), (-1, 0), (-1, 1), (0, -1), (0, 1), (1, -1), (1, 0), (1, 1))


def from_behind(value, axis, steps):
    count = lax.axis_size(axis)
    initial, last = (max(0, -steps), min(count, count - steps))
    return lax.ppermute(value, axis, [(source, source + steps) for source in range(initial, last)])


def layer_input(tokens, levels, modulation):
    values = tokens.astype(jnp.float32)
    average = jnp.mean(values, axis=-1, keepdims=True)
    centred = values - average
    spread = jnp.mean(centred * centred, axis=-1, keepdims=True)
    normed = centred * lax.rsqrt(spread + 1e-06)
    onehot = (levels[:, None] == jnp.arange(LEVELS, dtype=jnp.int32)[None, :]).astype(jnp.float32)
    chosen = jnp.dot(onehot, modulation.reshape(LEVELS, 2 * D), precision=lax.Precision.HIGHEST)
    shifts = chosen[:, :D].reshape(-1, 1, 1, 1, D)
    scales = chosen[:, D:].reshape(-1, 1, 1, 1, D)
    return (normed * (1.0 + scales) + shifts).astype(jnp.bfloat16)


def root_norm(values, gains):
    return (
        values * lax.rsqrt(jnp.mean(values * values, axis=-1, keepdims=True) + 1e-06) * gains
    ).astype(jnp.bfloat16)


def project_tokens(tokens, projection, norm_gain, modulation, levels):
    modulated = layer_input(tokens, levels, modulation)
    inner_width = projection.shape[1] // 3
    projected = jnp.dot(modulated.reshape(-1, D), projection, preferred_element_type=jnp.float32)
    queries = root_norm(projected[:, :inner_width], norm_gain[0])
    key_rows = root_norm(projected[:, inner_width : 2 * inner_width], norm_gain[1])
    values = projected[:, 2 * inner_width :].astype(jnp.bfloat16)
    out_shape = tokens.shape[:-1] + (inner_width,)
    return (
        queries.reshape(out_shape),
        jnp.concatenate([key_rows.reshape(out_shape), values.reshape(out_shape)], axis=-1),
    )


def step_range(step):
    if step < 0:
        return np.arange(-PAD, 0)
    if step > 0:
        return np.arange(TILE, TILE + PAD)
    return np.arange(0, TILE)


def window_offsets():
    row_parts = []
    col_parts = []
    pairs = ((0, 0),) + OFFSETS
    for row_step, col_step in pairs:
        rows_here = step_range(row_step)
        cols_here = step_range(col_step)
        row_parts.append(np.repeat(rows_here, cols_here.shape[0]))
        col_parts.append(np.tile(cols_here, rows_here.shape[0]))
    return (np.concatenate(row_parts).astype(np.int32), np.concatenate(col_parts).astype(np.int32))


def rim_piece(tile_kv, row_step, col_step):
    sliced = tile_kv
    if row_step < 0:
        sliced = sliced[:, TILE - PAD :]
    elif row_step > 0:
        sliced = sliced[:, :PAD]
    if col_step < 0:
        sliced = sliced[:, :, TILE - PAD :]
    elif col_step > 0:
        sliced = sliced[:, :, :PAD]
    return sliced


def assemble(center, rim_list):
    width = center.shape[-1]
    lead = center.shape[0]
    flat_parts = [center.reshape(lead, -1, width)] + [
        piece_rim.reshape(lead, -1, width) for piece_rim in rim_list
    ]
    return jnp.concatenate(flat_parts, axis=1)


def shards(tokens, projection, norm_gain, modulation, levels, frame_order):
    queries, keys_values = project_tokens(tokens, projection, norm_gain, modulation, levels)
    local_frames = queries.shape[0]
    query_count = TILE * TILE
    score_scale = 1.0 / math.sqrt(HD)
    query_tiles = queries.reshape(local_frames, query_count, HEADS, HD)
    tile_kv = keys_values.reshape(local_frames, TILE, TILE, 2 * HEADS * HD)
    tile_cols = lax.axis_size("ha") // TROWS
    position = lax.axis_index("ha")
    row_offsets, col_offsets = window_offsets()
    key_count = row_offsets.shape[0]
    row_ids = position // tile_cols * TILE + jnp.asarray(row_offsets)
    col_ids = position % tile_cols * TILE + jnp.asarray(col_offsets)
    window_inside = (
        (row_ids >= 0) & (row_ids < TROWS * TILE) & (col_ids >= 0) & (col_ids < tile_cols * TILE)
    )
    own_order = lax.dynamic_slice_in_dim(
        frame_order, lax.axis_index("tm") * local_frames, local_frames
    )

    def attend_group(state_now, window, key_order):
        visible = key_order[None, :] <= own_order[:, None]
        maxima, totals, accumulated = state_now
        window_kv = window.reshape(window.shape[0], key_count, 2, HEADS, HD)
        scores = (
            jnp.einsum(
                "fqhd,gkhd->fqhgk",
                query_tiles,
                window_kv[:, :, 0],
                preferred_element_type=jnp.float32,
            )
            * score_scale
        )
        allowed = visible[:, None, None, :, None] & window_inside[None, None, None, None, :]
        newest = jnp.maximum(maxima, jnp.max(jnp.where(allowed, scores, LOWEST), axis=(3, 4)))
        rescale = jnp.exp(maxima - newest)
        exp_scores = jnp.where(allowed, jnp.exp(scores - newest[..., None, None]), 0.0)
        totals = rescale * totals + jnp.sum(exp_scores, axis=(3, 4))
        product = jnp.einsum(
            "fqhgk,gkhd->fqhd",
            exp_scores.astype(jnp.bfloat16),
            window_kv[:, :, 1],
            preferred_element_type=jnp.float32,
        )
        accumulated = rescale[..., None] * accumulated + product
        return (newest, totals, accumulated)

    stat_shape = (local_frames, query_count, HEADS)
    initial = (
        jnp.full(stat_shape, LOWEST, jnp.float32),
        jnp.zeros(stat_shape, jnp.float32),
        jnp.zeros(stat_shape + (HD,), jnp.float32),
    )
    rim_list = [
        from_behind(
            rim_piece(tile_kv, row_step, col_step), "ha", -(row_step * tile_cols + col_step)
        )
        for row_step, col_step in OFFSETS
    ]
    own_window = assemble(tile_kv, rim_list)
    state_now = initial
    arrived = lax.all_gather(own_window, "tm", axis=0, tiled=True)
    grouped = arrived.reshape((-1, local_frames) + arrived.shape[1:])
    orders = frame_order.reshape(-1, local_frames)

    def scan_step(carried, scan_item):
        return (attend_group(carried, scan_item[0], scan_item[1]), None)

    state_now, _ = lax.scan(scan_step, state_now, (grouped, orders))
    totals = state_now[1]
    accumulated = state_now[2]
    output = accumulated / totals[..., None]
    output = output.reshape(local_frames, 1, TILE, TILE, HEADS * HD)
    return output.astype(jnp.bfloat16)


def solution(mesh):
    in_specs = (P("tm", "ha", None, None, None), P(), P(), P(), P("tm"), P())
    out_specs = P("tm", "ha", None, None, None)
    return jax.shard_map(shards, mesh=mesh, in_specs=in_specs, out_specs=out_specs, check_vma=False)
```

profile of v0, /device:TPU:1, one launch (start us, length us, event | category | flops | bytes accessed | tf_op | source)
XLA Modules:
  0.0 713.5 jit_solution(11161908738234044659)
XLA Ops:
  16.9 7.0 collective-permute-start
  34.5 7.0 collective-permute-start.1
  51.7 16.9 %concatenate.17 = bf16[2,400,1536]{2,1,0:T(8,128)(2,1)} concatenate(bf16[2,256,1536]{2,1,0:T(8,128)(2,1)S(1)} %pad_maximum_fusion, bf16[2,4,1536]{2,1,0:T(4,128)(2,1)} %reshape.158, bf16[2,32,1536]{2,1,0:T(8,128)(2,1)S(1)} %bitcast.91, bf16[2,4,1536]{2,1,0:T(4,128)(2,1)} %reshape.160, bf16[2,32,1536]{2,1,0:T(8,128)(2,1)S(1)} %reshape.161, bf16[2,32,1536]{2,1,0:T(8,128)(2,1)S(1)} %reshape.162, ...), dimensions={1} | concatenate | bytes 4915200 | tf_op jit(solution)/shard_map/concatenate | solution.py:100
  70.8 224.8 %all-gather.2.cloned.1.call-done = bf16[32,400,1536]{2,1,0:T(8,128)(2,1)} async-done(((bf16[2,400,1536]{2,1,0:T(8,128)(2,1)}), bf16[32,400,1536]{2,1,0:T(8,128)(2,1)}) %all-gather.2.cloned.1.call-update) | async-done | bytes 39321616 | tf_op jit(solution)/shard_map/all_gather | solution.py:164
  295.7 406.9 %while.15 = (s32[]{:T(128)}, f32[2,256,6]{1,0,2:T(2,128)S(1)}, f32[2,256,6]{1,0,2:T(2,128)S(1)}, f32[2,256,6,128]{1,3,0,2:T(8,128)}, s32[16,2]{1,0:T(8,128)S(1)}...) while((s32[]{:T(128)}, f32[2,256,6]{1,0,2:T(2,128)S(1)}, ...), condition=%wide.region_7.8_spmd.clone, body=%wide.region_4.7_spmd.clone.sunk | while | flops 1286524928 | bytes 110799344 | solution.py:171
  299.1 4.9 reshape.176
  310.5 5.0 fusion.55
  324.6 4.9 reshape.176
  335.9 5.0 fusion.55
  350.0 4.9 reshape.176
  361.4 5.0 fusion.55
  386.8 5.0 fusion.55
  412.2 5.0 fusion.55
  437.7 5.0 fusion.55
  463.1 5.0 fusion.55
  488.5 5.0 fusion.55
  514.0 5.0 fusion.55
  539.4 5.0 fusion.55
  564.8 5.0 fusion.55
  590.3 5.0 fusion.55
  615.7 5.0 fusion.55
  641.1 5.0 fusion.55
  666.6 5.0 fusion.55
  692.0 5.0 fusion.55
  (421 shorter events, 347.3 us)
Async XLA Ops:
  6.5 289.1 %all-gather.2.cloned.1.call-start = ((), (), s32[]{:S(2)}) async-start(), calls=%async_computation | async-start | bytes 41779200 | tf_op jit(solution)/shard_map/all_gather | solution.py:164
  16.9 14.8 %collective-permute-start = (bf16[2,2,2,1536]{3,2,1,0:T(2,128)(2,1)S(1)}, bf16[2,2,2,1536]{3,2,1,0:T(2,128)(2,1)S(1)}, u32[]{:S(2)}, u32[]{:S(2)}) collective-permute-start(bf16[2,2,2,1536]{3,2,1,0:T(2,128)(2,1)S(1)} %get-tuple-element.157), channel_id=1, source_target_pairs={{0,5},{1,6},{2,7},{8,13},{9,14},{10,15},{16,21},{17,22},{18,23},{2... | collective-permute-start | bytes 73736 | tf_op jit(solution)/shard_map/ppermute | solution.py:25
  24.0 9.9 %collective-permute-start.2 = (bf16[2,2,2,1536]{3,2,1,0:T(2,128)(2,1)S(1)}, bf16[2,2,2,1536]{3,2,1,0:T(2,128)(2,1)S(1)}, u32[]{:S(2)}, u32[]{:S(2)}) collective-permute-start(bf16[2,2,2,1536]{3,2,1,0:T(2,128)(2,1)S(1)} %get-tuple-element.156), channel_id=1, source_target_pairs={{0,3},{1,4},{2,5},{3,6},{4,7},{8,11},{9,12},{10,13},{11,14},{12,15... | collective-permute-start | bytes 73736 | tf_op jit(solution)/shard_map/ppermute | solution.py:25
  25.3 16.3 %collective-permute-start.5 = (bf16[2,2,2,1536]{3,2,1,0:T(2,128)(2,1)S(1)}, bf16[2,2,2,1536]{3,2,1,0:T(2,128)(2,1)S(1)}, u32[]{:S(2)}, u32[]{:S(2)}) collective-permute-start(bf16[2,2,2,1536]{3,2,1,0:T(2,128)(2,1)S(1)} %get-tuple-element.155), channel_id=1, source_target_pairs={{3,0},{4,1},{5,2},{6,3},{7,4},{11,8},{12,9},{13,10},{14,11},{15,12... | collective-permute-start | bytes 73736 | tf_op jit(solution)/shard_map/ppermute | solution.py:25
  26.6 21.3 %collective-permute-start.7 = (bf16[2,2,2,1536]{3,2,1,0:T(2,128)(2,1)}, bf16[2,2,2,1536]{3,2,1,0:T(2,128)(2,1)}, u32[]{:S(2)}, u32[]{:S(2)}) collective-permute-start(bf16[2,2,2,1536]{3,2,1,0:T(2,128)(2,1)} %get-tuple-element.154), channel_id=1, source_target_pairs={{5,0},{6,1},{7,2},{13,8},{14,9},{15,10},{21,16},{22,17},{23,18},{2... | collective-permute-start | bytes 73736 | tf_op jit(solution)/shard_map/ppermute | solution.py:25
  28.8 20.4 %collective-permute-start.3 = (bf16[2,16,2,1536]{3,2,1,0:T(2,128)(2,1)S(1)}, bf16[2,16,2,1536]{3,2,1,0:T(2,128)(2,1)S(1)}, u32[]{:S(2)}, u32[]{:S(2)}) collective-permute-start(bf16[2,16,2,1536]{3,2,1,0:T(2,128)(2,1)S(1)} %get-tuple-element.161), channel_id=1, source_target_pairs={{0,1},{1,2},{2,3},{3,4},{4,5},{5,6},{6,7},{8,9},{9,10},{10,11},{11... | collective-permute-start | bytes 589832 | tf_op jit(solution)/shard_map/ppermute | solution.py:25
  31.8 17.6 %collective-permute-start.4 = (bf16[2,16,2,1536]{3,2,1,0:T(2,128)(2,1)}, bf16[2,16,2,1536]{3,2,1,0:T(2,128)(2,1)S(1)}, u32[]{:S(2)}, u32[]{:S(2)}) collective-permute-start(bf16[2,16,2,1536]{3,2,1,0:T(2,128)(2,1)} %get-tuple-element.160), channel_id=1, source_target_pairs={{1,0},{2,1},{3,2},{4,3},{5,4},{6,5},{7,6},{9,8},{10,9},{11,10},{12... | collective-permute-start | bytes 589832 | tf_op jit(solution)/shard_map/ppermute | solution.py:25
  34.5 14.9 %collective-permute-start.1 = (bf16[2,2,16,1536]{3,2,1,0:T(8,128)(2,1)}, bf16[2,2,16,1536]{3,2,1,0:T(8,128)(2,1)S(1)}, u32[]{:S(2)}, u32[]{:S(2)}) collective-permute-start(bf16[2,2,16,1536]{3,2,1,0:T(8,128)(2,1)} %get-tuple-element.159), channel_id=1, source_target_pairs={{0,4},{1,5},{2,6},{3,7},{8,12},{9,13},{10,14},{11,15},{16,20},{17,... | collective-permute-start | bytes 589832 | tf_op jit(solution)/shard_map/ppermute | solution.py:25
  42.2 9.6 %collective-permute-start.6 = (bf16[2,2,16,1536]{3,2,1,0:T(8,128)(2,1)S(1)}, bf16[2,2,16,1536]{3,2,1,0:T(8,128)(2,1)S(1)}, u32[]{:S(2)}, u32[]{:S(2)}) collective-permute-start(bf16[2,2,16,1536]{3,2,1,0:T(8,128)(2,1)S(1)} %get-tuple-element.158), channel_id=1, source_target_pairs={{4,0},{5,1},{6,2},{7,3},{12,8},{13,9},{14,10},{15,11},{20,16},{21,... | collective-permute-start | bytes 589832 | tf_op jit(solution)/shard_map/ppermute | solution.py:25
  68.7 227.0 %copy-start.6 = (s32[400]{0:T(512)S(1)}, s32[400]{0:T(512)}, u32[]{:S(2)}) copy-start(s32[400]{0:T(512)} %constant.85.clone.9) | copy-start | bytes 4804
  68.7 227.0 %copy-start.7 = (s32[400]{0:T(512)S(1)}, s32[400]{0:T(512)}, u32[]{:S(2)}) copy-start(s32[400]{0:T(512)} %constant.86.clone.9) | copy-start | bytes 4804
  305.8 9.8 %copy-start.4 = (f32[2,256,6,128]{1,3,0,2:T(8,128)S(1)}, f32[2,256,6,128]{1,3,0,2:T(8,128)}, u32[]{:S(2)}) copy-start(f32[2,256,6,128]{1,3,0,2:T(8,128)} %get-tuple-element.256) | copy-start | bytes 4718596 | tf_op jit(solution)/shard_map/while
  331.3 9.8 %copy-start.4 = (f32[2,256,6,128]{1,3,0,2:T(8,128)S(1)}, f32[2,256,6,128]{1,3,0,2:T(8,128)}, u32[]{:S(2)}) copy-start(f32[2,256,6,128]{1,3,0,2:T(8,128)} %get-tuple-element.256) | copy-start | bytes 4718596 | tf_op jit(solution)/shard_map/while
  356.7 9.8 %copy-start.4 = (f32[2,256,6,128]{1,3,0,2:T(8,128)S(1)}, f32[2,256,6,128]{1,3,0,2:T(8,128)}, u32[]{:S(2)}) copy-start(f32[2,256,6,128]{1,3,0,2:T(8,128)} %get-tuple-element.256) | copy-start | bytes 4718596 | tf_op jit(solution)/shard_map/while
  382.1 9.8 %copy-start.4 = (f32[2,256,6,128]{1,3,0,2:T(8,128)S(1)}, f32[2,256,6,128]{1,3,0,2:T(8,128)}, u32[]{:S(2)}) copy-start(f32[2,256,6,128]{1,3,0,2:T(8,128)} %get-tuple-element.256) | copy-start | bytes 4718596 | tf_op jit(solution)/shard_map/while
  407.6 9.8 %copy-start.4 = (f32[2,256,6,128]{1,3,0,2:T(8,128)S(1)}, f32[2,256,6,128]{1,3,0,2:T(8,128)}, u32[]{:S(2)}) copy-start(f32[2,256,6,128]{1,3,0,2:T(8,128)} %get-tuple-element.256) | copy-start | bytes 4718596 | tf_op jit(solution)/shard_map/while
  433.0 9.8 %copy-start.4 = (f32[2,256,6,128]{1,3,0,2:T(8,128)S(1)}, f32[2,256,6,128]{1,3,0,2:T(8,128)}, u32[]{:S(2)}) copy-start(f32[2,256,6,128]{1,3,0,2:T(8,128)} %get-tuple-element.256) | copy-start | bytes 4718596 | tf_op jit(solution)/shard_map/while
  458.4 9.8 %copy-start.4 = (f32[2,256,6,128]{1,3,0,2:T(8,128)S(1)}, f32[2,256,6,128]{1,3,0,2:T(8,128)}, u32[]{:S(2)}) copy-start(f32[2,256,6,128]{1,3,0,2:T(8,128)} %get-tuple-element.256) | copy-start | bytes 4718596 | tf_op jit(solution)/shard_map/while
  483.9 9.8 %copy-start.4 = (f32[2,256,6,128]{1,3,0,2:T(8,128)S(1)}, f32[2,256,6,128]{1,3,0,2:T(8,128)}, u32[]{:S(2)}) copy-start(f32[2,256,6,128]{1,3,0,2:T(8,128)} %get-tuple-element.256) | copy-start | bytes 4718596 | tf_op jit(solution)/shard_map/while
  509.3 9.8 %copy-start.4 = (f32[2,256,6,128]{1,3,0,2:T(8,128)S(1)}, f32[2,256,6,128]{1,3,0,2:T(8,128)}, u32[]{:S(2)}) copy-start(f32[2,256,6,128]{1,3,0,2:T(8,128)} %get-tuple-element.256) | copy-start | bytes 4718596 | tf_op jit(solution)/shard_map/while
  534.7 9.8 %copy-start.4 = (f32[2,256,6,128]{1,3,0,2:T(8,128)S(1)}, f32[2,256,6,128]{1,3,0,2:T(8,128)}, u32[]{:S(2)}) copy-start(f32[2,256,6,128]{1,3,0,2:T(8,128)} %get-tuple-element.256) | copy-start | bytes 4718596 | tf_op jit(solution)/shard_map/while
  560.2 9.8 %copy-start.4 = (f32[2,256,6,128]{1,3,0,2:T(8,128)S(1)}, f32[2,256,6,128]{1,3,0,2:T(8,128)}, u32[]{:S(2)}) copy-start(f32[2,256,6,128]{1,3,0,2:T(8,128)} %get-tuple-element.256) | copy-start | bytes 4718596 | tf_op jit(solution)/shard_map/while
  585.6 9.8 %copy-start.4 = (f32[2,256,6,128]{1,3,0,2:T(8,128)S(1)}, f32[2,256,6,128]{1,3,0,2:T(8,128)}, u32[]{:S(2)}) copy-start(f32[2,256,6,128]{1,3,0,2:T(8,128)} %get-tuple-element.256) | copy-start | bytes 4718596 | tf_op jit(solution)/shard_map/while
  687.3 9.8 %copy-start.4 = (f32[2,256,6,128]{1,3,0,2:T(8,128)S(1)}, f32[2,256,6,128]{1,3,0,2:T(8,128)}, u32[]{:S(2)}) copy-start(f32[2,256,6,128]{1,3,0,2:T(8,128)} %get-tuple-element.256) | copy-start | bytes 4718596 | tf_op jit(solution)/shard_map/while
  (75 other events, 352.6 us)
Sparse Core Ops, SparseCore 0:
  68.8 226.8 all-gather.1
where the time goes:
time: 717 us; the launch traced here: 714 us
  local copies, waits for them, and re-layouts  237 us (33%)
  waiting for transfers between devices  227 us (32%)
  matrix products  122 us (17%)
  other arithmetic  88 us (12%)
  starting transfers between devices  23.7 us (3%)
  between operations  13.8 us (2%)
    all_gather x1, waiting for transfers between devices, shards(): arrived = lax.all_gather(own_window, 'tm', axis=0, tiled=True)  225 us
    reduce_sum x16, other arithmetic, attend_group(): totals = rescale * totals + jnp.sum(exp_scores, axis=(3, 4))  80.7 us
    reshape x16, local copies, waits for them, and re-layouts, attend_group(): window_kv = window.reshape(window.shape[0], key_count, 2, HEADS, HD)  78.4 us
    dot_general x16, matrix products, attend_group(): jnp.einsum('fqhd,gkhd->fqhgk', query_tiles, window_kv[:, :, 0], preferred...  74.3 us
    dynamic_slice x16, local copies, waits for them, and re-layouts, shards(): state_now, _ = lax.scan(scan_step, state_now, (grouped, orders))  52.4 us
    dot_general x16, matrix products, attend_group(): jnp.einsum('fqhgk,gkhd->fqhd', exp_scores.astype(jnp.bfloat16), window_kv...  44 us
    while x176, local copies, waits for them, and re-layouts  43.7 us
    slice x16, local copies, waits for them, and re-layouts, attend_group(): window_kv[:, :, 1]  28.8 us
  transfers between devices with their start and end apart: 9, of which 2 were waited for; matrix products, arithmetic and copies ran while one was open for 1% of the time, Pallas kernels for 0%

commit v1 on v0

v1 whole, which is shorter than its diff:
```python
import functools
import math

import jax
import jax.numpy as jnp
from jax import lax
from jax.experimental import pallas as pl
from jax.experimental.pallas import tpu as pltpu
from jax.sharding import PartitionSpec as P

D = 1536
HEADS = 6
HD = 128
TILE = 16
PAD = 2
TOKENS = TILE * TILE
QD = HEADS * HD
FRAMES = 32
CHIPS = 16
SLOTS = 8
RIM = 112
LOWEST = -1e30
LOG2E = math.log2(math.e)
SCALE = LOG2E / math.sqrt(HD)
AXES = ("tm", "ha")


def device_pairs(target):
    pairs = []
    for tm in range(CHIPS):
        for ha in range(8):
            goal = target(tm, ha // 2, ha % 2)
            if goal is not None:
                pairs.append((tm * 8 + ha, goal[0] * 8 + goal[1] * 2 + goal[2]))
    return pairs


def project_kernel(info, tokens, weights, gains, modulation, own, away, inputs):
    part = pl.program_id(0)
    step = pl.program_id(1)

    @pl.when(part == 0)
    def _():
        values = tokens[0].astype(jnp.float32)
        average = jnp.mean(values, axis=-1, keepdims=True)
        centred = values - average
        spread = jnp.mean(centred * centred, axis=-1, keepdims=True)
        normed = centred * lax.rsqrt(spread + 1e-06)
        shift = modulation[0, 0:1, :]
        scale = modulation[0, 1:2, :]
        inputs[step] = (normed * (1.0 + scale) + shift).astype(jnp.bfloat16)

    raw = jnp.dot(inputs[step], weights[...], preferred_element_type=jnp.float32)

    def put(result):
        result = result.astype(jnp.bfloat16)

        @pl.when(step == 0)
        def _():
            for head in range(HEADS):
                away[head, 0] = result[:, head * HD : (head + 1) * HD]

        @pl.when(step == 1)
        def _():
            for head in range(HEADS):
                own[head, 0] = result[:, head * HD : (head + 1) * HD]

    @pl.when(part < 2)
    def _():
        row = jnp.where(part == 0, gains[0:1, :], gains[1:2, :])
        put(raw * lax.rsqrt(jnp.mean(raw * raw, axis=-1, keepdims=True) + 1e-06) * row)

    @pl.when(part == 2)
    def _():
        put(raw)


def project(tokens, projection, norm_gain, modulation, levels, core):
    info = jnp.stack([core, levels[0], levels[1]])

    def frame(step, info):
        return info[0] + 1 - step - 2 * info[0] * (1 - step)

    return pl.pallas_call(
        project_kernel,
        grid_spec=pltpu.PrefetchScalarGridSpec(
            num_scalar_prefetch=1,
            grid=(3, 2),
            in_specs=[
                pl.BlockSpec((1, TOKENS, D), lambda p, s, info: (jnp.where(p == 0, frame(s, info), frame(1, info)), 0, 0)),
                pl.BlockSpec((D, QD), lambda p, s, info: (0, p)),
                pl.BlockSpec((2, QD), lambda p, s, info: (0, 0)),
                pl.BlockSpec((1, 2, D), lambda p, s, info: (info[1 + frame(s, info)], 0, 0)),
            ],
            out_specs=[
                pl.BlockSpec((SLOTS, 1, TOKENS, HD), lambda p, s, info: (info[0], p, 0, 0)),
                pl.BlockSpec((SLOTS, 1, TOKENS, HD), lambda p, s, info: (0, p, 0, 0)),
            ],
            scratch_shapes=[pltpu.VMEM((2, TOKENS, D), jnp.bfloat16)],
        ),
        out_shape=[
            jax.ShapeDtypeStruct((CHIPS, 3, TOKENS, HD), jnp.bfloat16),
            jax.ShapeDtypeStruct((SLOTS, 3, TOKENS, HD), jnp.bfloat16),
        ],
        compiler_params=pltpu.CompilerParams(vmem_limit_bytes=48 * 1024 * 1024),
        name="project",
    )(info, tokens, projection, norm_gain, modulation)


def soft_step(query, keys, values, bias, state):
    top, total, mixed = state
    scores = lax.dot_general(query, keys, (((1,), (1,)), ((), ())), preferred_element_type=jnp.float32)
    if bias is not None:
        scores = scores + bias
    count = keys.shape[0]
    groups = count // HD
    highest = scores[:, :HD]
    for group in range(1, groups):
        highest = jnp.maximum(highest, scores[:, group * HD : (group + 1) * HD])
    highest = jnp.max(highest, axis=-1, keepdims=True) * SCALE
    newest = jnp.maximum(top, jnp.broadcast_to(highest, top.shape))
    rescale = jnp.exp2(top - newest)
    total = total * rescale
    pieces = []
    for group in range(groups):
        piece = jnp.exp2(scores[:, group * HD : (group + 1) * HD] * SCALE - newest)
        total = total + piece
        pieces.append(piece.astype(jnp.bfloat16))
    weights = jnp.concatenate(pieces, axis=1)
    mixed = mixed * rescale + jnp.dot(weights, values, preferred_element_type=jnp.float32)
    return newest, total, mixed


def sort_frames(info, near, far, near_at, keys, values, sem, size):
    def start(time, carry):
        slot = info[time]
        chip = slot // 2
        mine = slot % 2 == info[FRAMES]
        rows = pl.ds(pl.multiple_of(time * size, size), size)

        @pl.when(mine)
        def _():
            pltpu.make_async_copy(near.at[chip, near_at], keys.at[rows], sem.at[0]).start()
            pltpu.make_async_copy(near.at[chip, near_at + 1], values.at[rows], sem.at[1]).start()

        @pl.when(jnp.logical_not(mine))
        def _():
            pltpu.make_async_copy(far.at[chip, 0], keys.at[rows], sem.at[0]).start()
            pltpu.make_async_copy(far.at[chip, 1], values.at[rows], sem.at[1]).start()

        return carry

    lax.fori_loop(0, FRAMES, start, 0)
    pltpu.make_async_copy(keys, keys, sem.at[0]).wait()
    pltpu.make_async_copy(values, values, sem.at[1]).wait()


WIDE = 1024


def main_kernel(info, query, near, far, top_out, total_out, mixed_out, keys, values, sem):
    index = pl.program_id(0)

    @pl.when(index == 0)
    def _():
        sort_frames(info, near, far, 1, keys, values, sem, TOKENS)

    frames = info[FRAMES + 1 + index]
    mine = query[0, 0]
    top_out[0] = jnp.full((TOKENS, HD), LOWEST, jnp.float32)
    total_out[0] = jnp.zeros((TOKENS, HD), jnp.float32)
    mixed_out[0] = jnp.zeros((TOKENS, HD), jnp.float32)

    def run(first, count):
        rows = pl.ds(pl.multiple_of(first, TOKENS), count)
        state = (top_out[0], total_out[0], mixed_out[0])
        top, total, mixed = soft_step(mine, keys[rows], values[rows], None, state)
        top_out[0] = top
        total_out[0] = total
        mixed_out[0] = mixed

    per = WIDE // TOKENS
    whole = frames // per

    def body(step, carry):
        run(step * WIDE, WIDE)
        return carry

    lax.fori_loop(0, whole, body, 0)

    def tail(step, carry):
        run(whole * WIDE + step * TOKENS, TOKENS)
        return carry

    lax.fori_loop(0, frames - whole * per, tail, 0)


RIM_WIDE = 512


def rim_kernel(info, query, near, far, bias, top_in, total_in, mixed_in, out, keys, values, sem):
    index = pl.program_id(0)

    @pl.when(index == 0)
    def _():
        sort_frames(info, near, far, 0, keys, values, sem, RIM)

    visible = info[FRAMES + 1 + index] * RIM
    mine = query[0, 0]

    def body(step, state):
        rows = pl.ds(pl.multiple_of(step * RIM_WIDE, RIM_WIDE), RIM_WIDE)
        place = lax.broadcasted_iota(jnp.int32, (1, RIM_WIDE), 1) + step * RIM_WIDE
        row_bias = jnp.where(place < visible, bias[0:1, rows], LOWEST)
        return soft_step(mine, keys[rows], values[rows], row_bias, state)

    steps = (visible + RIM_WIDE - 1) // RIM_WIDE
    top, total, mixed = lax.fori_loop(0, steps, body, (top_in[0], total_in[0], mixed_in[0]))
    out[0] = (mixed / jnp.sum(total, axis=-1, keepdims=True)).astype(jnp.bfloat16)


def attend_main(info, received, far):
    state_spec = pl.BlockSpec((1, TOKENS, HD), lambda i, info: (i, 0, 0))
    state_shape = jax.ShapeDtypeStruct((CHIPS, TOKENS, HD), jnp.float32)
    return pl.pallas_call(
        main_kernel,
        grid_spec=pltpu.PrefetchScalarGridSpec(
            num_scalar_prefetch=1,
            grid=(CHIPS,),
            in_specs=[
                pl.BlockSpec((1, 1, TOKENS, HD), lambda i, info: (i, 0, 0, 0)),
                pl.BlockSpec(memory_space=pl.ANY),
                pl.BlockSpec(memory_space=pl.ANY),
            ],
            out_specs=[state_spec] * 3,
            scratch_shapes=[
                pltpu.VMEM((FRAMES * TOKENS, HD), jnp.bfloat16),
                pltpu.VMEM((FRAMES * TOKENS, HD), jnp.bfloat16),
                pltpu.SemaphoreType.DMA((2,)),
            ],
        ),
        out_shape=[state_shape] * 3,
        compiler_params=pltpu.CompilerParams(vmem_limit_bytes=48 * 1024 * 1024),
        name="attend_main",
    )(info, received, received, far)


def attend_rims(info, received, near, far, bias, state):
    state_spec = pl.BlockSpec((1, TOKENS, HD), lambda i, info: (i, 0, 0))
    return pl.pallas_call(
        rim_kernel,
        grid_spec=pltpu.PrefetchScalarGridSpec(
            num_scalar_prefetch=1,
            grid=(CHIPS,),
            in_specs=[
                pl.BlockSpec((1, 1, TOKENS, HD), lambda i, info: (i, 0, 0, 0)),
                pl.BlockSpec(memory_space=pl.ANY),
                pl.BlockSpec(memory_space=pl.ANY),
                pl.BlockSpec((1, FRAMES * RIM), lambda i, info: (0, 0)),
            ]
            + [state_spec] * 3,
            out_specs=state_spec,
            scratch_shapes=[
                pltpu.VMEM((FRAMES * RIM, HD), jnp.bfloat16),
                pltpu.VMEM((FRAMES * RIM, HD), jnp.bfloat16),
                pltpu.SemaphoreType.DMA((2,)),
            ],
        ),
        out_shape=jax.ShapeDtypeStruct((CHIPS, TOKENS, HD), jnp.bfloat16),
        compiler_params=pltpu.CompilerParams(vmem_limit_bytes=48 * 1024 * 1024),
        name="attend_rims",
    )(info, received, near, far, bias, *state)


def swap_cores(value):
    return lax.ppermute(value, "ha", [(i, i ^ 1) for i in range(8)])


def to_right(tm, z, core):
    if tm < SLOTS:
        return (tm + SLOTS, z, core)
    return (tm - SLOTS, z + 1, core) if z % 2 == 0 else None


def to_left(tm, z, core):
    if tm >= SLOTS:
        return (tm - SLOTS, z, core)
    return (tm + SLOTS, z - 1, core) if z % 2 == 1 else None


def rim_keys(main, depth, kind):
    left = lax.ppermute(main[:, :, :, TILE - PAD :], AXES, device_pairs(to_right))
    right = lax.ppermute(main[:, :, :, :PAD], AXES, device_pairs(to_left))

    def rows(first):
        span = slice(first, first + PAD)
        return jnp.concatenate([left[:, :, span], main[:, :, span], right[:, :, span]], axis=3)

    edge = jnp.where(depth < 2, rows(TILE - PAD), rows(0))
    across = lax.ppermute(edge, "ha", [(i, i ^ 4) for i in range(8)])
    flat = [piece.reshape(CHIPS, 2, -1, HD) for piece in (left, right, across)]
    spare = jnp.zeros((CHIPS, 2, RIM - sum(p.shape[2] for p in flat), HD), jnp.bfloat16)
    return jnp.concatenate(flat + [spare], axis=2)


def rim_bias(column):
    place = jnp.arange(RIM, dtype=jnp.int32)
    across = (place - 64) % 20
    is_across = (place >= 64) & (place < 104)
    is_left = (place < 32) | (is_across & (across < PAD))
    is_right = ((place >= 32) & (place < 64)) | (is_across & (across >= TILE + PAD))
    valid = (place < 104) & ~(is_left & (column == 0)) & ~(is_right & (column == 3))
    return jnp.tile(jnp.where(valid, 0.0, LOWEST).astype(jnp.float32), FRAMES)[None]


def shards(tokens, projection, norm_gain, modulation, levels, frame_order):
    chip = lax.axis_index("tm")
    place = lax.axis_index("ha")
    depth = place // 2
    core = place % 2
    sending, away = project(tokens.reshape(2, TOKENS, D), projection, norm_gain, modulation, levels, core)
    other = swap_cores(away)
    sending = lax.dynamic_update_slice_in_dim(sending, other, (1 - core) * SLOTS, 0)
    received = lax.all_to_all(sending, "tm", 0, 0, tiled=True)
    far = swap_cores(received[:, 1:])

    slots = jnp.zeros((FRAMES,), jnp.int32).at[frame_order].set(jnp.arange(FRAMES, dtype=jnp.int32))
    own_order = lax.dynamic_index_in_dim(frame_order.reshape(CHIPS, 2), core, 1, keepdims=False)
    info = jnp.concatenate([slots, core[None], own_order + 1])

    state = attend_main(info, received, far)
    rims = rim_keys(received[:, 1:].reshape(CHIPS, 2, TILE, TILE, HD), depth, chip // SLOTS)
    far_rims = swap_cores(rims)
    bias = rim_bias((2 * depth + chip // SLOTS) % 4)
    mixed = attend_rims(info, received, rims, far_rims, bias, state)

    back = lax.all_to_all(mixed, "tm", 0, 0, tiled=True)
    stay = lax.dynamic_slice_in_dim(back, core * SLOTS, HEADS, 0)
    leave = lax.dynamic_slice_in_dim(back, (1 - core) * SLOTS, HEADS, 0)
    come = swap_cores(leave)
    both = jnp.where(core == 0, jnp.stack([stay, come]), jnp.stack([come, stay]))
    return both.transpose(0, 2, 1, 3).reshape(2, 1, TILE, TILE, QD)


def solution(mesh):
    in_specs = (P("tm", "ha", None, None, None), P(), P(), P(), P("tm"), P())
    out_specs = P("tm", "ha", None, None, None)
    return jax.shard_map(shards, mesh=mesh, in_specs=in_specs, out_specs=out_specs, check_vma=False)
```

time: 717 us -> 224 us (0.31)
  local copies, waits for them, and re-layouts: 237 us -> 16 us
  waiting for transfers between devices: 227 us -> 32.2 us
  matrix products: 122 us -> 0 us
  Pallas kernels: 0 us -> 108 us
  other arithmetic: 88 us -> 1.47 us
  blocking collectives: 0 us -> 45.3 us
  between operations: 13.8 us -> 0.24 us
    all_gather x1 -> x0, waiting for transfers between devices: 225 us -> none  [shards(): arrived = lax.all_gather(own_window, 'tm', axis=0, tiled=True)]
    dot_general x34 -> x0, matrix products: 122 us -> none  [the longest x16 74.3 us: attend_group(): jnp.einsum('fqhd,gkhd->fqhgk', query_tiles, window_kv[:, :, 0], preferred...]
    pallas_call x0 -> x3, Pallas kernels: none -> 108 us  [the longest x1 54.9 us: attend_main(): pl.pallas_call(main_kernel, grid_spec=pltpu.PrefetchScalarGridSpec(num_sc...]
    reshape x23 -> x3, local copies, waits for them, and re-layouts: 84.1 us -> 1.94 us  [the longest x1 1.78 us: shards(): return both.transpose(0, 2, 1, 3).reshape(2, 1, TILE, TILE, QD)]
    reduce_sum x19 -> x0, other arithmetic: 81.8 us -> none  [the longest x16 80.7 us: attend_group(): totals = rescale * totals + jnp.sum(exp_scores, axis=(3, 4))]
    dynamic_slice x17 -> x0, local copies, waits for them, and re-layouts: 52.4 us -> none  [the longest x16 52.4 us: shards(): state_now, _ = lax.scan(scan_step, state_now, (grouped, orders))]
    all_to_all x0 -> x1, blocking collectives: none -> 45.3 us  [shards(): received = lax.all_to_all(sending, 'tm', 0, 0, tiled=True)]
    while x176 -> x0, local copies, waits for them, and re-layouts: 43.7 us -> none
  transfers between devices with their start and end apart: 9 -> 8, of which waited for: 2 -> 5; matrix products, arithmetic and copies ran while one was open for 1% -> 2% of each run, Pallas kernels for 0% -> 25%
where the time goes in v1:
time: 224 us; the launch traced here: 223 us
  Pallas kernels  108 us (48%)
  blocking collectives  45.3 us (20%)
  waiting for transfers between devices  32.2 us (14%)
  starting transfers between devices  19.5 us (9%)
  local copies, waits for them, and re-layouts  16 us (7%)
    pallas_call x1, Pallas kernels, attend_main(): pl.pallas_call(main_kernel, grid_spec=pltpu.PrefetchScalarGridSpec(num_sc...  54.9 us
    all_to_all x1, blocking collectives, shards(): received = lax.all_to_all(sending, 'tm', 0, 0, tiled=True)  45.3 us
    pallas_call x1, Pallas kernels, attend_rims(): pl.pallas_call(rim_kernel, grid_spec=pltpu.PrefetchScalarGridSpec(num_sca...  42.3 us
    all_to_all x1, waiting for transfers between devices, shards(): back = lax.all_to_all(mixed, 'tm', 0, 0, tiled=True)  14.6 us
    pallas_call x1, Pallas kernels, project(): pl.pallas_call(project_kernel, grid_spec=pltpu.PrefetchScalarGridSpec(num...  10.6 us
    ppermute x1, waiting for transfers between devices, rim_keys(): across = lax.ppermute(edge, 'ha', [(i, i ^ 4) for i in range(8)])  8.72 us
    unnamed x16, local copies, waits for them, and re-layouts  6.22 us
    ppermute x1, starting transfers between devices, rim_keys(): lax.ppermute(main[:, :, :, TILE - PAD:], AXES, device_pairs(to_right))  5.79 us
  transfers between devices with their start and end apart: 8, of which 5 were waited for; matrix products, arithmetic and copies ran while one was open for 2% of the time, Pallas kernels for 25%

profile of v1, /device:TPU:1, one launch (start us, length us, event | category | flops | bytes accessed | tf_op | source)
XLA Modules:
  0.0 222.6 jit_solution(1182129504735496311)
XLA Ops:
  0.0 0.7 pad_add_fusion.1.info
  0.7 1.4 copy-done.1
  2.1 1.1 copy-done.2
  3.9 10.6 %project.1 = (bf16[16,3,256,128]{3,2,1,0:T(8,128)(2,1)}, bf16[8,3,256,128]{3,2,1,0:T(8,128)(2,1)S(1)}) custom-call(s32[3]{0:T(128)S(1)} %pad_add_fusion.1.info, bf16[2,256,1536]{2,1,0:T(8,128)(2,1)S(1)} %bitcast.12, bf16[1536,2304]{1,0:T(8,128)(2,1)} %weights.1, f32[2,768]{1,0:T(2,128)S(1)} %copy-done.3, f32[50,2,1536]{2,1,0:T(2,128)S(1)} %copy-done.2), custom_call_target="tpu_custom_call" | custom-call | tf_op jit(solution)/shard_map/project/pallas_call | solution.py:84
  14.5 1.5 collective-permute-start
  16.0 3.0 %collective-permute-done = bf16[8,3,256,128]{3,2,1,0:T(8,128)(2,1)S(1)} collective-permute-done((bf16[8,3,256,128]{3,2,1,0:T(8,128)(2,1)S(1)}, bf16[8,3,256,128]{3,2,1,0:T(8,128)(2,1)S(1)}, u32[]{:S(2)}, u32[]{:S(2)}) %collective-permute-start) | collective-permute-done | bytes 1572896 | tf_op jit(solution)/shard_map/ppermute | solution.py:276
  19.0 1.3 constant_dynamic-update-slice_fusion
  20.3 45.3 %all_to_all.10.query.near = bf16[16,3,256,128]{3,2,1,0:T(8,128)(2,1)S(1)} all-to-all(bf16[16,3,256,128]{3,2,1,0:T(8,128)(2,1)} %constant_dynamic-update-slice_fusion), channel_id=1, replica_groups=mesh['tm'=16,'ha'=8] {'tm'}, dimensions={0} | all-to-all | bytes 6291456 | tf_op jit(solution)/shard_map/all_to_all | solution.py:324
  65.6 1.6 slice.40
  67.9 2.0 fusion.5
  70.2 1.3 collective-permute-start.2
  71.5 2.2 collective-permute-start.5
  74.0 5.8 %collective-permute-start.1 = (bf16[16,2,16,2,128]{4,0,3,2,1:T(8,128)(2,1)S(1)}, bf16[16,2,16,2,128]{4,0,3,2,1:T(8,128)(2,1)S(1)}, u32[]{:S(2)}, u32[]{:S(2)}) collective-permute-start(bf16[16,2,16,2,128]{4,0,3,2,1:T(8,128)(2,1)S(1)} %copy.16), channel_id=1, source_target_pairs={{0,64},{1,65},{2,66},{3,67},{4,68},{5,69},{6,70},{7,71},{8,72},{9,... | collective-permute-start | bytes 786440 | tf_op jit(solution)/shard_map/ppermute | solution.py:292
  79.8 1.1 fusion.4
  81.2 4.2 %collective-permute-done.1 = bf16[16,2,16,2,128]{4,0,3,2,1:T(8,128)(2,1)S(1)} collective-permute-done((bf16[16,2,16,2,128]{4,0,3,2,1:T(8,128)(2,1)S(1)}, bf16[16,2,16,2,128]{4,0,3,2,1:T(8,128)(2,1)S(1)}, u32[]{:S(2)}, u32[]{:S(2)}) %collective-permute-start.1) | collective-permute-done | bytes 262176 | tf_op jit(solution)/shard_map/ppermute | solution.py:292
  85.5 3.7 %collective-permute-start.3 = (bf16[16,2,2,20,128]{4,0,3,2,1:T(8,128)(2,1)S(1)}, bf16[16,2,2,20,128]{4,0,3,2,1:T(8,128)(2,1)S(1)}, u32[]{:S(2)}, u32[]{:S(2)}) collective-permute-start(bf16[16,2,2,20,128]{4,0,3,2,1:T(8,128)(2,1)S(1)} %maximum_select_fusion.1), channel_id=1, source_target_pairs={{0,4},{1,5},{2,6},{3,7},{4,0},{5,1},{6,2},{7,3},{8,12},{9,13},{10,... | collective-permute-start | bytes 983048 | tf_op jit(solution)/shard_map/ppermute | solution.py:300
  89.8 8.7 %collective-permute-done.3 = bf16[16,2,2,20,128]{4,0,3,2,1:T(8,128)(2,1)S(1)} collective-permute-done((bf16[16,2,2,20,128]{4,0,3,2,1:T(8,128)(2,1)S(1)}, bf16[16,2,2,20,128]{4,0,3,2,1:T(8,128)(2,1)S(1)}, u32[]{:S(2)}, u32[]{:S(2)}) %collective-permute-start.3) | collective-permute-done | bytes 327712 | tf_op jit(solution)/shard_map/ppermute | solution.py:300
  100.6 54.9 %attend_main.1 = (f32[16,256,128]{2,1,0:T(8,128)S(1)}, f32[16,256,128]{2,1,0:T(8,128)S(1)}, f32[16,256,128]{2,1,0:T(8,128)}) custom-call(s32[49]{0:T(128)S(1)} %pad_add_fusion.info, bf16[16,3,256,128]{3,2,1,0:T(8,128)(2,1)} %copy-done.4, bf16[16,3,256,128]{3,2,1,0:T(8,128)(2,1)} %copy-done.4, bf16[16,2,256,128]{3,2,1,0:T(8,128)(2,1)} %collective-permute-done.5.far), custom_call_target="tpu_custom_call" | custom-call | tf_op jit(solution)/shard_map/attend_main/pallas_call | solution.py:225
  155.5 1.4 copy-done
  156.9 42.3 %attend_rims.1 = bf16[16,256,128]{2,1,0:T(8,128)(2,1)} custom-call(s32[49]{0:T(128)S(1)} %pad_add_fusion.info, bf16[16,3,256,128]{3,2,1,0:T(8,128)(2,1)} %copy-done.4, bf16[16,2,112,128]{3,2,1,0:T(8,128)(2,1)S(1)} %maximum_maximum_fusion.near, bf16[16,2,112,128]{3,2,1,0:T(8,128)(2,1)S(1)} %collective-permute-done.4.far, ...), custom_call_target="tpu_custom_call" | custom-call | tf_op jit(solution)/shard_map/attend_rims/pallas_call | solution.py:250
  199.1 4.5 %all-to-all-start.1 = ((bf16[16,256,128]{2,1,0:T(8,128)(2,1)}), bf16[16,256,128]{2,1,0:T(8,128)(2,1)S(1)}, u32[]{:S(2)}, u32[]{:S(2)}) async-start(bf16[16,256,128]{2,1,0:T(8,128)(2,1)} %attend_rims.1), calls=%async_computation.1 | async-start | bytes 2097152 | tf_op jit(solution)/shard_map/all_to_all | solution.py:337
  203.7 14.6 %all-to-all-done.1 = bf16[16,256,128]{2,1,0:T(8,128)(2,1)S(1)} async-done(((bf16[16,256,128]{2,1,0:T(8,128)(2,1)}), bf16[16,256,128]{2,1,0:T(8,128)(2,1)S(1)}, u32[]{:S(2)}, u32[]{:S(2)}) %all-to-all-start.1) | async-done | bytes 1048608 | tf_op jit(solution)/shard_map/all_to_all | solution.py:337
  218.4 1.7 collective-permute-done.6
  220.8 1.8 reshape.64
  (39 shorter events, 5.9 us)
Async XLA Ops:
  0.7 1.4 copy-start.1
  2.1 1.1 copy-start.2
  3.2 0.7 copy-start.3
  14.5 4.5 %collective-permute-start = (bf16[8,3,256,128]{3,2,1,0:T(8,128)(2,1)S(1)}, bf16[8,3,256,128]{3,2,1,0:T(8,128)(2,1)S(1)}, u32[]{:S(2)}, u32[]{:S(2)}) collective-permute-start(bf16[8,3,256,128]{3,2,1,0:T(8,128)(2,1)S(1)} %get-tuple-element.11), channel_id=1, source_target_pairs={{0,1},{1,0},{2,3},{3,2},{4,5},{5,4},{6,7},{7,6},{8,9},{9,8},{10,11... | collective-permute-start | bytes 4718600 | tf_op jit(solution)/shard_map/ppermute | solution.py:276
  65.6 2.3 %copy-start.4 = (bf16[16,3,256,128]{3,2,1,0:T(8,128)(2,1)}, bf16[16,3,256,128]{3,2,1,0:T(8,128)(2,1)S(1)}, u32[]{:S(2)}) copy-start(bf16[16,3,256,128]{3,2,1,0:T(8,128)(2,1)S(1)} %all_to_all.10.query.near) | copy-start | bytes 9437188
  70.2 11.0 %collective-permute-start.2 = (bf16[16,2,16,2,128]{4,0,3,2,1:T(8,128)(2,1)S(1)}, bf16[16,2,16,2,128]{4,0,3,2,1:T(8,128)(2,1)S(1)}, u32[]{:S(2)}, u32[]{:S(2)}) collective-permute-start(bf16[16,2,16,2,128]{4,0,3,2,1:T(8,128)(2,1)S(1)} %copy.17), channel_id=1, source_target_pairs={{2,64},{3,65},{6,68},{7,69},{10,72},{11,73},{14,76},{15,77},{18,80... | collective-permute-start | bytes 786440 | tf_op jit(solution)/shard_map/ppermute | solution.py:293
  71.5 29.1 %collective-permute-start.5 = (bf16[16,2,256,128]{3,2,1,0:T(8,128)(2,1)}, bf16[16,2,256,128]{3,2,1,0:T(8,128)(2,1)}, u32[]{:S(2)}, u32[]{:S(2)}) collective-permute-start(bf16[16,2,256,128]{3,2,1,0:T(8,128)(2,1)} %slice.40), channel_id=1, source_target_pairs={{0,1},{1,0},{2,3},{3,2},{4,5},{5,4},{6,7},{7,6},{8,9},{9,8},{10,11... | collective-permute-start | bytes 6291464 | tf_op jit(solution)/shard_map/ppermute | solution.py:276
  74.0 11.5 %collective-permute-start.1 = (bf16[16,2,16,2,128]{4,0,3,2,1:T(8,128)(2,1)S(1)}, bf16[16,2,16,2,128]{4,0,3,2,1:T(8,128)(2,1)S(1)}, u32[]{:S(2)}, u32[]{:S(2)}) collective-permute-start(bf16[16,2,16,2,128]{4,0,3,2,1:T(8,128)(2,1)S(1)} %copy.16), channel_id=1, source_target_pairs={{0,64},{1,65},{2,66},{3,67},{4,68},{5,69},{6,70},{7,71},{8,72},{9,... | collective-permute-start | bytes 786440 | tf_op jit(solution)/shard_map/ppermute | solution.py:292
  85.5 14.0 %copy-start.5 = (s32[32]{0:T(128)S(1)}, s32[32]{0:T(128)}, u32[]{:S(2)}) copy-start(s32[32]{0:T(128)} %param.11) | copy-start | bytes 388
  85.5 13.0 %collective-permute-start.3 = (bf16[16,2,2,20,128]{4,0,3,2,1:T(8,128)(2,1)S(1)}, bf16[16,2,2,20,128]{4,0,3,2,1:T(8,128)(2,1)S(1)}, u32[]{:S(2)}, u32[]{:S(2)}) collective-permute-start(bf16[16,2,2,20,128]{4,0,3,2,1:T(8,128)(2,1)S(1)} %maximum_select_fusion.1), channel_id=1, source_target_pairs={{0,4},{1,5},{2,6},{3,7},{4,0},{5,1},{6,2},{7,3},{8,12},{9,13},{10,... | collective-permute-start | bytes 983048 | tf_op jit(solution)/shard_map/ppermute | solution.py:300
  98.9 58.0 %collective-permute-start.4 = (bf16[16,2,112,128]{3,2,1,0:T(8,128)(2,1)S(1)}, bf16[16,2,112,128]{3,2,1,0:T(8,128)(2,1)S(1)}, u32[]{:S(2)}, u32[]{:S(2)}) collective-permute-start(bf16[16,2,112,128]{3,2,1,0:T(8,128)(2,1)S(1)} %maximum_maximum_fusion.near), channel_id=1, source_target_pairs={{0,1},{1,0},{2,3},{3,2},{4,5},{5,4},{6,7},{7,6},{8,9},{9,8},{10,11... | collective-permute-start | bytes 2752520 | tf_op jit(solution)/shard_map/ppermute | solution.py:276
  155.5 1.4 copy-start
  199.1 19.1 %all-to-all-start.1 = ((bf16[16,256,128]{2,1,0:T(8,128)(2,1)}), bf16[16,256,128]{2,1,0:T(8,128)(2,1)S(1)}, u32[]{:S(2)}, u32[]{:S(2)}) async-start(bf16[16,256,128]{2,1,0:T(8,128)(2,1)} %attend_rims.1), calls=%async_computation.1 | async-start | bytes 2097152 | tf_op jit(solution)/shard_map/all_to_all | solution.py:337
  218.3 1.8 collective-permute-start.6

commit v2 on v1

v2 whole, which is shorter than its diff:
```python
import functools
import math

import jax
import jax.numpy as jnp
from jax import lax
from jax.experimental import pallas as pl
from jax.experimental.pallas import tpu as pltpu
from jax.sharding import PartitionSpec as P

D = 1536
HEADS = 6
HD = 128
TILE = 16
PAD = 2
TOKENS = TILE * TILE
QD = HEADS * HD
FRAMES = 32
CHIPS = 16
SLOTS = 8
RIM = 112
LOWEST = -1e30
LOG2E = math.log2(math.e)
SCALE = LOG2E / math.sqrt(HD)
AXES = ("tm", "ha")


def device_pairs(target):
    pairs = []
    for tm in range(CHIPS):
        for ha in range(8):
            goal = target(tm, ha // 2, ha % 2)
            if goal is not None:
                pairs.append((tm * 8 + ha, goal[0] * 8 + goal[1] * 2 + goal[2]))
    return pairs


def project_kernel(info, tokens, weights, gains, modulation, own, away, inputs):
    part = pl.program_id(0)
    step = pl.program_id(1)

    @pl.when(part == 0)
    def _():
        values = tokens[0].astype(jnp.float32)
        average = jnp.mean(values, axis=-1, keepdims=True)
        centred = values - average
        spread = jnp.mean(centred * centred, axis=-1, keepdims=True)
        normed = centred * lax.rsqrt(spread + 1e-06)
        shift = modulation[0, 0:1, :]
        scale = modulation[0, 1:2, :]
        inputs[step] = (normed * (1.0 + scale) + shift).astype(jnp.bfloat16)

    raw = jnp.dot(inputs[step], weights[...], preferred_element_type=jnp.float32)

    def put(result):
        result = result.astype(jnp.bfloat16)

        @pl.when(step == 0)
        def _():
            for head in range(HEADS):
                away[head, 0] = result[:, head * HD : (head + 1) * HD]

        @pl.when(step == 1)
        def _():
            for head in range(HEADS):
                own[head, 0] = result[:, head * HD : (head + 1) * HD]

    @pl.when(part < 2)
    def _():
        row = jnp.where(part == 0, gains[0:1, :], gains[1:2, :])
        put(raw * lax.rsqrt(jnp.mean(raw * raw, axis=-1, keepdims=True) + 1e-06) * row)

    @pl.when(part == 2)
    def _():
        put(raw)


def project(tokens, projection, norm_gain, modulation, levels, core):
    info = jnp.stack([core, levels[0], levels[1]])

    def frame(step, info):
        return info[0] + 1 - step - 2 * info[0] * (1 - step)

    return pl.pallas_call(
        project_kernel,
        grid_spec=pltpu.PrefetchScalarGridSpec(
            num_scalar_prefetch=1,
            grid=(3, 2),
            in_specs=[
                pl.BlockSpec((1, TOKENS, D), lambda p, s, info: (jnp.where(p == 0, frame(s, info), frame(1, info)), 0, 0)),
                pl.BlockSpec((D, QD), lambda p, s, info: (0, p)),
                pl.BlockSpec((2, QD), lambda p, s, info: (0, 0)),
                pl.BlockSpec((1, 2, D), lambda p, s, info: (info[1 + frame(s, info)], 0, 0)),
            ],
            out_specs=[
                pl.BlockSpec((SLOTS, 1, TOKENS, HD), lambda p, s, info: (info[0], p, 0, 0)),
                pl.BlockSpec((SLOTS, 1, TOKENS, HD), lambda p, s, info: (0, p, 0, 0)),
            ],
            scratch_shapes=[pltpu.VMEM((2, TOKENS, D), jnp.bfloat16)],
        ),
        out_shape=[
            jax.ShapeDtypeStruct((CHIPS, 3, TOKENS, HD), jnp.bfloat16),
            jax.ShapeDtypeStruct((SLOTS, 3, TOKENS, HD), jnp.bfloat16),
        ],
        compiler_params=pltpu.CompilerParams(vmem_limit_bytes=48 * 1024 * 1024),
        name="project",
    )(info, tokens, projection, norm_gain, modulation)


STREAMS = 2
EACH = CHIPS // STREAMS
WIDE = 512
LIMIT = EACH * (FRAMES * TOKENS // WIDE)
ROWS = STREAMS * (EACH + 1)


def plan(order, core, size, slots, chips, pick, block, left):
    for slot in range(FRAMES):
        slots[order[slot]] = slot

    def clear(step, carry):
        for stream in range(STREAMS):
            pick[stream, step] = EACH
            block[stream, step] = 0
            left[stream, step] = WIDE
        return carry

    def visit(turn, carry):
        place = carry[0]
        time = FRAMES - 1 - turn
        slot = slots[time]
        mine = slot % 2 == core
        lane = place % (2 * STREAMS)
        stream = jnp.where(lane < STREAMS, lane, 2 * STREAMS - 1 - lane)
        row = place // STREAMS
        rows = (time + 1) * size
        count = jnp.where(mine, (rows + WIDE - 1) // WIDE, 0)
        used = carry[1]
        for other in range(1, STREAMS):
            used = jnp.where(stream == other, carry[1 + other], used)

        @pl.when(mine)
        def _():
            chips[row * STREAMS + stream] = slot // 2

        def fill(step, inner):
            pick[stream, used + step] = row
            block[stream, used + step] = step
            left[stream, used + step] = rows - step * WIDE
            return inner

        lax.fori_loop(0, count, fill, 0)
        grown = tuple(carry[1 + s] + jnp.where(stream == s, count, 0) for s in range(STREAMS))
        return (place + jnp.where(mine, 1, 0),) + grown

    zero = jnp.int32(0)
    lax.fori_loop(0, LIMIT + 2, clear, 0)
    totals = lax.fori_loop(0, FRAMES, visit, (zero,) + (zero,) * STREAMS)[1:]
    return functools.reduce(jnp.maximum, totals)


def fold(values, combine):
    return combine(values.reshape(values.shape[0] // 8, 8, values.shape[1]), axis=0)


def sweep(trip, scored, queries, keys, values, tops, totals, mixes, pick, block, left, raws):
    def spots_of(step):
        spots = []
        for stream in range(STREAMS):
            row = pick[stream, step] * STREAMS + stream
            first = pl.multiple_of(block[stream, step] * WIDE, WIDE)
            spots.append((row, pl.ds(first, WIDE)))
        return spots

    def ask(step, slot):
        for stream, (row, rows) in enumerate(spots_of(step)):
            raws[slot][stream][...] = jnp.dot(keys[rows], queries[row], preferred_element_type=jnp.float32)

    def answer(step, slot):
        spots = spots_of(step)
        weighed = []
        for stream, (row, rows) in enumerate(spots):
            scores = scored(raws[slot][stream][...], rows, left[stream, step])
            highest = jnp.max(fold(scores, jnp.max), axis=0, keepdims=True) * SCALE
            top = tops[row]
            newest = jnp.maximum(top, highest)
            rescale = jnp.exp2(top - newest)
            weights = jnp.exp2(scores * SCALE - newest[0:1])
            total = totals[row] * rescale + fold(weights, jnp.sum)
            weighed.append((newest, total, rescale, weights.astype(jnp.bfloat16)))
        fresh = [jnp.dot(values[:, rows], weighed[stream][3], preferred_element_type=jnp.float32) for stream, (row, rows) in enumerate(spots)]
        mixed = [mixes[row] * weighed[stream][2][0:1] + fresh[stream] for stream, (row, rows) in enumerate(spots)]
        for stream, (row, rows) in enumerate(spots):
            tops[row] = weighed[stream][0]
            totals[row] = weighed[stream][1]
            mixes[row] = mixed[stream]

    def body(pair, carry):
        ask(2 * pair + 1, 1)
        answer(2 * pair, 0)
        ask(2 * pair + 2, 0)
        answer(2 * pair + 1, 1)
        return carry

    ask(0, 0)
    lax.fori_loop(0, (trip + 1) // 2, body, 0)


def gather_frames(order_slots, core, near, far, near_at, keys, staged, sem, size):
    def start(time, carry):
        slot = order_slots[time]
        chip = slot // 2
        mine = slot % 2 == core
        rows = pl.ds(pl.multiple_of(time * size, size), size)

        @pl.when(mine)
        def _():
            pltpu.make_async_copy(near.at[chip, near_at], keys.at[rows], sem.at[0]).start()
            pltpu.make_async_copy(near.at[chip, near_at + 1], staged.at[rows], sem.at[1]).start()

        @pl.when(jnp.logical_not(mine))
        def _():
            pltpu.make_async_copy(far.at[chip, 0], keys.at[rows], sem.at[0]).start()
            pltpu.make_async_copy(far.at[chip, 1], staged.at[rows], sem.at[1]).start()

        return carry

    lax.fori_loop(0, FRAMES, start, 0)


def turn_values(staged, values, total):
    def turn(step, carry):
        rows = pl.ds(pl.multiple_of(step * WIDE, WIDE), WIDE)
        values[:, rows] = staged[rows].T
        return carry

    lax.fori_loop(0, total // WIDE, turn, 0)


def turn_queries(chips, staged, queries):
    for place in range(CHIPS):
        queries[place] = staged[chips[place]].T


def main_kernel(info, near, far, tops, totals, mixes, queries, asked, keys, staged, values, slots, chips, pick, block, left, sem, *raws):
    core = info[FRAMES]
    trip = plan(info, core, TOKENS, slots, chips, pick, block, left)
    asking = pltpu.make_async_copy(near.at[:, 0], asked, sem.at[2])
    asking.start()
    gather_frames(slots, core, near, far, 1, keys, staged, sem, TOKENS)
    tops[...] = jnp.full(tops.shape, LOWEST, jnp.float32)
    totals[...] = jnp.zeros(totals.shape, jnp.float32)
    mixes[...] = jnp.zeros(mixes.shape, jnp.float32)
    queries[pl.ds(CHIPS, STREAMS)] = jnp.zeros((STREAMS, HD, TOKENS), jnp.bfloat16)
    asking.wait()
    turn_queries(chips, asked, queries)
    pltpu.make_async_copy(keys, keys, sem.at[0]).wait()
    pltpu.make_async_copy(staged, staged, sem.at[1]).wait()
    turn_values(staged, values, FRAMES * TOKENS)

    def scored(raw, rows, remain):
        half = WIDE // 2
        return jnp.concatenate([raw[:half], raw[half:] + jnp.where(remain < WIDE, LOWEST, 0.0)], axis=0)

    sweep(trip, scored, queries, keys, values, tops, totals, mixes, pick, block, left, (raws[:STREAMS], raws[STREAMS:]))


def rim_kernel(info, near, far, bias, queries, tops_in, totals_in, mixes_in, out, tops, totals, mixes, keys, staged, values, slots, chips, pick, block, left, sem, *raws):
    core = info[FRAMES]
    trip = plan(info, core, RIM, slots, chips, pick, block, left)
    gather_frames(slots, core, near, far, 0, keys, staged, sem, RIM)
    tops[...] = tops_in[...]
    totals[...] = totals_in[...]
    mixes[...] = mixes_in[...]
    pltpu.make_async_copy(keys, keys, sem.at[0]).wait()
    pltpu.make_async_copy(staged, staged, sem.at[1]).wait()
    turn_values(staged, values, FRAMES * RIM)

    def scored(raw, rows, remain):
        place = lax.broadcasted_iota(jnp.int32, (WIDE, HD), 0)
        added = jnp.where(place < remain, bias[rows], LOWEST)
        return jnp.concatenate([raw[:, :HD] + added, raw[:, HD:] + added], axis=1)

    sweep(trip, scored, queries, keys, values, tops, totals, mixes, pick, block, left, (raws[:STREAMS], raws[STREAMS:]))
    for place in range(CHIPS):
        whole = jnp.sum(totals[place], axis=0, keepdims=True)
        out[chips[place]] = (mixes[place] / whole).T.astype(jnp.bfloat16)


STATE = [
    jax.ShapeDtypeStruct((ROWS, 8, TOKENS), jnp.float32),
    jax.ShapeDtypeStruct((ROWS, 8, TOKENS), jnp.float32),
    jax.ShapeDtypeStruct((ROWS, HD, TOKENS), jnp.float32),
]


def key_scratch(total):
    return [
        pltpu.VMEM((total, HD), jnp.bfloat16),
        pltpu.VMEM((total, HD), jnp.bfloat16),
        pltpu.VMEM((HD, total), jnp.bfloat16),
        pltpu.SMEM((FRAMES,), jnp.int32),
        pltpu.SMEM((CHIPS,), jnp.int32),
        pltpu.SMEM((STREAMS, LIMIT + 2), jnp.int32),
        pltpu.SMEM((STREAMS, LIMIT + 2), jnp.int32),
        pltpu.SMEM((STREAMS, LIMIT + 2), jnp.int32),
        pltpu.SemaphoreType.DMA((3,)),
    ] + [pltpu.VMEM((WIDE, TOKENS), jnp.float32)] * (2 * STREAMS)


def whole(shape):
    return pl.BlockSpec(shape, lambda i, info: (0,) * len(shape))


def attend_main(info, received, far):
    shapes = STATE + [jax.ShapeDtypeStruct((ROWS, HD, TOKENS), jnp.bfloat16)]
    return pl.pallas_call(
        main_kernel,
        grid_spec=pltpu.PrefetchScalarGridSpec(
            num_scalar_prefetch=1,
            grid=(1,),
            in_specs=[pl.BlockSpec(memory_space=pl.ANY), pl.BlockSpec(memory_space=pl.ANY)],
            out_specs=[whole(s.shape) for s in shapes],
            scratch_shapes=[pltpu.VMEM((CHIPS, TOKENS, HD), jnp.bfloat16)] + key_scratch(FRAMES * TOKENS),
        ),
        out_shape=shapes,
        cost_estimate=pl.CostEstimate(flops=10**10, bytes_accessed=8 * 10**6, transcendentals=2 * 10**7),
        compiler_params=pltpu.CompilerParams(vmem_limit_bytes=48 * 1024 * 1024),
        name="attend_main",
    )(info, received, far)


def attend_rims(info, near, far, bias, state):
    shapes = [s.shape for s in STATE]
    out = (CHIPS, TOKENS, HD)
    return pl.pallas_call(
        rim_kernel,
        grid_spec=pltpu.PrefetchScalarGridSpec(
            num_scalar_prefetch=1,
            grid=(1,),
            in_specs=[pl.BlockSpec(memory_space=pl.ANY), pl.BlockSpec(memory_space=pl.ANY), whole(bias.shape)]
            + [whole((ROWS, HD, TOKENS))]
            + [whole(s) for s in shapes],
            out_specs=whole(out),
            scratch_shapes=[pltpu.VMEM(s.shape, s.dtype) for s in STATE] + key_scratch(FRAMES * RIM),
        ),
        out_shape=jax.ShapeDtypeStruct(out, jnp.bfloat16),
        cost_estimate=pl.CostEstimate(flops=4 * 10**9, bytes_accessed=8 * 10**6, transcendentals=10**7),
        compiler_params=pltpu.CompilerParams(vmem_limit_bytes=48 * 1024 * 1024),
        name="attend_rims",
    )(info, near, far, bias, state[3], *state[:3])


def swap_cores(value):
    return lax.ppermute(value, "ha", [(i, i ^ 1) for i in range(8)])


def to_right(tm, z, core):
    if tm < SLOTS:
        return (tm + SLOTS, z, core)
    return (tm - SLOTS, z + 1, core) if z % 2 == 0 else None


def to_left(tm, z, core):
    if tm >= SLOTS:
        return (tm - SLOTS, z, core)
    return (tm + SLOTS, z - 1, core) if z % 2 == 1 else None


def across(step):
    def target(tm, z, core):
        goal = step(tm, z, core)
        return None if goal is None else (goal[0], goal[1] ^ 2, core)

    return target


def rim_pieces(main, depth):
    upper = depth < 2
    edge = jnp.where(upper, main[:, :, TILE - PAD :], main[:, :, :PAD])
    return [
        lax.ppermute(main[:, :, :, TILE - PAD :], AXES, device_pairs(to_right)),
        lax.ppermute(main[:, :, :, :PAD], AXES, device_pairs(to_left)),
        lax.ppermute(edge, "ha", [(i, i ^ 4) for i in range(8)]),
        lax.ppermute(edge[:, :, :, TILE - PAD :], AXES, device_pairs(across(to_right))),
        lax.ppermute(edge[:, :, :, :PAD], AXES, device_pairs(across(to_left))),
    ]


def rim_keys(pieces):
    flat = [piece.reshape(CHIPS, 2, -1, HD) for piece in pieces]
    spare = jnp.zeros((CHIPS, 2, RIM - sum(p.shape[2] for p in flat), HD), jnp.bfloat16)
    return jnp.concatenate(flat + [spare], axis=2)


def rim_bias(column):
    place = jnp.arange(RIM, dtype=jnp.int32)
    is_left = (place < 32) | ((place >= 96) & (place < 100))
    is_right = ((place >= 32) & (place < 64)) | ((place >= 100) & (place < 104))
    valid = (place < 104) & ~(is_left & (column == 0)) & ~(is_right & (column == 3))
    column_of = jnp.tile(jnp.where(valid, 0.0, LOWEST).astype(jnp.float32), FRAMES)
    return jnp.broadcast_to(column_of[:, None], (FRAMES * RIM, HD))


def shards(tokens, projection, norm_gain, modulation, levels, frame_order):
    chip = lax.axis_index("tm")
    place = lax.axis_index("ha")
    depth = place // 2
    core = place % 2
    sending, away = project(tokens.reshape(2, TOKENS, D), projection, norm_gain, modulation, levels, core)
    other = swap_cores(away)
    sending = lax.dynamic_update_slice_in_dim(sending, other, (1 - core) * SLOTS, 0)
    received = lax.all_to_all(sending, "tm", 0, 0, tiled=True)
    far = swap_cores(received[:, 1:])

    info = jnp.concatenate([frame_order, core[None]])
    pieces = rim_pieces(received[:, 1:].reshape(CHIPS, 2, TILE, TILE, HD), depth)
    state = attend_main(info, received, far)
    pieces, top = lax.optimization_barrier((pieces, state[0]))
    state = [top, *state[1:]]
    rims = rim_keys(pieces)
    far_rims = swap_cores(rims)
    bias = rim_bias((2 * depth + chip // SLOTS) % 4)
    mixed = attend_rims(info, rims, far_rims, bias, state)

    back = lax.all_to_all(mixed, "tm", 0, 0, tiled=True)
    stay = lax.dynamic_slice_in_dim(back, core * SLOTS, HEADS, 0)
    leave = lax.dynamic_slice_in_dim(back, (1 - core) * SLOTS, HEADS, 0)
    come = swap_cores(leave)
    both = jnp.where(core == 0, jnp.stack([stay, come]), jnp.stack([come, stay]))
    return both.transpose(0, 2, 1, 3).reshape(2, 1, TILE, TILE, QD)


def solution(mesh):
    in_specs = (P("tm", "ha", None, None, None), P(), P(), P(), P("tm"), P())
    out_specs = P("tm", "ha", None, None, None)
    return jax.shard_map(shards, mesh=mesh, in_specs=in_specs, out_specs=out_specs, check_vma=False)
```

time: 224 us -> 200 us (0.89)
  Pallas kernels: 108 us -> 70.3 us
  starting transfers between devices: 19.5 us -> 42.3 us
  waiting for transfers between devices: 32.2 us -> 18.3 us
  local copies, waits for them, and re-layouts: 16 us -> 18.8 us
    pallas_call x1, Pallas kernels: 54.9 us -> 35.1 us  [attend_main(): pl.pallas_call(main_kernel, grid_spec=pltpu.PrefetchScalarGridSpec(num_sc...]
    pallas_call x1, Pallas kernels: 42.3 us -> 24.5 us  [attend_rims(): pl.pallas_call(rim_kernel, grid_spec=pltpu.PrefetchScalarGridSpec(num_sca...]
    ppermute x4, starting transfers between devices: 4.26 us -> 18.7 us  [swap_cores(): return lax.ppermute(value, 'ha', [(i, i ^ 1) for i in range(8)])]
    ppermute x3 -> x5, waiting for transfers between devices: 12.9 us -> 0.01 us  [the longest x1 0.01 us: rim_pieces(): lax.ppermute(edge[:, :, :, TILE - PAD:], AXES, device_pairs(across(to_rig...]
    all_to_all x1, starting transfers between devices: 4.53 us -> 9.19 us  [shards(): back = lax.all_to_all(mixed, 'tm', 0, 0, tiled=True)]
    ppermute x3 -> x5, starting transfers between devices: 10.8 us -> 14.5 us  [the longest x1 5.5 us: rim_pieces(): lax.ppermute(edge[:, :, :, TILE - PAD:], AXES, device_pairs(across(to_rig...]
    concatenate x1, local copies, waits for them, and re-layouts: 0.08 us -> 3.1 us  [rim_keys(): return jnp.concatenate(flat + [spare], axis=2)]
    all_to_all x1, waiting for transfers between devices: 14.6 us -> 11.9 us  [shards(): back = lax.all_to_all(mixed, 'tm', 0, 0, tiled=True)]
  transfers between devices with their start and end apart: 8 -> 10, of which waited for: 5 -> 4; matrix products, arithmetic and copies ran while one was open for 2% -> 2% of each run, Pallas kernels for 25% -> 18%
where the time goes in v2:
time: 200 us; the launch traced here: 197 us
  Pallas kernels  70.3 us (35%)
  blocking collectives  45.3 us (23%)
  starting transfers between devices  42.3 us (21%)
  local copies, waits for them, and re-layouts  18.8 us (9%)
  waiting for transfers between devices  18.3 us (9%)
  other arithmetic  2.02 us (1%)
    all_to_all x1, blocking collectives, shards(): received = lax.all_to_all(sending, 'tm', 0, 0, tiled=True)  45.3 us
    pallas_call x1, Pallas kernels, attend_main(): pl.pallas_call(main_kernel, grid_spec=pltpu.PrefetchScalarGridSpec(num_sc...  35.1 us
    pallas_call x1, Pallas kernels, attend_rims(): pl.pallas_call(rim_kernel, grid_spec=pltpu.PrefetchScalarGridSpec(num_sca...  24.5 us
    ppermute x4, starting transfers between devices, swap_cores(): return lax.ppermute(value, 'ha', [(i, i ^ 1) for i in range(8)])  18.7 us
    all_to_all x1, waiting for transfers between devices, shards(): back = lax.all_to_all(mixed, 'tm', 0, 0, tiled=True)  11.9 us
    pallas_call x1, Pallas kernels, project(): pl.pallas_call(project_kernel, grid_spec=pltpu.PrefetchScalarGridSpec(num...  10.6 us
    all_to_all x1, starting transfers between devices, shards(): back = lax.all_to_all(mixed, 'tm', 0, 0, tiled=True)  9.19 us
    unnamed x22, local copies, waits for them, and re-layouts  7.73 us
  transfers between devices with their start and end apart: 10, of which 4 were waited for; matrix products, arithmetic and copies ran while one was open for 2% of the time, Pallas kernels for 18%

profile of v2, /device:TPU:1, one launch (start us, length us, event | category | flops | bytes accessed | tf_op | source)
XLA Modules:
  0.0 197.2 jit_solution(14176383429216655317)
XLA Ops:
  0.7 1.4 copy-done
  3.9 10.6 %project.1 = (bf16[16,3,256,128]{3,2,1,0:T(8,128)(2,1)}, bf16[8,3,256,128]{3,2,1,0:T(8,128)(2,1)S(1)}) custom-call(s32[3]{0:T(128)S(1)} %pad_add_fusion.1.info, bf16[2,256,1536]{2,1,0:T(8,128)(2,1)S(1)} %bitcast.14, bf16[1536,2304]{1,0:T(8,128)(2,1)} %weights.1, f32[2,768]{1,0:T(2,128)S(1)} %copy-done.2, f32[50,2,1536]{2,1,0:T(2,128)S(1)} %copy-done.1), custom_call_target="tpu_custom_call" | custom-call | tf_op jit(solution)/shard_map/project/pallas_call | solution.py:84
  14.5 1.5 collective-permute-start
  16.0 3.0 %collective-permute-done = bf16[8,3,256,128]{3,2,1,0:T(8,128)(2,1)S(1)} collective-permute-done((bf16[8,3,256,128]{3,2,1,0:T(8,128)(2,1)S(1)}, bf16[8,3,256,128]{3,2,1,0:T(8,128)(2,1)S(1)}, u32[]{:S(2)}, u32[]{:S(2)}) %collective-permute-start) | collective-permute-done | bytes 1572896 | tf_op jit(solution)/shard_map/ppermute | solution.py:355
  20.3 45.3 %all_to_all.10.near = bf16[16,3,256,128]{3,2,1,0:T(8,128)(2,1)S(1)} all-to-all(bf16[16,3,256,128]{3,2,1,0:T(8,128)(2,1)} %constant_dynamic-update-slice_fusion), channel_id=1, replica_groups=mesh['tm'=16,'ha'=8] {'tm'}, dimensions={0} | all-to-all | bytes 6291456 | tf_op jit(solution)/shard_map/all_to_all | solution.py:413
  65.6 1.6 copy-done.6
  67.3 1.5 slice.32
  68.8 2.1 %collective-permute-start.6 = (bf16[16,2,256,128]{3,2,1,0:T(8,128)(2,1)}, bf16[16,2,256,128]{3,2,1,0:T(8,128)(2,1)S(1)}, u32[]{:S(2)}, u32[]{:S(2)}) collective-permute-start(bf16[16,2,256,128]{3,2,1,0:T(8,128)(2,1)} %slice.32), channel_id=1, source_target_pairs={{0,1},{1,0},{2,3},{3,2},{4,5},{5,4},{6,7},{7,6},{8,9},{9,8},{10,11... | collective-permute-start | bytes 6291464 | tf_op jit(solution)/shard_map/ppermute | solution.py:355
  70.9 2.1 %fusion.1 = (bf16[16,2,16,2,128]{4,3,2,1,0:T(2,128)(2,1)S(1)}, bf16[16,2,16,2,128]{4,3,2,1,0:T(2,128)(2,1)S(1)}) fusion(bf16[16,2,16,16,128]{4,3,2,1,0:T(8,128)(2,1)} %bitcast.2), kind=kLoop, calls=%fused_computation.9 | loop fusion | bytes 1048576 | tf_op jit(solution)/shard_map/slice | solution.py:383
  73.0 2.7 %collective-permute-start.1 = (bf16[16,2,16,2,128]{4,3,2,1,0:T(2,128)(2,1)S(1)}, bf16[16,2,16,2,128]{4,3,2,1,0:T(2,128)(2,1)S(1)}, u32[]{:S(2)}, u32[]{:S(2)}) collective-permute-start(bf16[16,2,16,2,128]{4,3,2,1,0:T(2,128)(2,1)S(1)} %get-tuple-element.30), channel_id=1, source_target_pairs={{0,64},{1,65},{2,66},{3,67},{4,68},{5,69},{6,70},{7,71},{8,72},{9,... | collective-permute-start | bytes 786440 | tf_op jit(solution)/shard_map/ppermute | solution.py:382
  75.7 1.3 collective-permute-start.2
  78.1 3.7 %collective-permute-start.3 = (bf16[16,2,2,16,128]{4,3,2,1,0:T(8,128)(2,1)S(1)}, bf16[16,2,2,16,128]{4,3,2,1,0:T(8,128)(2,1)S(1)}, u32[]{:S(2)}, u32[]{:S(2)}) collective-permute-start(bf16[16,2,2,16,128]{4,3,2,1,0:T(8,128)(2,1)S(1)} %slice_select_fusion), channel_id=1, source_target_pairs={{0,4},{1,5},{2,6},{3,7},{4,0},{5,1},{6,2},{7,3},{8,12},{9,13},{10,... | collective-permute-start | bytes 786440 | tf_op jit(solution)/shard_map/ppermute | solution.py:384
  81.8 5.5 %collective-permute-start.4 = (bf16[16,2,2,2,128]{4,3,2,1,0:T(2,128)(2,1)S(1)}, bf16[16,2,2,2,128]{4,3,2,1,0:T(2,128)(2,1)S(1)}, u32[]{:S(2)}, u32[]{:S(2)}) collective-permute-start(bf16[16,2,2,2,128]{4,3,2,1,0:T(2,128)(2,1)S(1)} %get-tuple-element.34), channel_id=1, source_target_pairs={{0,68},{1,69},{2,70},{3,71},{4,64},{5,65},{6,66},{7,67},{8,76},{9,... | collective-permute-start | bytes 98312 | tf_op jit(solution)/shard_map/ppermute | solution.py:385
  88.7 35.1 %attend_main.1 = (f32[18,8,256]{2,1,0:T(8,128)S(1)}, f32[18,8,256]{2,1,0:T(8,128)S(1)}, f32[18,128,256]{2,1,0:T(8,128)S(1)}, bf16[18,128,256]{2,1,0:T(8,128)(2,1)S(1)}) custom-call(s32[33]{0:T(128)S(1)} %pad_add_fusion.info, bf16[16,3,256,128]{3,2,1,0:T(8,128)(2,1)} %copy-done.6, bf16[16,2,256,128]{3,2,1,0:T(8,128)(2,1)S(1)} %collective-permute-done.6.far), custom_call_target="tpu_custom_call" | custom-call | flops 10000000000 | bytes 8000000 | tf_op jit(solution)/shard_map/attend_main/pallas_call | solution.py:317
  123.8 1.4 copy-done.3
  126.8 3.1 %concatenate.7.near = bf16[16,2,112,128]{3,2,1,0:T(8,128)(2,1)S(1)} concatenate(bf16[16,2,32,128]{3,2,1,0:T(8,128)(2,1)} %bitcast.16, bf16[16,2,32,128]{3,2,1,0:T(8,128)(2,1)} %bitcast.17, bf16[16,2,32,128]{3,2,1,0:T(8,128)(2,1)} %bitcast.18, bf16[16,2,4,128]{3,2,1,0:T(4,128)(2,1)S(1)} %bitcast.19, bf16[16,2,4,128]{3,2,1,0:T(4,128)(2,1)S(1)} %bitcast.20, ...), dimensions={2} | concatenate | bytes 1835008 | tf_op jit(solution)/shard_map/concatenate | solution.py:393
  129.9 8.8 %collective-permute-start.7 = (bf16[16,2,112,128]{3,2,1,0:T(8,128)(2,1)S(1)}, bf16[16,2,112,128]{3,2,1,0:T(8,128)(2,1)S(1)}, u32[]{:S(2)}, u32[]{:S(2)}) collective-permute-start(bf16[16,2,112,128]{3,2,1,0:T(8,128)(2,1)S(1)} %concatenate.7.near), channel_id=1, source_target_pairs={{0,1},{1,0},{2,3},{3,2},{4,5},{5,4},{6,7},{7,6},{8,9},{9,8},{10,11... | collective-permute-start | bytes 2752520 | tf_op jit(solution)/shard_map/ppermute | solution.py:355
  138.7 2.0 %collective-permute-done.7.far = bf16[16,2,112,128]{3,2,1,0:T(8,128)(2,1)S(1)} collective-permute-done((bf16[16,2,112,128]{3,2,1,0:T(8,128)(2,1)S(1)}, bf16[16,2,112,128]{3,2,1,0:T(8,128)(2,1)S(1)}, u32[]{:S(2)}, u32[]{:S(2)}) %collective-permute-start.7) | collective-permute-done | bytes 917536 | tf_op jit(solution)/shard_map/ppermute | solution.py:355
  141.3 24.5 %attend_rims.1 = bf16[16,256,128]{2,1,0:T(8,128)(2,1)} custom-call(s32[33]{0:T(128)S(1)} %pad_add_fusion.info, bf16[16,2,112,128]{3,2,1,0:T(8,128)(2,1)S(1)} %concatenate.7.near, bf16[16,2,112,128]{3,2,1,0:T(8,128)(2,1)S(1)} %collective-permute-done.7.far, f32[3584,128]{1,0:T(8,128)S(1)} %broadcast_in_dim.26.bias, ...), custom_call_target="tpu_custom_call" | custom-call | flops 4000000000 | bytes 8000000 | tf_op jit(solution)/shard_map/attend_rims/pallas_call | solution.py:336
  165.8 9.2 %all-to-all-start.1 = ((bf16[16,256,128]{2,1,0:T(8,128)(2,1)}), bf16[16,256,128]{2,1,0:T(8,128)(2,1)S(1)}, u32[]{:S(2)}, u32[]{:S(2)}) async-start(bf16[16,256,128]{2,1,0:T(8,128)(2,1)} %attend_rims.1), calls=%async_computation.1 | async-start | bytes 2097152 | tf_op jit(solution)/shard_map/all_to_all | solution.py:426
  175.0 11.9 %all-to-all-done.1 = bf16[16,256,128]{2,1,0:T(8,128)(2,1)S(1)} async-done(((bf16[16,256,128]{2,1,0:T(8,128)(2,1)}), bf16[16,256,128]{2,1,0:T(8,128)(2,1)S(1)}, u32[]{:S(2)}, u32[]{:S(2)}) %all-to-all-start.1) | async-done | bytes 1048608 | tf_op jit(solution)/shard_map/all_to_all | solution.py:426
  187.0 6.4 %collective-permute-start.8 = (bf16[6,256,128]{2,1,0:T(8,128)(2,1)S(1)}, bf16[6,256,128]{2,1,0:T(8,128)(2,1)S(1)}, u32[]{:S(2)}, u32[]{:S(2)}) collective-permute-start(bf16[6,256,128]{2,1,0:T(8,128)(2,1)S(1)} %get-tuple-element.32), channel_id=1, source_target_pairs={{0,1},{1,0},{2,3},{3,2},{4,5},{5,4},{6,7},{7,6},{8,9},{9,8},{10,11... | collective-permute-start | bytes 1179656 | tf_op jit(solution)/shard_map/ppermute | solution.py:355
  193.3 1.3 collective-permute-done.8
  195.4 1.8 reshape.60
  (39 shorter events, 9.1 us)
Async XLA Ops:
  0.7 1.4 copy-start
  2.1 1.1 copy-start.1
  3.2 0.7 copy-start.2
  14.5 4.5 %collective-permute-start = (bf16[8,3,256,128]{3,2,1,0:T(8,128)(2,1)S(1)}, bf16[8,3,256,128]{3,2,1,0:T(8,128)(2,1)S(1)}, u32[]{:S(2)}, u32[]{:S(2)}) collective-permute-start(bf16[8,3,256,128]{3,2,1,0:T(8,128)(2,1)S(1)} %get-tuple-element.18), channel_id=1, source_target_pairs={{0,1},{1,0},{2,3},{3,2},{4,5},{5,4},{6,7},{7,6},{8,9},{9,8},{10,11... | collective-permute-start | bytes 4718600 | tf_op jit(solution)/shard_map/ppermute | solution.py:355
  65.6 1.6 copy-start.6
  67.3 3.6 %copy-start.10 = (s32[32]{0:T(128)S(1)}, s32[32]{0:T(128)}, u32[]{:S(2)}) copy-start(s32[32]{0:T(128)} %param.11) | copy-start | bytes 388
  68.8 18.6 %collective-permute-start.6 = (bf16[16,2,256,128]{3,2,1,0:T(8,128)(2,1)}, bf16[16,2,256,128]{3,2,1,0:T(8,128)(2,1)S(1)}, u32[]{:S(2)}, u32[]{:S(2)}) collective-permute-start(bf16[16,2,256,128]{3,2,1,0:T(8,128)(2,1)} %slice.32), channel_id=1, source_target_pairs={{0,1},{1,0},{2,3},{3,2},{4,5},{5,4},{6,7},{7,6},{8,9},{9,8},{10,11... | collective-permute-start | bytes 6291464 | tf_op jit(solution)/shard_map/ppermute | solution.py:355
  73.0 52.8 %collective-permute-start.1 = (bf16[16,2,16,2,128]{4,3,2,1,0:T(2,128)(2,1)S(1)}, bf16[16,2,16,2,128]{4,3,2,1,0:T(2,128)(2,1)S(1)}, u32[]{:S(2)}, u32[]{:S(2)}) collective-permute-start(bf16[16,2,16,2,128]{4,3,2,1,0:T(2,128)(2,1)S(1)} %get-tuple-element.30), channel_id=1, source_target_pairs={{0,64},{1,65},{2,66},{3,67},{4,68},{5,69},{6,70},{7,71},{8,72},{9,... | collective-permute-start | bytes 786440 | tf_op jit(solution)/shard_map/ppermute | solution.py:382
  75.7 50.1 %collective-permute-start.2 = (bf16[16,2,16,2,128]{4,3,2,1,0:T(2,128)(2,1)S(1)}, bf16[16,2,16,2,128]{4,3,2,1,0:T(2,128)(2,1)S(1)}, u32[]{:S(2)}, u32[]{:S(2)}) collective-permute-start(bf16[16,2,16,2,128]{4,3,2,1,0:T(2,128)(2,1)S(1)} %get-tuple-element.29), channel_id=1, source_target_pairs={{2,64},{3,65},{6,68},{7,69},{10,72},{11,73},{14,76},{15,77},{18,80... | collective-permute-start | bytes 786440 | tf_op jit(solution)/shard_map/ppermute | solution.py:383
  78.1 47.8 %collective-permute-start.3 = (bf16[16,2,2,16,128]{4,3,2,1,0:T(8,128)(2,1)S(1)}, bf16[16,2,2,16,128]{4,3,2,1,0:T(8,128)(2,1)S(1)}, u32[]{:S(2)}, u32[]{:S(2)}) collective-permute-start(bf16[16,2,2,16,128]{4,3,2,1,0:T(8,128)(2,1)S(1)} %slice_select_fusion), channel_id=1, source_target_pairs={{0,4},{1,5},{2,6},{3,7},{4,0},{5,1},{6,2},{7,3},{8,12},{9,13},{10,... | collective-permute-start | bytes 786440 | tf_op jit(solution)/shard_map/ppermute | solution.py:384
  81.8 44.0 %collective-permute-start.4 = (bf16[16,2,2,2,128]{4,3,2,1,0:T(2,128)(2,1)S(1)}, bf16[16,2,2,2,128]{4,3,2,1,0:T(2,128)(2,1)S(1)}, u32[]{:S(2)}, u32[]{:S(2)}) collective-permute-start(bf16[16,2,2,2,128]{4,3,2,1,0:T(2,128)(2,1)S(1)} %get-tuple-element.34), channel_id=1, source_target_pairs={{0,68},{1,69},{2,70},{3,71},{4,64},{5,65},{6,66},{7,67},{8,76},{9,... | collective-permute-start | bytes 98312 | tf_op jit(solution)/shard_map/ppermute | solution.py:385
  87.4 38.5 %collective-permute-start.5 = (bf16[16,2,2,2,128]{4,3,2,1,0:T(2,128)(2,1)S(1)}, bf16[16,2,2,2,128]{4,3,2,1,0:T(2,128)(2,1)S(1)}, u32[]{:S(2)}, u32[]{:S(2)}) collective-permute-start(bf16[16,2,2,2,128]{4,3,2,1,0:T(2,128)(2,1)S(1)} %get-tuple-element.33), channel_id=1, source_target_pairs={{2,68},{3,69},{6,64},{7,65},{10,76},{11,77},{14,72},{15,73},{18,84... | collective-permute-start | bytes 98312 | tf_op jit(solution)/shard_map/ppermute | solution.py:386
  123.8 1.4 copy-start.3
  125.2 0.7 copy-start.4
  125.9 15.4 %copy-start.5 = (f32[18,8,256]{2,1,0:T(8,128)S(1)}, f32[18,8,256]{2,1,0:T(8,128)}, u32[]{:S(2)}) copy-start(f32[18,8,256]{2,1,0:T(8,128)} %copy-done.4) | copy-start | bytes 442372
  125.9 0.7 copy-start.7
  125.9 0.8 copy-start.8
  125.9 0.8 copy-start.9
  129.9 10.9 %collective-permute-start.7 = (bf16[16,2,112,128]{3,2,1,0:T(8,128)(2,1)S(1)}, bf16[16,2,112,128]{3,2,1,0:T(8,128)(2,1)S(1)}, u32[]{:S(2)}, u32[]{:S(2)}) collective-permute-start(bf16[16,2,112,128]{3,2,1,0:T(8,128)(2,1)S(1)} %concatenate.7.near), channel_id=1, source_target_pairs={{0,1},{1,0},{2,3},{3,2},{4,5},{5,4},{6,7},{7,6},{8,9},{9,8},{10,11... | collective-permute-start | bytes 2752520 | tf_op jit(solution)/shard_map/ppermute | solution.py:355
  165.8 21.1 %all-to-all-start.1 = ((bf16[16,256,128]{2,1,0:T(8,128)(2,1)}), bf16[16,256,128]{2,1,0:T(8,128)(2,1)S(1)}, u32[]{:S(2)}, u32[]{:S(2)}) async-start(bf16[16,256,128]{2,1,0:T(8,128)(2,1)} %attend_rims.1), calls=%async_computation.1 | async-start | bytes 2097152 | tf_op jit(solution)/shard_map/all_to_all | solution.py:426
  187.0 7.7 %collective-permute-start.8 = (bf16[6,256,128]{2,1,0:T(8,128)(2,1)S(1)}, bf16[6,256,128]{2,1,0:T(8,128)(2,1)S(1)}, u32[]{:S(2)}, u32[]{:S(2)}) collective-permute-start(bf16[6,256,128]{2,1,0:T(8,128)(2,1)S(1)} %get-tuple-element.32), channel_id=1, source_target_pairs={{0,1},{1,0},{2,3},{3,2},{4,5},{5,4},{6,7},{7,6},{8,9},{9,8},{10,11... | collective-permute-start | bytes 1179656 | tf_op jit(solution)/shard_map/ppermute | solution.py:355

commit v3 on v2

v3 whole, which is shorter than its diff:
```python
import functools
import math

import jax
import jax.numpy as jnp
from jax import lax
from jax.experimental import pallas as pl
from jax.experimental.pallas import tpu as pltpu
from jax.sharding import PartitionSpec as P

D = 1536
HEADS = 6
HD = 128
TILE = 16
PAD = 2
TOKENS = TILE * TILE
QD = HEADS * HD
FRAMES = 32
CHIPS = 16
SLOTS = 8
RIM = 112
LENGTH = 3 * TOKENS + 2 * RIM
LOWEST = -1e30
LOG2E = math.log2(math.e)
SCALE = LOG2E / math.sqrt(HD)
AXES = ("tm", "ha")


def project_kernel(info, tokens, weights, gains, first, second, own, away, inputs):
    part = pl.program_id(0)
    core = info[0]

    @pl.when(part == 0)
    def _():
        for turn in range(2):
            frame = 1 - core if turn == 0 else core
            values = tokens[frame].astype(jnp.float32)
            average = jnp.mean(values, axis=-1, keepdims=True)
            centred = values - average
            spread = jnp.mean(centred * centred, axis=-1, keepdims=True)
            normed = centred * lax.rsqrt(spread + 1e-06)
            shift = jnp.where(frame == 0, first[0, 0:1, :], second[0, 0:1, :])
            scale = jnp.where(frame == 0, first[0, 1:2, :], second[0, 1:2, :])
            inputs[pl.ds(turn * TOKENS, TOKENS)] = (normed * (1.0 + scale) + shift).astype(jnp.bfloat16)

    raw = jnp.dot(inputs[...], weights[...], preferred_element_type=jnp.float32)

    def put(result):
        result = result.astype(jnp.bfloat16)
        for head in range(HEADS):
            columns = slice(head * HD, (head + 1) * HD)
            away[head] = result[:TOKENS, columns]
            own[head] = result[TOKENS:, columns]

    @pl.when(part < 2)
    def _():
        row = jnp.where(part == 0, gains[0:1, :], gains[1:2, :])
        put(raw * lax.rsqrt(jnp.mean(raw * raw, axis=-1, keepdims=True) + 1e-06) * row)

    @pl.when(part == 2)
    def _():
        put(raw)


def project(tokens, projection, norm_gain, modulation, levels, core):
    info = jnp.concatenate([core[None], levels])
    return pl.pallas_call(
        project_kernel,
        grid_spec=pltpu.PrefetchScalarGridSpec(
            num_scalar_prefetch=1,
            grid=(3,),
            in_specs=[
                pl.BlockSpec((2, TOKENS, D), lambda p, info: (0, 0, 0)),
                pl.BlockSpec((D, QD), lambda p, info: (0, p)),
                pl.BlockSpec((2, QD), lambda p, info: (0, 0)),
                pl.BlockSpec((1, 2, D), lambda p, info: (info[1], 0, 0)),
                pl.BlockSpec((1, 2, D), lambda p, info: (info[2], 0, 0)),
            ],
            out_specs=[
                pl.BlockSpec((SLOTS, TOKENS, HD), lambda p, info: (info[0], p, 0)),
                pl.BlockSpec((SLOTS, TOKENS, HD), lambda p, info: (0, p, 0)),
            ],
            scratch_shapes=[pltpu.VMEM((2 * TOKENS, D), jnp.bfloat16)],
        ),
        out_shape=[
            jax.ShapeDtypeStruct((CHIPS, LENGTH, HD), jnp.bfloat16),
            jax.ShapeDtypeStruct((SLOTS, 3 * TOKENS, HD), jnp.bfloat16),
        ],
        compiler_params=pltpu.CompilerParams(vmem_limit_bytes=48 * 1024 * 1024),
        name="project",
    )(info, tokens, projection, norm_gain, modulation, modulation)


STREAMS = 2
EACH = CHIPS // STREAMS
WIDE = 512
LIMIT = EACH * (FRAMES * TOKENS // WIDE)
ROWS = STREAMS * (EACH + 1)


def plan(core, size, slots, chips, pick, block, left):
    def visit(turn, carry):
        place = carry[0]
        time = FRAMES - 1 - turn
        slot = slots[time]
        mine = slot % 2 == core
        lane = place % (2 * STREAMS)
        stream = jnp.where(lane < STREAMS, lane, 2 * STREAMS - 1 - lane)
        row = place // STREAMS
        rows = (time + 1) * size
        count = jnp.where(mine, (rows + WIDE - 1) // WIDE, 0)
        used = carry[1]
        for other in range(1, STREAMS):
            used = jnp.where(stream == other, carry[1 + other], used)

        @pl.when(mine)
        def _():
            chips[row * STREAMS + stream] = slot // 2

        def fill(step, inner):
            pick[stream, used + step] = row
            block[stream, used + step] = step
            left[stream, used + step] = rows - step * WIDE
            return inner

        lax.fori_loop(0, count, fill, 0)
        grown = tuple(carry[1 + s] + jnp.where(stream == s, count, 0) for s in range(STREAMS))
        return (place + jnp.where(mine, 1, 0),) + grown

    zero = jnp.int32(0)
    totals = lax.fori_loop(0, FRAMES, visit, (zero,) + (zero,) * STREAMS)[1:]
    trip = functools.reduce(jnp.maximum, totals)
    for stream in range(STREAMS):

        def clear(step, carry):
            pick[stream, step] = EACH
            block[stream, step] = 0
            left[stream, step] = WIDE
            return carry

        lax.fori_loop(totals[stream], trip + 2, clear, 0)
    return trip


def fold(values, combine):
    return combine(values.reshape(values.shape[0] // 8, 8, values.shape[1]), axis=0)


def sweep(trip, scored, queries, keys, values, tops, totals, mixes, pick, block, left, raws):
    def spots_of(step):
        spots = []
        for stream in range(STREAMS):
            row = pick[stream, step] * STREAMS + stream
            first = pl.multiple_of(block[stream, step] * WIDE, WIDE)
            spots.append((row, pl.ds(first, WIDE)))
        return spots

    def ask(step, slot):
        for stream, (row, rows) in enumerate(spots_of(step)):
            raws[slot][stream][...] = jnp.dot(keys[rows], queries[row], preferred_element_type=jnp.float32)

    def answer(step, slot):
        spots = spots_of(step)
        weighed = []
        for stream, (row, rows) in enumerate(spots):
            scores = scored(raws[slot][stream][...], rows, left[stream, step])
            highest = jnp.max(fold(scores, jnp.max), axis=0, keepdims=True) * SCALE
            top = tops[row]
            newest = jnp.maximum(top, highest)
            rescale = jnp.exp2(top - newest)
            weights = jnp.exp2(scores * SCALE - newest[0:1])
            total = totals[row] * rescale + fold(weights, jnp.sum)
            weighed.append((newest, total, rescale, weights.astype(jnp.bfloat16)))
        fresh = [jnp.dot(values[:, rows], weighed[stream][3], preferred_element_type=jnp.float32) for stream, (row, rows) in enumerate(spots)]
        mixed = [mixes[row] * weighed[stream][2][0:1] + fresh[stream] for stream, (row, rows) in enumerate(spots)]
        for stream, (row, rows) in enumerate(spots):
            tops[row] = weighed[stream][0]
            totals[row] = weighed[stream][1]
            mixes[row] = mixed[stream]

    def body(pair, carry):
        ask(2 * pair + 1, 1)
        answer(2 * pair, 0)
        ask(2 * pair + 2, 0)
        answer(2 * pair + 1, 1)
        return carry

    ask(0, 0)
    lax.fori_loop(0, (trip + 1) // 2, body, 0)


def gather_frames(slots, core, near, far, moves, sem):
    def start(time, carry):
        slot = slots[time]
        chip = slot // 2
        mine = slot % 2 == core

        def copy(source):
            for number, (first, size, target) in enumerate(moves):
                rows = pl.ds(pl.multiple_of(time * size, size), size)
                pltpu.make_async_copy(source.at[chip, pl.ds(first, size)], target.at[rows], sem.at[number]).start()

        pl.when(mine)(lambda: copy(near))
        pl.when(jnp.logical_not(mine))(lambda: copy(far))
        return carry

    lax.fori_loop(0, FRAMES, start, 0)


def turn_values(staged, values, total):
    def turn(step, carry):
        rows = pl.ds(pl.multiple_of(step * WIDE, WIDE), WIDE)
        values[:, rows] = staged[rows].T
        return carry

    lax.fori_loop(0, total // WIDE, turn, 0)


def turn_queries(chips, staged, queries):
    for place in range(CHIPS):
        queries[place] = staged[chips[place]].T


def attend_kernel(info, near, far, bias, out, *scratch):
    tops, totals, mixes, asked, queries, keys, staged, values, rim_keys, rim_staged, rim_values, slots, chips = scratch[:13]
    lists, rim_lists, sem, raws = scratch[13:16], scratch[16:19], scratch[19], scratch[20:]
    raws = (raws[:STREAMS], raws[STREAMS:])
    core = info[FRAMES]
    for slot in range(FRAMES):
        slots[info[slot]] = slot
    asking = pltpu.make_async_copy(near.at[:, pl.ds(0, TOKENS)], asked, sem.at[4])
    asking.start()
    rim_at = 3 * TOKENS
    moves = (
        (TOKENS, TOKENS, keys),
        (2 * TOKENS, TOKENS, staged),
        (rim_at, RIM, rim_keys),
        (rim_at + RIM, RIM, rim_staged),
    )
    gather_frames(slots, core, near, far, moves, sem)
    trip = plan(core, TOKENS, slots, chips, *lists)
    rim_trip = plan(core, RIM, slots, chips, *rim_lists)
    tops[...] = jnp.full(tops.shape, LOWEST, jnp.float32)
    totals[...] = jnp.zeros(totals.shape, jnp.float32)
    mixes[...] = jnp.zeros(mixes.shape, jnp.float32)
    queries[pl.ds(CHIPS, STREAMS)] = jnp.zeros((STREAMS, HD, TOKENS), jnp.bfloat16)
    asking.wait()
    turn_queries(chips, asked, queries)
    for number, move in enumerate(moves):
        pltpu.make_async_copy(move[2], move[2], sem.at[number]).wait()
    turn_values(staged, values, FRAMES * TOKENS)
    turn_values(rim_staged, rim_values, FRAMES * RIM)

    def scored(raw, rows, remain):
        half = WIDE // 2
        return jnp.concatenate([raw[:half], raw[half:] + jnp.where(remain < WIDE, LOWEST, 0.0)], axis=0)

    sweep(trip, scored, queries, keys, values, tops, totals, mixes, *lists, raws)

    def rim_scored(raw, rows, remain):
        place = lax.broadcasted_iota(jnp.int32, (WIDE, HD), 0)
        added = jnp.where(place < remain, bias[rows], LOWEST)
        return jnp.concatenate([raw[:, :HD] + added, raw[:, HD:] + added], axis=1)

    sweep(rim_trip, rim_scored, queries, rim_keys, rim_values, tops, totals, mixes, *rim_lists, raws)
    for place in range(CHIPS):
        whole = jnp.sum(totals[place], axis=0, keepdims=True)
        out[chips[place]] = (mixes[place] / whole).T.astype(jnp.bfloat16)


def attend(info, near, far, bias):
    lists = [pltpu.SMEM((STREAMS, LIMIT + 2), jnp.int32)] * 3
    return pl.pallas_call(
        attend_kernel,
        grid_spec=pltpu.PrefetchScalarGridSpec(
            num_scalar_prefetch=1,
            grid=(1,),
            in_specs=[
                pl.BlockSpec(memory_space=pl.ANY),
                pl.BlockSpec(memory_space=pl.ANY),
                pl.BlockSpec(bias.shape, lambda i, info: (0, 0)),
            ],
            out_specs=pl.BlockSpec((CHIPS, TOKENS, HD), lambda i, info: (0, 0, 0)),
            scratch_shapes=[
                pltpu.VMEM((ROWS, 8, TOKENS), jnp.float32),
                pltpu.VMEM((ROWS, 8, TOKENS), jnp.float32),
                pltpu.VMEM((ROWS, HD, TOKENS), jnp.float32),
                pltpu.VMEM((CHIPS, TOKENS, HD), jnp.bfloat16),
                pltpu.VMEM((ROWS, HD, TOKENS), jnp.bfloat16),
                pltpu.VMEM((FRAMES * TOKENS, HD), jnp.bfloat16),
                pltpu.VMEM((FRAMES * TOKENS, HD), jnp.bfloat16),
                pltpu.VMEM((HD, FRAMES * TOKENS), jnp.bfloat16),
                pltpu.VMEM((FRAMES * RIM, HD), jnp.bfloat16),
                pltpu.VMEM((FRAMES * RIM, HD), jnp.bfloat16),
                pltpu.VMEM((HD, FRAMES * RIM), jnp.bfloat16),
                pltpu.SMEM((FRAMES,), jnp.int32),
                pltpu.SMEM((CHIPS,), jnp.int32),
            ]
            + lists
            + lists
            + [pltpu.SemaphoreType.DMA((5,))]
            + [pltpu.VMEM((WIDE, TOKENS), jnp.float32)] * (2 * STREAMS),
        ),
        out_shape=jax.ShapeDtypeStruct((CHIPS, TOKENS, HD), jnp.bfloat16),
        compiler_params=pltpu.CompilerParams(vmem_limit_bytes=48 * 1024 * 1024),
        name="attend",
    )(info, near, far, bias)


def swap_cores(value):
    return lax.ppermute(value, "ha", [(i, i ^ 1) for i in range(8)])


def swap_depth(value, bits):
    return lax.ppermute(value, "ha", [(i, i ^ (2 * bits)) for i in range(8)])


def rim_rows(pair, depth):
    even = depth % 2 == 0
    upper = depth < 2

    def edge(strip):
        return jnp.where(upper, strip[..., TILE - PAD :, :, :], strip[..., :PAD, :, :])

    sent = jnp.where(even, pair[1, :, :, :, TILE - PAD :], pair[0, :, :, :, :PAD])
    outer = swap_depth(sent, 1)
    above = swap_depth(edge(pair), 2)
    corner = swap_depth(edge(sent), 3)
    inner = (pair[1, :, :, :, :PAD], pair[0, :, :, :, TILE - PAD :])
    inner_corner = (above[1, :, :, :, :PAD], above[0, :, :, :, TILE - PAD :])
    spare = jnp.zeros((SLOTS, 2, RIM - 104, HD), jnp.bfloat16)

    def flat(piece):
        return piece.reshape(SLOTS, 2, -1, HD)

    both = []
    for tile in range(2):
        rows = [inner[tile], above[tile], inner_corner[tile], outer, corner]
        both.append(jnp.concatenate([flat(r) for r in rows] + [spare], axis=2))
    return jnp.concatenate(both, axis=0).reshape(CHIPS, 2 * RIM, HD)


def rim_bias(outer_valid):
    place = jnp.arange(RIM, dtype=jnp.int32)
    valid = (place < 68) | ((place < 104) & outer_valid)
    column_of = jnp.tile(jnp.where(valid, 0.0, LOWEST).astype(jnp.float32), FRAMES)
    return jnp.broadcast_to(column_of[:, None], (FRAMES * RIM, HD))


def shards(tokens, projection, norm_gain, modulation, levels, frame_order):
    chip = lax.axis_index("tm")
    place = lax.axis_index("ha")
    depth = place // 2
    core = place % 2
    sending, away = project(tokens.reshape(2, TOKENS, D), projection, norm_gain, modulation, levels, core)
    other = swap_cores(away)
    first = (1 - core) * SLOTS
    sending = lax.dynamic_update_slice(sending, other, (first, 0, 0))
    pair = sending[:, TOKENS : 3 * TOKENS].reshape(2, SLOTS, 2, TILE, TILE, HD)
    sending = lax.dynamic_update_slice(sending, rim_rows(pair, depth), (0, 3 * TOKENS, 0))
    received = lax.all_to_all(sending, "tm", 0, 0, tiled=True)
    far = swap_cores(received)

    info = jnp.concatenate([frame_order, core[None]])
    odd_tile = chip // SLOTS
    bias = rim_bias(depth % 2 != odd_tile)
    mixed = attend(info, received, far, bias)

    back = lax.all_to_all(mixed, "tm", 0, 0, tiled=True)
    stay = lax.dynamic_slice_in_dim(back, core * SLOTS, HEADS, 0)
    leave = lax.dynamic_slice_in_dim(back, (1 - core) * SLOTS, HEADS, 0)
    come = swap_cores(leave)
    both = jnp.where(core == 0, jnp.stack([stay, come]), jnp.stack([come, stay]))
    return both.transpose(0, 2, 1, 3).reshape(2, 1, TILE, TILE, QD)


def solution(mesh):
    in_specs = (P("tm", "ha", None, None, None), P(), P(), P(), P("tm"), P())
    out_specs = P("tm", "ha", None, None, None)
    return jax.shard_map(shards, mesh=mesh, in_specs=in_specs, out_specs=out_specs, check_vma=False)
```

time: 200 us -> 182 us (0.910)
  starting transfers between devices: 42.3 us -> 15.7 us
  waiting for transfers between devices: 18.3 us -> 34.2 us
  blocking collectives: 45.3 us -> 54.5 us
  Pallas kernels: 70.3 us -> 61.7 us
  local copies, waits for them, and re-layouts: 18.8 us -> 11.3 us
    ppermute x4 -> x3, starting transfers between devices: 18.7 us -> 7.32 us  [swap_cores(): return lax.ppermute(value, 'ha', [(i, i ^ 1) for i in range(8)])]
    ppermute x5 -> x3, starting transfers between devices: 14.5 us -> 4.66 us  [swap_depth(): return lax.ppermute(value, 'ha', [(i, i ^ 2 * bits) for i in range(8)])]
    all_to_all x1, blocking collectives: 45.3 us -> 54.5 us  [shards(): received = lax.all_to_all(sending, 'tm', 0, 0, tiled=True)]
    ppermute x5 -> x3, waiting for transfers between devices: 0.01 us -> 8.24 us  [swap_depth(): return lax.ppermute(value, 'ha', [(i, i ^ 2 * bits) for i in range(8)])]
    pallas_call x2 -> x1, Pallas kernels: 59.6 us -> 52.5 us  [attend(): pl.pallas_call(attend_kernel, grid_spec=pltpu.PrefetchScalarGridSpec(num_...]
    all_to_all x1, starting transfers between devices: 9.19 us -> 3.66 us  [shards(): back = lax.all_to_all(mixed, 'tm', 0, 0, tiled=True)]
    ppermute x4 -> x3, waiting for transfers between devices: 6.39 us -> 11.2 us  [swap_cores(): return lax.ppermute(value, 'ha', [(i, i ^ 1) for i in range(8)])]
    unnamed x22 -> x8, local copies, waits for them, and re-layouts: 7.73 us -> 3.17 us
  transfers between devices with their start and end apart: 10 -> 7, of which waited for: 4 -> 7; matrix products, arithmetic and copies ran while one was open for 2% -> 0% of each run, Pallas kernels for 18% -> 0%
where the time goes in v3:
time: 182 us; the launch traced here: 179 us
  Pallas kernels  61.7 us (34%)
  blocking collectives  54.5 us (30%)
  waiting for transfers between devices  34.2 us (19%)
  starting transfers between devices  15.7 us (9%)
  local copies, waits for them, and re-layouts  11.3 us (6%)
    all_to_all x1, blocking collectives, shards(): received = lax.all_to_all(sending, 'tm', 0, 0, tiled=True)  54.5 us
    pallas_call x1, Pallas kernels, attend(): pl.pallas_call(attend_kernel, grid_spec=pltpu.PrefetchScalarGridSpec(num_...  52.5 us
    all_to_all x1, waiting for transfers between devices, shards(): back = lax.all_to_all(mixed, 'tm', 0, 0, tiled=True)  14.8 us
    ppermute x3, waiting for transfers between devices, swap_cores(): return lax.ppermute(value, 'ha', [(i, i ^ 1) for i in range(8)])  11.2 us
    pallas_call x1, Pallas kernels, project(): pl.pallas_call(project_kernel, grid_spec=pltpu.PrefetchScalarGridSpec(num...  9.18 us
    ppermute x3, waiting for transfers between devices, swap_depth(): return lax.ppermute(value, 'ha', [(i, i ^ 2 * bits) for i in range(8)])  8.24 us
    ppermute x3, starting transfers between devices, swap_cores(): return lax.ppermute(value, 'ha', [(i, i ^ 1) for i in range(8)])  7.32 us
    ppermute x3, starting transfers between devices, swap_depth(): return lax.ppermute(value, 'ha', [(i, i ^ 2 * bits) for i in range(8)])  4.66 us
  transfers between devices with their start and end apart: 7, of which 7 were waited for; matrix products, arithmetic and copies ran while one was open for 0% of the time, Pallas kernels for 0%

profile of v3, /device:TPU:1, one launch (start us, length us, event | category | flops | bytes accessed | tf_op | source)
XLA Modules:
  0.0 178.9 jit_solution(15608980477718077953)
XLA Ops:
  0.0 0.7 pad_add_fusion.1.info
  0.7 1.1 copy-done
  1.8 1.4 copy-done.1
  3.2 0.7 copy-done.2
  3.9 9.2 %project.1 = (bf16[16,992,128]{2,1,0:T(8,128)(2,1)}, bf16[8,768,128]{2,1,0:T(8,128)(2,1)S(1)}) custom-call(s32[3]{0:T(128)S(1)} %pad_add_fusion.1.info, bf16[2,256,1536]{2,1,0:T(8,128)(2,1)S(1)} %bitcast.20, bf16[1536,2304]{1,0:T(8,128)(2,1)} %weights.1, f32[2,768]{1,0:T(2,128)S(1)} %copy-done.2, f32[50,2,1536]{2,1,0:T(2,128)S(1)} %copy-done, ...), custom_call_target="tpu_custom_call" | custom-call | tf_op jit(solution)/shard_map/project/pallas_call | solution.py:67
  13.1 1.4 collective-permute-start
  14.5 3.0 %collective-permute-done = bf16[8,768,128]{2,1,0:T(8,128)(2,1)S(1)} collective-permute-done((bf16[8,768,128]{2,1,0:T(8,128)(2,1)S(1)}, bf16[8,768,128]{2,1,0:T(8,128)(2,1)S(1)}, u32[]{:S(2)}, u32[]{:S(2)}) %collective-permute-start) | collective-permute-done | bytes 1572896 | tf_op jit(solution)/shard_map/ppermute | solution.py:311
  17.5 1.4 constant_dynamic-update-slice_fusion.1
  19.0 1.7 slice.52
  20.8 3.8 %collective-permute-start.1 = (bf16[2,8,2,2,16,128]{5,4,3,2,1,0:T(8,128)(2,1)S(1)}, bf16[2,8,2,2,16,128]{5,4,3,2,1,0:T(8,128)(2,1)S(1)}, u32[]{:S(2)}, u32[]{:S(2)}) collective-permute-start(bf16[2,8,2,2,16,128]{5,4,3,2,1,0:T(8,128)(2,1)S(1)} %slice_select_fusion), channel_id=1, source_target_pairs={{0,4},{1,5},{2,6},{3,7},{4,0},{5,1},{6,2},{7,3},{8,12},{9,13},{10,... | collective-permute-start | bytes 786440 | tf_op jit(solution)/shard_map/ppermute | solution.py:315
  24.9 0.8 collective-permute-start.2
  25.9 5.0 %collective-permute-done.1 = bf16[2,8,2,2,16,128]{5,4,3,2,1,0:T(8,128)(2,1)S(1)} collective-permute-done((bf16[2,8,2,2,16,128]{5,4,3,2,1,0:T(8,128)(2,1)S(1)}, bf16[2,8,2,2,16,128]{5,4,3,2,1,0:T(8,128)(2,1)S(1)}, u32[]{:S(2)}, u32[]{:S(2)}) %collective-permute-start.1) | collective-permute-done | bytes 262176 | tf_op jit(solution)/shard_map/ppermute | solution.py:315
  31.4 2.8 %collective-permute-done.2 = bf16[8,2,16,2,128]{4,3,2,1,0:T(2,128)(2,1)S(1)} collective-permute-done((bf16[8,2,16,2,128]{4,3,2,1,0:T(2,128)(2,1)S(1)}, bf16[8,2,16,2,128]{4,3,2,1,0:T(2,128)(2,1)S(1)}, u32[]{:S(2)}, u32[]{:S(2)}) %collective-permute-start.2) | collective-permute-done | bytes 131104 | tf_op jit(solution)/shard_map/ppermute | solution.py:315
  35.1 1.1 constant_dynamic-update-slice_fusion
  36.2 54.5 %all_to_all.10.near = bf16[16,992,128]{2,1,0:T(8,128)(2,1)} all-to-all(bf16[16,992,128]{2,1,0:T(8,128)(2,1)} %constant_dynamic-update-slice_fusion), channel_id=1, replica_groups=mesh['tm'=16,'ha'=8] {'tm'}, dimensions={0} | all-to-all | bytes 8126464 | tf_op jit(solution)/shard_map/all_to_all | solution.py:361
  90.7 2.6 %collective-permute-start.4 = (bf16[16,992,128]{2,1,0:T(8,128)(2,1)}, bf16[16,992,128]{2,1,0:T(8,128)(2,1)}, u32[]{:S(2)}, u32[]{:S(2)}) collective-permute-start(bf16[16,992,128]{2,1,0:T(8,128)(2,1)} %all_to_all.10.near), channel_id=1, source_target_pairs={{0,1},{1,0},{2,3},{3,2},{4,5},{5,4},{6,7},{7,6},{8,9},{9,8},{10,11... | collective-permute-start | bytes 12189704 | tf_op jit(solution)/shard_map/ppermute | solution.py:311
  93.4 6.8 %collective-permute-done.4.far = bf16[16,992,128]{2,1,0:T(8,128)(2,1)} collective-permute-done((bf16[16,992,128]{2,1,0:T(8,128)(2,1)}, bf16[16,992,128]{2,1,0:T(8,128)(2,1)}, u32[]{:S(2)}, u32[]{:S(2)}) %collective-permute-start.4) | collective-permute-done | bytes 4063264 | tf_op jit(solution)/shard_map/ppermute | solution.py:311
  100.7 52.5 %attend.1 = bf16[16,256,128]{2,1,0:T(8,128)(2,1)} custom-call(s32[33]{0:T(128)S(1)} %pad_add_fusion.info, bf16[16,992,128]{2,1,0:T(8,128)(2,1)} %all_to_all.10.near, bf16[16,992,128]{2,1,0:T(8,128)(2,1)} %collective-permute-done.4.far, f32[3584,128]{1,0:T(8,128)S(1)} %broadcast_in_dim.27.bias), custom_call_target="tpu_custom_call" | custom-call | tf_op jit(solution)/shard_map/attend/pallas_call | solution.py:273
  153.3 3.7 %all-to-all-start.1 = ((bf16[16,256,128]{2,1,0:T(8,128)(2,1)}), bf16[16,256,128]{2,1,0:T(8,128)(2,1)S(1)}, u32[]{:S(2)}, u32[]{:S(2)}) async-start(bf16[16,256,128]{2,1,0:T(8,128)(2,1)} %attend.1), calls=%async_computation.1 | async-start | bytes 2097152 | tf_op jit(solution)/shard_map/all_to_all | solution.py:369
  157.0 14.8 %all-to-all-done.1 = bf16[16,256,128]{2,1,0:T(8,128)(2,1)S(1)} async-done(((bf16[16,256,128]{2,1,0:T(8,128)(2,1)}), bf16[16,256,128]{2,1,0:T(8,128)(2,1)S(1)}, u32[]{:S(2)}, u32[]{:S(2)}) %all-to-all-start.1) | async-done | bytes 1048608 | tf_op jit(solution)/shard_map/all_to_all | solution.py:369
  171.8 3.3 %collective-permute-start.5 = (bf16[6,256,128]{2,1,0:T(8,128)(2,1)S(1)}, bf16[6,256,128]{2,1,0:T(8,128)(2,1)S(1)}, u32[]{:S(2)}, u32[]{:S(2)}) collective-permute-start(bf16[6,256,128]{2,1,0:T(8,128)(2,1)S(1)} %get-tuple-element.13), channel_id=1, source_target_pairs={{0,1},{1,0},{2,3},{3,2},{4,5},{5,4},{6,7},{7,6},{8,9},{9,8},{10,11... | collective-permute-start | bytes 1179656 | tf_op jit(solution)/shard_map/ppermute | solution.py:311
  175.1 1.3 collective-permute-done.5
  176.6 0.5 copy.7
  177.2 1.8 reshape.37
  (23 shorter events, 2.7 us)
Async XLA Ops:
  0.7 1.1 copy-start
  1.8 1.4 copy-start.1
  3.2 0.7 copy-start.2
  13.1 4.4 %collective-permute-start = (bf16[8,768,128]{2,1,0:T(8,128)(2,1)S(1)}, bf16[8,768,128]{2,1,0:T(8,128)(2,1)S(1)}, u32[]{:S(2)}, u32[]{:S(2)}) collective-permute-start(bf16[8,768,128]{2,1,0:T(8,128)(2,1)S(1)} %get-tuple-element.8), channel_id=1, source_target_pairs={{0,1},{1,0},{2,3},{3,2},{4,5},{5,4},{6,7},{7,6},{8,9},{9,8},{10,11... | collective-permute-start | bytes 4718600 | tf_op jit(solution)/shard_map/ppermute | solution.py:311
  20.8 10.1 %collective-permute-start.1 = (bf16[2,8,2,2,16,128]{5,4,3,2,1,0:T(8,128)(2,1)S(1)}, bf16[2,8,2,2,16,128]{5,4,3,2,1,0:T(8,128)(2,1)S(1)}, u32[]{:S(2)}, u32[]{:S(2)}) collective-permute-start(bf16[2,8,2,2,16,128]{5,4,3,2,1,0:T(8,128)(2,1)S(1)} %slice_select_fusion), channel_id=1, source_target_pairs={{0,4},{1,5},{2,6},{3,7},{4,0},{5,1},{6,2},{7,3},{8,12},{9,13},{10,... | collective-permute-start | bytes 786440 | tf_op jit(solution)/shard_map/ppermute | solution.py:315
  24.9 9.2 %collective-permute-start.2 = (bf16[8,2,16,2,128]{4,3,2,1,0:T(2,128)(2,1)S(1)}, bf16[8,2,16,2,128]{4,3,2,1,0:T(2,128)(2,1)S(1)}, u32[]{:S(2)}, u32[]{:S(2)}) collective-permute-start(bf16[8,2,16,2,128]{4,3,2,1,0:T(2,128)(2,1)S(1)} %get-tuple-element.10), channel_id=1, source_target_pairs={{0,2},{1,3},{2,0},{3,1},{4,6},{5,7},{6,4},{7,5},{8,10},{9,11},{10,... | collective-permute-start | bytes 393224 | tf_op jit(solution)/shard_map/ppermute | solution.py:315
  25.8 5.6 %collective-permute-start.3 = (bf16[8,2,2,2,128]{4,3,2,1,0:T(2,128)(2,1)S(1)}, bf16[8,2,2,2,128]{4,3,2,1,0:T(2,128)(2,1)S(1)}, u32[]{:S(2)}, u32[]{:S(2)}) collective-permute-start(bf16[8,2,2,2,128]{4,3,2,1,0:T(2,128)(2,1)S(1)} %broadcast_select_fusion.1), channel_id=1, source_target_pairs={{0,6},{1,7},{2,4},{3,5},{4,2},{5,3},{6,0},{7,1},{8,14},{9,15},{10,... | collective-permute-start | bytes 49160 | tf_op jit(solution)/shard_map/ppermute | solution.py:315
  36.2 57.2 %copy-start.3 = (s32[32]{0:T(128)S(1)}, s32[32]{0:T(128)}, u32[]{:S(2)}) copy-start(s32[32]{0:T(128)} %param.11) | copy-start | bytes 388
  90.7 9.6 %collective-permute-start.4 = (bf16[16,992,128]{2,1,0:T(8,128)(2,1)}, bf16[16,992,128]{2,1,0:T(8,128)(2,1)}, u32[]{:S(2)}, u32[]{:S(2)}) collective-permute-start(bf16[16,992,128]{2,1,0:T(8,128)(2,1)} %all_to_all.10.near), channel_id=1, source_target_pairs={{0,1},{1,0},{2,3},{3,2},{4,5},{5,4},{6,7},{7,6},{8,9},{9,8},{10,11... | collective-permute-start | bytes 12189704 | tf_op jit(solution)/shard_map/ppermute | solution.py:311
  153.3 18.5 %all-to-all-start.1 = ((bf16[16,256,128]{2,1,0:T(8,128)(2,1)}), bf16[16,256,128]{2,1,0:T(8,128)(2,1)S(1)}, u32[]{:S(2)}, u32[]{:S(2)}) async-start(bf16[16,256,128]{2,1,0:T(8,128)(2,1)} %attend.1), calls=%async_computation.1 | async-start | bytes 2097152 | tf_op jit(solution)/shard_map/all_to_all | solution.py:369
  171.8 4.7 %collective-permute-start.5 = (bf16[6,256,128]{2,1,0:T(8,128)(2,1)S(1)}, bf16[6,256,128]{2,1,0:T(8,128)(2,1)S(1)}, u32[]{:S(2)}, u32[]{:S(2)}) collective-permute-start(bf16[6,256,128]{2,1,0:T(8,128)(2,1)S(1)} %get-tuple-element.13), channel_id=1, source_target_pairs={{0,1},{1,0},{2,3},{3,2},{4,5},{5,4},{6,7},{7,6},{8,9},{9,8},{10,11... | collective-permute-start | bytes 1179656 | tf_op jit(solution)/shard_map/ppermute | solution.py:311

commit v4 on v3

--- a/solution.py
+++ b/solution.py
@@ -26,12 +26,19 @@
 AXES = ("tm", "ha")
 
 
-def project_kernel(info, tokens, weights, gains, first, second, own, away, inputs):
+def project_kernel(info, tokens_hbm, weights, gains, modulation, own, away, inputs, tokens, rows, sem):
     part = pl.program_id(0)
     core = info[0]
 
     @pl.when(part == 0)
     def _():
+        copies = [pltpu.make_async_copy(tokens_hbm, tokens, sem.at[0])]
+        for frame in range(2):
+            copies.append(pltpu.make_async_copy(modulation.at[info[1 + frame]], rows.at[frame], sem.at[1 + frame]))
+        for copy in copies:
+            copy.start()
+        for copy in copies:
+            copy.wait()
         for turn in range(2):
             frame = 1 - core if turn == 0 else core
             values = tokens[frame].astype(jnp.float32)
@@ -39,8 +46,8 @@
             centred = values - average
             spread = jnp.mean(centred * centred, axis=-1, keepdims=True)
             normed = centred * lax.rsqrt(spread + 1e-06)
-            shift = jnp.where(frame == 0, first[0, 0:1, :], second[0, 0:1, :])
-            scale = jnp.where(frame == 0, first[0, 1:2, :], second[0, 1:2, :])
+            shift = rows[frame, 0:1, :]
+            scale = rows[frame, 1:2, :]
             inputs[pl.ds(turn * TOKENS, TOKENS)] = (normed * (1.0 + scale) + shift).astype(jnp.bfloat16)
 
     raw = jnp.dot(inputs[...], weights[...], preferred_element_type=jnp.float32)
@@ -60,6 +67,10 @@
     @pl.when(part == 2)
     def _():
         put(raw)
+
+
+def in_hbm(value):
+    return pltpu.with_memory_space_constraint(value, pltpu.HBM)
 
 
 def project(tokens, projection, norm_gain, modulation, levels, core):
@@ -70,17 +81,21 @@
             num_scalar_prefetch=1,
             grid=(3,),
             in_specs=[
-                pl.BlockSpec((2, TOKENS, D), lambda p, info: (0, 0, 0)),
+                pl.BlockSpec(memory_space=pltpu.HBM),
                 pl.BlockSpec((D, QD), lambda p, info: (0, p)),
                 pl.BlockSpec((2, QD), lambda p, info: (0, 0)),
-                pl.BlockSpec((1, 2, D), lambda p, info: (info[1], 0, 0)),
-                pl.BlockSpec((1, 2, D), lambda p, info: (info[2], 0, 0)),
+                pl.BlockSpec(memory_space=pltpu.HBM),
             ],
             out_specs=[
                 pl.BlockSpec((SLOTS, TOKENS, HD), lambda p, info: (info[0], p, 0)),
                 pl.BlockSpec((SLOTS, TOKENS, HD), lambda p, info: (0, p, 0)),
             ],
-            scratch_shapes=[pltpu.VMEM((2 * TOKENS, D), jnp.bfloat16)],
+            scratch_shapes=[
+                pltpu.VMEM((2 * TOKENS, D), jnp.bfloat16),
+                pltpu.VMEM((2, TOKENS, D), jnp.bfloat16),
+                pltpu.VMEM((2, 2, D), jnp.float32),
+                pltpu.SemaphoreType.DMA((3,)),
+            ],
         ),
         out_shape=[
             jax.ShapeDtypeStruct((CHIPS, LENGTH, HD), jnp.bfloat16),
@@ -88,22 +103,23 @@
         ],
         compiler_params=pltpu.CompilerParams(vmem_limit_bytes=48 * 1024 * 1024),
         name="project",
-    )(info, tokens, projection, norm_gain, modulation, modulation)
-
-
-STREAMS = 2
+    )(info, in_hbm(tokens), projection, norm_gain, in_hbm(modulation))
+
+
+STREAMS = 4
 EACH = CHIPS // STREAMS
 WIDE = 512
+PIECE = 256
 LIMIT = EACH * (FRAMES * TOKENS // WIDE)
 ROWS = STREAMS * (EACH + 1)
 
 
-def plan(core, size, slots, chips, pick, block, left):
+def plan(core, size, slots, bits, chips, pick, block, left):
     def visit(turn, carry):
         place = carry[0]
         time = FRAMES - 1 - turn
         slot = slots[time]
-        mine = slot % 2 == core
+        mine = (slot + bits[slot // 2] + core) % 2 == 0
         lane = place % (2 * STREAMS)
         stream = jnp.where(lane < STREAMS, lane, 2 * STREAMS - 1 - lane)
         row = place // STREAMS
@@ -146,46 +162,57 @@
     return combine(values.reshape(values.shape[0] // 8, 8, values.shape[1]), axis=0)
 
 
-def sweep(trip, scored, queries, keys, values, tops, totals, mixes, pick, block, left, raws):
+def sweep(trip, scored, queries, keys, values, tops, totals, mixes, pick, block, left, raws, peaks):
     def spots_of(step):
         spots = []
         for stream in range(STREAMS):
             row = pick[stream, step] * STREAMS + stream
             first = pl.multiple_of(block[stream, step] * WIDE, WIDE)
-            spots.append((row, pl.ds(first, WIDE)))
+            spots.append((row, first, left[stream, step]))
         return spots
 
-    def ask(step, slot):
-        for stream, (row, rows) in enumerate(spots_of(step)):
-            raws[slot][stream][...] = jnp.dot(keys[rows], queries[row], preferred_element_type=jnp.float32)
-
-    def answer(step, slot):
-        spots = spots_of(step)
-        weighed = []
-        for stream, (row, rows) in enumerate(spots):
-            scores = scored(raws[slot][stream][...], rows, left[stream, step])
-            highest = jnp.max(fold(scores, jnp.max), axis=0, keepdims=True) * SCALE
+    def ask(spot, part):
+        row, first, remain = spot
+        rows = pl.ds(pl.multiple_of(first + part * PIECE, PIECE), PIECE)
+        raw = jnp.dot(keys[rows], queries[row], preferred_element_type=jnp.float32)
+        return scored(raw, rows, remain - part * PIECE)
+
+    def advance(step, slot):
+        now = spots_of(step)
+        then = spots_of(step + 1)
+        state = []
+        for stream, (row, first, remain) in enumerate(now):
+            highest = jnp.max(peaks[slot][stream][...], axis=0, keepdims=True) * SCALE
             top = tops[row]
             newest = jnp.maximum(top, highest)
             rescale = jnp.exp2(top - newest)
-            weights = jnp.exp2(scores * SCALE - newest[0:1])
-            total = totals[row] * rescale + fold(weights, jnp.sum)
-            weighed.append((newest, total, rescale, weights.astype(jnp.bfloat16)))
-        fresh = [jnp.dot(values[:, rows], weighed[stream][3], preferred_element_type=jnp.float32) for stream, (row, rows) in enumerate(spots)]
-        mixed = [mixes[row] * weighed[stream][2][0:1] + fresh[stream] for stream, (row, rows) in enumerate(spots)]
-        for stream, (row, rows) in enumerate(spots):
-            tops[row] = weighed[stream][0]
-            totals[row] = weighed[stream][1]
-            mixes[row] = mixed[stream]
+            state.append([newest, totals[row] * rescale, mixes[row] * rescale[0:1], None])
+        for part in range(WIDE // PIECE):
+            span = slice(part * PIECE, (part + 1) * PIECE)
+            for stream, (row, first, remain) in enumerate(now):
+                raw = ask(then[stream], part)
+                raws[1 - slot][stream][span] = raw
+                peak = fold(raw, jnp.max)
+                held = state[stream]
+                held[3] = peak if part == 0 else jnp.maximum(held[3], peak)
+                weights = jnp.exp2(raws[slot][stream][span] * SCALE - held[0][0:1])
+                held[1] = held[1] + fold(weights, jnp.sum)
+                columns = pl.ds(pl.multiple_of(first + part * PIECE, PIECE), PIECE)
+                held[2] = held[2] + jnp.dot(values[:, columns], weights.astype(jnp.bfloat16), preferred_element_type=jnp.float32)
+        for stream, (row, first, remain) in enumerate(now):
+            tops[row], totals[row], mixes[row], peaks[1 - slot][stream][...] = state[stream]
 
     def body(pair, carry):
-        ask(2 * pair + 1, 1)
-        answer(2 * pair, 0)
-        ask(2 * pair + 2, 0)
-        answer(2 * pair + 1, 1)
+        advance(2 * pair, 0)
+        advance(2 * pair + 1, 1)
         return carry
 
-    ask(0, 0)
+    for stream, spot in enumerate(spots_of(0)):
+        for part in range(WIDE // PIECE):
+            raw = ask(spot, part)
+            raws[0][stream][part * PIECE : (part + 1) * PIECE] = raw
+            peak = fold(raw, jnp.max)
+            peaks[0][stream][...] = peak if part == 0 else jnp.maximum(peaks[0][stream][...], peak)
     lax.fori_loop(0, (trip + 1) // 2, body, 0)
 
 
@@ -221,15 +248,27 @@
         queries[place] = staged[chips[place]].T
 
 
-def attend_kernel(info, near, far, bias, out, *scratch):
+def attend_kernel(info, near, far, bias, out, bits, *scratch):
     tops, totals, mixes, asked, queries, keys, staged, values, rim_keys, rim_staged, rim_values, slots, chips = scratch[:13]
     lists, rim_lists, sem, raws = scratch[13:16], scratch[16:19], scratch[19], scratch[20:]
-    raws = (raws[:STREAMS], raws[STREAMS:])
+    raws, peaks = raws[: 2 * STREAMS], raws[2 * STREAMS :]
+    raws, peaks = [(r[:STREAMS], r[STREAMS:]) for r in (raws, peaks)]
     core = info[FRAMES]
     for slot in range(FRAMES):
         slots[info[slot]] = slot
-    asking = pltpu.make_async_copy(near.at[:, pl.ds(0, TOKENS)], asked, sem.at[4])
-    asking.start()
+    ahead = jnp.int32(0)
+    for chip in range(CHIPS):
+        even = info[2 * chip]
+        odd = info[2 * chip + 1]
+        turned = (ahead >= 0) == (even > odd)
+        bits[chip] = jnp.where(turned, 1, 0)
+        ahead = ahead + jnp.where(turned, odd - even, even - odd)
+
+        def ask(source):
+            pltpu.make_async_copy(source.at[chip, pl.ds(0, TOKENS)], asked.at[chip], sem.at[4]).start()
+
+        pl.when(turned)(lambda: ask(far))
+        pl.when(jnp.logical_not(turned))(lambda: ask(near))
     rim_at = 3 * TOKENS
     moves = (
         (TOKENS, TOKENS, keys),
@@ -238,13 +277,13 @@
         (rim_at + RIM, RIM, rim_staged),
     )
     gather_frames(slots, core, near, far, moves, sem)
-    trip = plan(core, TOKENS, slots, chips, *lists)
-    rim_trip = plan(core, RIM, slots, chips, *rim_lists)
+    trip = plan(core, TOKENS, slots, bits, chips, *lists)
+    rim_trip = plan(core, RIM, slots, bits, chips, *rim_lists)
     tops[...] = jnp.full(tops.shape, LOWEST, jnp.float32)
     totals[...] = jnp.zeros(totals.shape, jnp.float32)
     mixes[...] = jnp.zeros(mixes.shape, jnp.float32)
     queries[pl.ds(CHIPS, STREAMS)] = jnp.zeros((STREAMS, HD, TOKENS), jnp.bfloat16)
-    asking.wait()
+    pltpu.make_async_copy(asked, asked, sem.at[4]).wait()
     turn_queries(chips, asked, queries)
     for number, move in enumerate(moves):
         pltpu.make_async_copy(move[2], move[2], sem.at[number]).wait()
@@ -252,17 +291,16 @@
     turn_values(rim_staged, rim_values, FRAMES * RIM)
 
     def scored(raw, rows, remain):
-        half = WIDE // 2
-        return jnp.concatenate([raw[:half], raw[half:] + jnp.where(remain < WIDE, LOWEST, 0.0)], axis=0)
-
-    sweep(trip, scored, queries, keys, values, tops, totals, mixes, *lists, raws)
+        return raw + jnp.where(remain <= 0, LOWEST, 0.0)
+
+    sweep(trip, scored, queries, keys, values, tops, totals, mixes, *lists, raws, peaks)
 
     def rim_scored(raw, rows, remain):
-        place = lax.broadcasted_iota(jnp.int32, (WIDE, HD), 0)
+        place = lax.broadcasted_iota(jnp.int32, (PIECE, HD), 0)
         added = jnp.where(place < remain, bias[rows], LOWEST)
         return jnp.concatenate([raw[:, :HD] + added, raw[:, HD:] + added], axis=1)
 
-    sweep(rim_trip, rim_scored, queries, rim_keys, rim_values, tops, totals, mixes, *rim_lists, raws)
+    sweep(rim_trip, rim_scored, queries, rim_keys, rim_values, tops, totals, mixes, *rim_lists, raws, peaks)
     for place in range(CHIPS):
         whole = jnp.sum(totals[place], axis=0, keepdims=True)
         out[chips[place]] = (mixes[place] / whole).T.astype(jnp.bfloat16)
@@ -280,7 +318,10 @@
                 pl.BlockSpec(memory_space=pl.ANY),
                 pl.BlockSpec(bias.shape, lambda i, info: (0, 0)),
             ],
-            out_specs=pl.BlockSpec((CHIPS, TOKENS, HD), lambda i, info: (0, 0, 0)),
+            out_specs=[
+                pl.BlockSpec((CHIPS, TOKENS, HD), lambda i, info: (0, 0, 0)),
+                pl.BlockSpec(memory_space=pltpu.SMEM),
+            ],
             scratch_shapes=[
                 pltpu.VMEM((ROWS, 8, TOKENS), jnp.float32),
                 pltpu.VMEM((ROWS, 8, TOKENS), jnp.float32),
@@ -299,9 +340,13 @@
             + lists
             + lists
             + [pltpu.SemaphoreType.DMA((5,))]
-            + [pltpu.VMEM((WIDE, TOKENS), jnp.float32)] * (2 * STREAMS),
+            + [pltpu.VMEM((WIDE, TOKENS), jnp.float32)] * (2 * STREAMS)
+            + [pltpu.VMEM((8, TOKENS), jnp.float32)] * (2 * STREAMS),
         ),
-        out_shape=jax.ShapeDtypeStruct((CHIPS, TOKENS, HD), jnp.bfloat16),
+        out_shape=[
+            jax.ShapeDtypeStruct((CHIPS, TOKENS, HD), jnp.bfloat16),
+            jax.ShapeDtypeStruct((CHIPS,), jnp.int32),
+        ],
         compiler_params=pltpu.CompilerParams(vmem_limit_bytes=48 * 1024 * 1024),
         name="attend",
     )(info, near, far, bias)
@@ -364,13 +409,14 @@
     info = jnp.concatenate([frame_order, core[None]])
     odd_tile = chip // SLOTS
     bias = rim_bias(depth % 2 != odd_tile)
-    mixed = attend(info, received, far, bias)
+    mixed, bits = attend(info, received, far, bias)
+    turned = lax.dynamic_index_in_dim(bits, chip, 0, keepdims=False)
 
     back = lax.all_to_all(mixed, "tm", 0, 0, tiled=True)
     stay = lax.dynamic_slice_in_dim(back, core * SLOTS, HEADS, 0)
     leave = lax.dynamic_slice_in_dim(back, (1 - core) * SLOTS, HEADS, 0)
     come = swap_cores(leave)
-    both = jnp.where(core == 0, jnp.stack([stay, come]), jnp.stack([come, stay]))
+    both = jnp.where(core == turned, jnp.stack([stay, come]), jnp.stack([come, stay]))
     return both.transpose(0, 2, 1, 3).reshape(2, 1, TILE, TILE, QD)
 
 

time: 182 us -> 172 us (0.945); the launches traced: 179 us -> 171 us
  Pallas kernels: 61.7 us -> 55.8 us
  starting transfers between devices: 15.7 us -> 12.4 us
    pallas_call x1, Pallas kernels: 52.5 us -> 45.7 us  [attend(): pl.pallas_call(attend_kernel, grid_spec=pltpu.PrefetchScalarGridSpec(num_...]
    ppermute x3, starting transfers between devices: 7.32 us -> 4.12 us  [swap_cores(): return lax.ppermute(value, 'ha', [(i, i ^ 1) for i in range(8)])]
  transfers between devices with their start and end apart: 7 -> 7, of which waited for: 7 -> 7; matrix products, arithmetic and copies ran while one was open for 0% -> 1% of each run, Pallas kernels for 0% -> 0%
where the time goes in v4:
time: 172 us; the launch traced here: 171 us
  Pallas kernels  55.8 us (32%)
  blocking collectives  54.5 us (32%)
  waiting for transfers between devices  34.5 us (20%)
  starting transfers between devices  12.4 us (7%)
  local copies, waits for them, and re-layouts  11.3 us (7%)
    all_to_all x1, blocking collectives, shards(): received = lax.all_to_all(sending, 'tm', 0, 0, tiled=True)  54.5 us
    pallas_call x1, Pallas kernels, attend(): pl.pallas_call(attend_kernel, grid_spec=pltpu.PrefetchScalarGridSpec(num_...  45.7 us
    all_to_all x1, waiting for transfers between devices, shards(): back = lax.all_to_all(mixed, 'tm', 0, 0, tiled=True)  16 us
    ppermute x3, waiting for transfers between devices, swap_cores(): return lax.ppermute(value, 'ha', [(i, i ^ 1) for i in range(8)])  10.3 us
    pallas_call x1, Pallas kernels, project(): pl.pallas_call(project_kernel, grid_spec=pltpu.PrefetchScalarGridSpec(num...  10.1 us
    ppermute x3, waiting for transfers between devices, swap_depth(): return lax.ppermute(value, 'ha', [(i, i ^ 2 * bits) for i in range(8)])  8.24 us
    ppermute x3, starting transfers between devices, swap_depth(): return lax.ppermute(value, 'ha', [(i, i ^ 2 * bits) for i in range(8)])  4.66 us
    ppermute x3, starting transfers between devices, swap_cores(): return lax.ppermute(value, 'ha', [(i, i ^ 1) for i in range(8)])  4.12 us
  transfers between devices with their start and end apart: 7, of which 7 were waited for; matrix products, arithmetic and copies ran while one was open for 1% of the time, Pallas kernels for 0%

profile of v4, /device:TPU:1, one launch (start us, length us, event | category | flops | bytes accessed | tf_op | source)
XLA Modules:
  0.0 170.9 jit_solution(7314572127962414508)
XLA Ops:
  0.0 0.7 pad_add_fusion.1.info
  0.7 0.7 copy-done.1
  1.4 10.1 %project.1 = (bf16[16,992,128]{2,1,0:T(8,128)(2,1)S(1)}, bf16[8,768,128]{2,1,0:T(8,128)(2,1)S(1)}) custom-call(s32[3]{0:T(128)S(1)} %pad_add_fusion.1.info, bf16[2,256,1536]{2,1,0:T(8,128)(2,1)} %bitcast.24, bf16[1536,2304]{1,0:T(8,128)(2,1)} %weights.1, f32[2,768]{1,0:T(2,128)S(1)} %copy-done.1, f32[50,2,1536]{2,1,0:T(2,128)} %modulation.1), custom_call_target="tpu_custom_call" | custom-call | tf_op jit(solution)/shard_map/project/pallas_call | solution.py:78
  11.6 1.9 %copy-done = bf16[16,992,128]{2,1,0:T(8,128)(2,1)} copy-done((bf16[16,992,128]{2,1,0:T(8,128)(2,1)}, bf16[16,992,128]{2,1,0:T(8,128)(2,1)S(1)}, u32[]{:S(2)}) %copy-start) | copy-done | bytes 4063256
  13.5 1.4 collective-permute-start
  14.9 3.0 %collective-permute-done = bf16[8,768,128]{2,1,0:T(8,128)(2,1)S(1)} collective-permute-done((bf16[8,768,128]{2,1,0:T(8,128)(2,1)S(1)}, bf16[8,768,128]{2,1,0:T(8,128)(2,1)S(1)}, u32[]{:S(2)}, u32[]{:S(2)}) %collective-permute-start) | collective-permute-done | bytes 1572896 | tf_op jit(solution)/shard_map/ppermute | solution.py:356
  17.9 1.4 constant_dynamic-update-slice_fusion.1
  19.4 1.7 %slice.52 = bf16[16,512,128]{2,1,0:T(8,128)(2,1)S(1)} slice(bf16[16,992,128]{2,1,0:T(8,128)(2,1)} %constant_dynamic-update-slice_fusion.1), slice={[0:16], [256:768], [0:128]} | slice | bytes 4194304 | tf_op jit(solution)/shard_map/slice | solution.py:404
  21.2 3.8 %collective-permute-start.1 = (bf16[2,8,2,2,16,128]{5,4,3,2,1,0:T(8,128)(2,1)S(1)}, bf16[2,8,2,2,16,128]{5,4,3,2,1,0:T(8,128)(2,1)S(1)}, u32[]{:S(2)}, u32[]{:S(2)}) collective-permute-start(bf16[2,8,2,2,16,128]{5,4,3,2,1,0:T(8,128)(2,1)S(1)} %slice_select_fusion), channel_id=1, source_target_pairs={{0,4},{1,5},{2,6},{3,7},{4,0},{5,1},{6,2},{7,3},{8,12},{9,13},{10,... | collective-permute-start | bytes 786440 | tf_op jit(solution)/shard_map/ppermute | solution.py:360
  25.4 0.8 collective-permute-start.2
  26.3 5.0 %collective-permute-done.1 = bf16[2,8,2,2,16,128]{5,4,3,2,1,0:T(8,128)(2,1)S(1)} collective-permute-done((bf16[2,8,2,2,16,128]{5,4,3,2,1,0:T(8,128)(2,1)S(1)}, bf16[2,8,2,2,16,128]{5,4,3,2,1,0:T(8,128)(2,1)S(1)}, u32[]{:S(2)}, u32[]{:S(2)}) %collective-permute-start.1) | collective-permute-done | bytes 262176 | tf_op jit(solution)/shard_map/ppermute | solution.py:360
  31.8 2.8 %collective-permute-done.2 = bf16[8,2,16,2,128]{4,3,2,1,0:T(2,128)(2,1)S(1)} collective-permute-done((bf16[8,2,16,2,128]{4,3,2,1,0:T(2,128)(2,1)S(1)}, bf16[8,2,16,2,128]{4,3,2,1,0:T(2,128)(2,1)S(1)}, u32[]{:S(2)}, u32[]{:S(2)}) %collective-permute-start.2) | collective-permute-done | bytes 131104 | tf_op jit(solution)/shard_map/ppermute | solution.py:360
  35.5 1.1 constant_dynamic-update-slice_fusion
  36.6 54.5 %all_to_all.10.near = bf16[16,992,128]{2,1,0:T(8,128)(2,1)} all-to-all(bf16[16,992,128]{2,1,0:T(8,128)(2,1)} %constant_dynamic-update-slice_fusion), channel_id=1, replica_groups=mesh['tm'=16,'ha'=8] {'tm'}, dimensions={0} | all-to-all | bytes 8126464 | tf_op jit(solution)/shard_map/all_to_all | solution.py:406
  91.1 2.6 %collective-permute-start.4 = (bf16[16,992,128]{2,1,0:T(8,128)(2,1)}, bf16[16,992,128]{2,1,0:T(8,128)(2,1)}, u32[]{:S(2)}, u32[]{:S(2)}) collective-permute-start(bf16[16,992,128]{2,1,0:T(8,128)(2,1)} %all_to_all.10.near), channel_id=1, source_target_pairs={{0,1},{1,0},{2,3},{3,2},{4,5},{5,4},{6,7},{7,6},{8,9},{9,8},{10,11... | collective-permute-start | bytes 12189704 | tf_op jit(solution)/shard_map/ppermute | solution.py:356
  93.9 6.8 %collective-permute-done.4.far = bf16[16,992,128]{2,1,0:T(8,128)(2,1)} collective-permute-done((bf16[16,992,128]{2,1,0:T(8,128)(2,1)}, bf16[16,992,128]{2,1,0:T(8,128)(2,1)}, u32[]{:S(2)}, u32[]{:S(2)}) %collective-permute-start.4) | collective-permute-done | bytes 4063264 | tf_op jit(solution)/shard_map/ppermute | solution.py:356
  100.6 0.5 broadcast_in_dim.27.bias
  101.2 45.7 %attend.1 = (bf16[16,256,128]{2,1,0:T(8,128)(2,1)}, s32[16]{0:T(128)S(1)}) custom-call(s32[33]{0:T(128)S(1)} %pad_add_fusion.info, bf16[16,992,128]{2,1,0:T(8,128)(2,1)} %all_to_all.10.near, bf16[16,992,128]{2,1,0:T(8,128)(2,1)} %collective-permute-done.4.far, f32[3584,128]{1,0:T(8,128)S(1)} %broadcast_in_dim.27.bias), custom_call_target="tpu_custom_call" | custom-call | tf_op jit(solution)/shard_map/attend/pallas_call | solution.py:311
  146.8 3.7 %all-to-all-start.1 = ((bf16[16,256,128]{2,1,0:T(8,128)(2,1)}), bf16[16,256,128]{2,1,0:T(8,128)(2,1)S(1)}, u32[]{:S(2)}, u32[]{:S(2)}) async-start(bf16[16,256,128]{2,1,0:T(8,128)(2,1)} %get-tuple-element.12), calls=%async_computation.1 | async-start | bytes 2097152 | tf_op jit(solution)/shard_map/all_to_all | solution.py:415
  150.5 16.0 %all-to-all-done.1 = bf16[16,256,128]{2,1,0:T(8,128)(2,1)S(1)} async-done(((bf16[16,256,128]{2,1,0:T(8,128)(2,1)}), bf16[16,256,128]{2,1,0:T(8,128)(2,1)S(1)}, u32[]{:S(2)}, u32[]{:S(2)}) %all-to-all-start.1) | async-done | bytes 1048608 | tf_op jit(solution)/shard_map/all_to_all | solution.py:415
  166.7 0.6 dynamic_slice.10
  167.9 0.5 collective-permute-done.5
  168.5 0.5 copy.7
  169.1 1.8 %reshape.37 = bf16[2,1,16,16,768]{4,3,2,0,1:T(8,128)(2,1)} reshape(bf16[2,256,6,128]{3,2,1,0:T(8,128)(2,1)S(1)} %copy.7) | data formatting | bytes 1572864 | tf_op jit(solution)/shard_map/reshape | solution.py:420
  (22 shorter events, 2.3 us)
Async XLA Ops:
  0.7 0.7 copy-start.1
  11.6 1.9 %copy-start = (bf16[16,992,128]{2,1,0:T(8,128)(2,1)}, bf16[16,992,128]{2,1,0:T(8,128)(2,1)S(1)}, u32[]{:S(2)}) copy-start(bf16[16,992,128]{2,1,0:T(8,128)(2,1)S(1)} %get-tuple-element.9) | copy-start | bytes 12189700
  13.5 4.5 %collective-permute-start = (bf16[8,768,128]{2,1,0:T(8,128)(2,1)S(1)}, bf16[8,768,128]{2,1,0:T(8,128)(2,1)S(1)}, u32[]{:S(2)}, u32[]{:S(2)}) collective-permute-start(bf16[8,768,128]{2,1,0:T(8,128)(2,1)S(1)} %get-tuple-element.10), channel_id=1, source_target_pairs={{0,1},{1,0},{2,3},{3,2},{4,5},{5,4},{6,7},{7,6},{8,9},{9,8},{10,11... | collective-permute-start | bytes 4718600 | tf_op jit(solution)/shard_map/ppermute | solution.py:356
  21.2 10.1 %collective-permute-start.1 = (bf16[2,8,2,2,16,128]{5,4,3,2,1,0:T(8,128)(2,1)S(1)}, bf16[2,8,2,2,16,128]{5,4,3,2,1,0:T(8,128)(2,1)S(1)}, u32[]{:S(2)}, u32[]{:S(2)}) collective-permute-start(bf16[2,8,2,2,16,128]{5,4,3,2,1,0:T(8,128)(2,1)S(1)} %slice_select_fusion), channel_id=1, source_target_pairs={{0,4},{1,5},{2,6},{3,7},{4,0},{5,1},{6,2},{7,3},{8,12},{9,13},{10,... | collective-permute-start | bytes 786440 | tf_op jit(solution)/shard_map/ppermute | solution.py:360
  25.4 9.2 %collective-permute-start.2 = (bf16[8,2,16,2,128]{4,3,2,1,0:T(2,128)(2,1)S(1)}, bf16[8,2,16,2,128]{4,3,2,1,0:T(2,128)(2,1)S(1)}, u32[]{:S(2)}, u32[]{:S(2)}) collective-permute-start(bf16[8,2,16,2,128]{4,3,2,1,0:T(2,128)(2,1)S(1)} %get-tuple-element.14), channel_id=1, source_target_pairs={{0,2},{1,3},{2,0},{3,1},{4,6},{5,7},{6,4},{7,5},{8,10},{9,11},{10,... | collective-permute-start | bytes 393224 | tf_op jit(solution)/shard_map/ppermute | solution.py:360
  26.2 5.6 %collective-permute-start.3 = (bf16[8,2,2,2,128]{4,3,2,1,0:T(2,128)(2,1)S(1)}, bf16[8,2,2,2,128]{4,3,2,1,0:T(2,128)(2,1)S(1)}, u32[]{:S(2)}, u32[]{:S(2)}) collective-permute-start(bf16[8,2,2,2,128]{4,3,2,1,0:T(2,128)(2,1)S(1)} %broadcast_select_fusion.1), channel_id=1, source_target_pairs={{0,6},{1,7},{2,4},{3,5},{4,2},{5,3},{6,0},{7,1},{8,14},{9,15},{10,... | collective-permute-start | bytes 49160 | tf_op jit(solution)/shard_map/ppermute | solution.py:360
  36.6 57.2 %copy-start.2 = (s32[32]{0:T(128)S(1)}, s32[32]{0:T(128)}, u32[]{:S(2)}) copy-start(s32[32]{0:T(128)} %param.11) | copy-start | bytes 388
  91.1 9.6 %collective-permute-start.4 = (bf16[16,992,128]{2,1,0:T(8,128)(2,1)}, bf16[16,992,128]{2,1,0:T(8,128)(2,1)}, u32[]{:S(2)}, u32[]{:S(2)}) collective-permute-start(bf16[16,992,128]{2,1,0:T(8,128)(2,1)} %all_to_all.10.near), channel_id=1, source_target_pairs={{0,1},{1,0},{2,3},{3,2},{4,5},{5,4},{6,7},{7,6},{8,9},{9,8},{10,11... | collective-permute-start | bytes 12189704 | tf_op jit(solution)/shard_map/ppermute | solution.py:356
  146.8 19.7 %all-to-all-start.1 = ((bf16[16,256,128]{2,1,0:T(8,128)(2,1)}), bf16[16,256,128]{2,1,0:T(8,128)(2,1)S(1)}, u32[]{:S(2)}, u32[]{:S(2)}) async-start(bf16[16,256,128]{2,1,0:T(8,128)(2,1)} %get-tuple-element.12), calls=%async_computation.1 | async-start | bytes 2097152 | tf_op jit(solution)/shard_map/all_to_all | solution.py:415
  166.6 1.8 %collective-permute-start.5 = (bf16[6,256,128]{2,1,0:T(8,128)(2,1)S(1)}, bf16[6,256,128]{2,1,0:T(8,128)(2,1)S(1)}, u32[]{:S(2)}, u32[]{:S(2)}) collective-permute-start(bf16[6,256,128]{2,1,0:T(8,128)(2,1)S(1)} %get-tuple-element.17), channel_id=1, source_target_pairs={{0,1},{1,0},{2,3},{3,2},{4,5},{5,4},{6,7},{7,6},{8,9},{9,8},{10,11... | collective-permute-start | bytes 1179656 | tf_op jit(solution)/shard_map/ppermute | solution.py:356

commit v5 on v4

--- a/solution.py
+++ b/solution.py
@@ -88,7 +88,7 @@
             ],
             out_specs=[
                 pl.BlockSpec((SLOTS, TOKENS, HD), lambda p, info: (info[0], p, 0)),
-                pl.BlockSpec((SLOTS, TOKENS, HD), lambda p, info: (0, p, 0)),
+                pl.BlockSpec((HEADS, TOKENS, HD), lambda p, info: (0, p, 0)),
             ],
             scratch_shapes=[
                 pltpu.VMEM((2 * TOKENS, D), jnp.bfloat16),
@@ -99,11 +99,11 @@
         ),
         out_shape=[
             jax.ShapeDtypeStruct((CHIPS, LENGTH, HD), jnp.bfloat16),
-            jax.ShapeDtypeStruct((SLOTS, 3 * TOKENS, HD), jnp.bfloat16),
+            jax.ShapeDtypeStruct((HEADS, 3 * TOKENS, HD), jnp.bfloat16),
         ],
         compiler_params=pltpu.CompilerParams(vmem_limit_bytes=48 * 1024 * 1024),
         name="project",
-    )(info, in_hbm(tokens), projection, norm_gain, in_hbm(modulation))
+    )(info, in_hbm(tokens), projection, in_hbm(norm_gain), in_hbm(modulation))
 
 
 STREAMS = 4
@@ -114,7 +114,9 @@
 ROWS = STREAMS * (EACH + 1)
 
 
-def plan(core, size, slots, bits, chips, pick, block, left):
+def plan(core, slots, bits, chips, seen, items, rim_items):
+    sizes = ((TOKENS, items), (RIM, rim_items))
+
     def visit(turn, carry):
         place = carry[0]
         time = FRAMES - 1 - turn
@@ -123,52 +125,56 @@
         lane = place % (2 * STREAMS)
         stream = jnp.where(lane < STREAMS, lane, 2 * STREAMS - 1 - lane)
         row = place // STREAMS
-        rows = (time + 1) * size
-        count = jnp.where(mine, (rows + WIDE - 1) // WIDE, 0)
-        used = carry[1]
-        for other in range(1, STREAMS):
-            used = jnp.where(stream == other, carry[1 + other], used)
 
         @pl.when(mine)
         def _():
             chips[row * STREAMS + stream] = slot // 2
-
-        def fill(step, inner):
-            pick[stream, used + step] = row
-            block[stream, used + step] = step
-            left[stream, used + step] = rows - step * WIDE
-            return inner
-
-        lax.fori_loop(0, count, fill, 0)
-        grown = tuple(carry[1 + s] + jnp.where(stream == s, count, 0) for s in range(STREAMS))
-        return (place + jnp.where(mine, 1, 0),) + grown
-
-    zero = jnp.int32(0)
-    totals = lax.fori_loop(0, FRAMES, visit, (zero,) + (zero,) * STREAMS)[1:]
-    trip = functools.reduce(jnp.maximum, totals)
+            seen[row * STREAMS + stream] = time + 1
+            for number, (size, target) in enumerate(sizes):
+                count = ((time + 1) * size + WIDE - 1) // WIDE
+                used = chips[CHIPS + number * STREAMS + stream]
+
+                def fill(step, inner):
+                    target[stream, used + step] = row * WIDE + step
+                    return inner
+
+                lax.fori_loop(0, count, fill, 0)
+                chips[CHIPS + number * STREAMS + stream] = used + count
+
+        return (place + jnp.where(mine, 1, 0),)
+
+    for number in range(2 * STREAMS):
+        chips[CHIPS + number] = 0
     for stream in range(STREAMS):
-
-        def clear(step, carry):
-            pick[stream, step] = EACH
-            block[stream, step] = 0
-            left[stream, step] = WIDE
-            return carry
-
-        lax.fori_loop(totals[stream], trip + 2, clear, 0)
-    return trip
+        seen[CHIPS + stream] = FRAMES
+    lax.fori_loop(0, FRAMES, visit, (jnp.int32(0),))
+    trips = []
+    for number, (size, target) in enumerate(sizes):
+        totals = [chips[CHIPS + number * STREAMS + stream] for stream in range(STREAMS)]
+        trip = functools.reduce(jnp.maximum, totals)
+        for stream in range(STREAMS):
+
+            def clear(step, carry):
+                target[stream, step] = EACH * WIDE
+                return carry
+
+            lax.fori_loop(totals[stream], trip + 2, clear, 0)
+        trips.append(trip)
+    return trips
 
 
 def fold(values, combine):
     return combine(values.reshape(values.shape[0] // 8, 8, values.shape[1]), axis=0)
 
 
-def sweep(trip, scored, queries, keys, values, tops, totals, mixes, pick, block, left, raws, peaks):
+def sweep(trip, scored, queries, keys, values, tops, totals, mixes, items, seen, size, raws, peaks):
     def spots_of(step):
         spots = []
         for stream in range(STREAMS):
-            row = pick[stream, step] * STREAMS + stream
-            first = pl.multiple_of(block[stream, step] * WIDE, WIDE)
-            spots.append((row, first, left[stream, step]))
+            item = items[stream, step]
+            row = item // WIDE * STREAMS + stream
+            first = pl.multiple_of(item % WIDE * WIDE, WIDE)
+            spots.append((row, first, seen[row] * size - first))
         return spots
 
     def ask(spot, part):
@@ -250,7 +256,8 @@
 
 def attend_kernel(info, near, far, bias, out, bits, *scratch):
     tops, totals, mixes, asked, queries, keys, staged, values, rim_keys, rim_staged, rim_values, slots, chips = scratch[:13]
-    lists, rim_lists, sem, raws = scratch[13:16], scratch[16:19], scratch[19], scratch[20:]
+    seen, items, rim_items, sem = scratch[13:17]
+    raws = scratch[17:]
     raws, peaks = raws[: 2 * STREAMS], raws[2 * STREAMS :]
     raws, peaks = [(r[:STREAMS], r[STREAMS:]) for r in (raws, peaks)]
     core = info[FRAMES]
@@ -277,8 +284,7 @@
         (rim_at + RIM, RIM, rim_staged),
     )
     gather_frames(slots, core, near, far, moves, sem)
-    trip = plan(core, TOKENS, slots, bits, chips, *lists)
-    rim_trip = plan(core, RIM, slots, bits, chips, *rim_lists)
+    trip, rim_trip = plan(core, slots, bits, chips, seen, items, rim_items)
     tops[...] = jnp.full(tops.shape, LOWEST, jnp.float32)
     totals[...] = jnp.zeros(totals.shape, jnp.float32)
     mixes[...] = jnp.zeros(mixes.shape, jnp.float32)
@@ -293,21 +299,20 @@
     def scored(raw, rows, remain):
         return raw + jnp.where(remain <= 0, LOWEST, 0.0)
 
-    sweep(trip, scored, queries, keys, values, tops, totals, mixes, *lists, raws, peaks)
+    sweep(trip, scored, queries, keys, values, tops, totals, mixes, items, seen, TOKENS, raws, peaks)
 
     def rim_scored(raw, rows, remain):
         place = lax.broadcasted_iota(jnp.int32, (PIECE, HD), 0)
         added = jnp.where(place < remain, bias[rows], LOWEST)
         return jnp.concatenate([raw[:, :HD] + added, raw[:, HD:] + added], axis=1)
 
-    sweep(rim_trip, rim_scored, queries, rim_keys, rim_values, tops, totals, mixes, *rim_lists, raws, peaks)
+    sweep(rim_trip, rim_scored, queries, rim_keys, rim_values, tops, totals, mixes, rim_items, seen, RIM, raws, peaks)
     for place in range(CHIPS):
         whole = jnp.sum(totals[place], axis=0, keepdims=True)
         out[chips[place]] = (mixes[place] / whole).T.astype(jnp.bfloat16)
 
 
 def attend(info, near, far, bias):
-    lists = [pltpu.SMEM((STREAMS, LIMIT + 2), jnp.int32)] * 3
     return pl.pallas_call(
         attend_kernel,
         grid_spec=pltpu.PrefetchScalarGridSpec(
@@ -335,10 +340,11 @@
                 pltpu.VMEM((FRAMES * RIM, HD), jnp.bfloat16),
                 pltpu.VMEM((HD, FRAMES * RIM), jnp.bfloat16),
                 pltpu.SMEM((FRAMES,), jnp.int32),
-                pltpu.SMEM((CHIPS,), jnp.int32),
+                pltpu.SMEM((CHIPS + 2 * STREAMS,), jnp.int32),
+                pltpu.SMEM((ROWS,), jnp.int32),
+                pltpu.SMEM((STREAMS, LIMIT + 2), jnp.int32),
+                pltpu.SMEM((STREAMS, LIMIT + 2), jnp.int32),
             ]
-            + lists
-            + lists
             + [pltpu.SemaphoreType.DMA((5,))]
             + [pltpu.VMEM((WIDE, TOKENS), jnp.float32)] * (2 * STREAMS)
             + [pltpu.VMEM((8, TOKENS), jnp.float32)] * (2 * STREAMS),
@@ -360,29 +366,39 @@
     return lax.ppermute(value, "ha", [(i, i ^ (2 * bits)) for i in range(8)])
 
 
-def rim_rows(pair, depth):
+def rim_rows(sending, depth):
+    lines = sending.reshape(2, SLOTS, LENGTH // TILE, TILE, HD)
     even = depth % 2 == 0
     upper = depth < 2
 
-    def edge(strip):
-        return jnp.where(upper, strip[..., TILE - PAD :, :, :], strip[..., :PAD, :, :])
-
-    sent = jnp.where(even, pair[1, :, :, :, TILE - PAD :], pair[0, :, :, :, :PAD])
+    def strip(tile, first):
+        piece = lines[tile, :HEADS, TILE : 3 * TILE, first : first + PAD]
+        return piece.reshape(HEADS, 2, TILE, PAD, HD)
+
+    def bottom_or_top(value, axis):
+        low = lax.slice_in_dim(value, TILE - PAD, TILE, axis=axis)
+        return jnp.where(upper, low, lax.slice_in_dim(value, 0, PAD, axis=axis))
+
+    def edge(first):
+        low = lines[:, :HEADS, first + TILE - PAD : first + TILE]
+        return jnp.where(upper, low, lines[:, :HEADS, first : first + PAD])
+
+    sent = jnp.where(even, strip(1, TILE - PAD), strip(0, 0))
     outer = swap_depth(sent, 1)
-    above = swap_depth(edge(pair), 2)
-    corner = swap_depth(edge(sent), 3)
-    inner = (pair[1, :, :, :, :PAD], pair[0, :, :, :, TILE - PAD :])
+    above = swap_depth(jnp.stack([edge(TILE), edge(2 * TILE)], axis=2), 2)
+    corner = swap_depth(bottom_or_top(sent, 2), 3)
+    inner = (strip(1, 0), strip(0, TILE - PAD))
     inner_corner = (above[1, :, :, :, :PAD], above[0, :, :, :, TILE - PAD :])
-    spare = jnp.zeros((SLOTS, 2, RIM - 104, HD), jnp.bfloat16)
+    spare = jnp.zeros((HEADS, 2, RIM - 104, HD), jnp.bfloat16)
 
     def flat(piece):
-        return piece.reshape(SLOTS, 2, -1, HD)
+        return piece.reshape(HEADS, 2, -1, HD)
 
     both = []
     for tile in range(2):
         rows = [inner[tile], above[tile], inner_corner[tile], outer, corner]
         both.append(jnp.concatenate([flat(r) for r in rows] + [spare], axis=2))
-    return jnp.concatenate(both, axis=0).reshape(CHIPS, 2 * RIM, HD)
+    return jnp.stack(both).reshape(2, HEADS, 2 * RIM, HD)
 
 
 def rim_bias(outer_valid):
@@ -401,8 +417,9 @@
     other = swap_cores(away)
     first = (1 - core) * SLOTS
     sending = lax.dynamic_update_slice(sending, other, (first, 0, 0))
-    pair = sending[:, TOKENS : 3 * TOKENS].reshape(2, SLOTS, 2, TILE, TILE, HD)
-    sending = lax.dynamic_update_slice(sending, rim_rows(pair, depth), (0, 3 * TOKENS, 0))
+    halves = sending.reshape(2, SLOTS, LENGTH, HD)
+    halves = lax.dynamic_update_slice(halves, rim_rows(sending, depth), (0, 0, 3 * TOKENS, 0))
+    sending = halves.reshape(CHIPS, LENGTH, HD)
     received = lax.all_to_all(sending, "tm", 0, 0, tiled=True)
     far = swap_cores(received)
 

time: 172 us -> 166 us (0.965); the launches traced: 171 us -> 167 us
  waiting for transfers between devices: 34.5 us -> 30 us
  local copies, waits for them, and re-layouts: 11.3 us -> 7.49 us
  other arithmetic: 1.48 us -> 4.69 us
  starting transfers between devices: 12.4 us -> 15.2 us
  Pallas kernels: 55.8 us -> 54 us
    ppermute x3, waiting for transfers between devices: 8.24 us -> 4.79 us  [swap_depth(): return lax.ppermute(value, 'ha', [(i, i ^ 2 * bits) for i in range(8)])]
    ppermute x3, starting transfers between devices: 4.12 us -> 6.91 us  [swap_cores(): return lax.ppermute(value, 'ha', [(i, i ^ 1) for i in range(8)])]
    pallas_call x1, Pallas kernels: 45.7 us -> 43.9 us  [attend(): pl.pallas_call(attend_kernel, grid_spec=pltpu.PrefetchScalarGridSpec(num_...]
    slice x1 -> x0, local copies, waits for them, and re-layouts: 1.75 us -> none  [shards(): pair = sending[:, TOKENS:3 * TOKENS].reshape(2, SLOTS, 2, TILE, TILE, HD)]
  transfers between devices with their start and end apart: 7 -> 7, of which waited for: 7 -> 7; matrix products, arithmetic and copies ran while one was open for 1% -> 2% of each run, Pallas kernels for 0% -> 0%
where the time goes in v5:
time: 166 us; the launch traced here: 167 us
  blocking collectives  54.5 us (33%)
  Pallas kernels  54 us (33%)
  waiting for transfers between devices  30 us (18%)
  starting transfers between devices  15.2 us (9%)
  local copies, waits for them, and re-layouts  7.49 us (5%)
  other arithmetic  4.69 us (3%)
    all_to_all x1, blocking collectives, shards(): received = lax.all_to_all(sending, 'tm', 0, 0, tiled=True)  54.5 us
    pallas_call x1, Pallas kernels, attend(): pl.pallas_call(attend_kernel, grid_spec=pltpu.PrefetchScalarGridSpec(num_...  43.9 us
    all_to_all x1, waiting for transfers between devices, shards(): back = lax.all_to_all(mixed, 'tm', 0, 0, tiled=True)  15.9 us
    pallas_call x1, Pallas kernels, project(): pl.pallas_call(project_kernel, grid_spec=pltpu.PrefetchScalarGridSpec(num...  10.1 us
    ppermute x3, waiting for transfers between devices, swap_cores(): return lax.ppermute(value, 'ha', [(i, i ^ 1) for i in range(8)])  9.34 us
    ppermute x3, starting transfers between devices, swap_cores(): return lax.ppermute(value, 'ha', [(i, i ^ 1) for i in range(8)])  6.91 us
    ppermute x3, waiting for transfers between devices, swap_depth(): return lax.ppermute(value, 'ha', [(i, i ^ 2 * bits) for i in range(8)])  4.79 us
    ppermute x3, starting transfers between devices, swap_depth(): return lax.ppermute(value, 'ha', [(i, i ^ 2 * bits) for i in range(8)])  4.66 us
  transfers between devices with their start and end apart: 7, of which 7 were waited for; matrix products, arithmetic and copies ran while one was open for 2% of the time, Pallas kernels for 0%

profile of v5, /device:TPU:1, one launch (start us, length us, event | category | flops | bytes accessed | tf_op | source)
XLA Modules:
  0.0 166.7 jit_solution(4948567093736481578)
XLA Ops:
  0.0 0.7 pad_add_fusion.1.info
  0.7 10.1 %project.1 = (bf16[16,992,128]{2,1,0:T(8,128)(2,1)S(1)}, bf16[6,768,128]{2,1,0:T(8,128)(2,1)S(1)}) custom-call(s32[3]{0:T(128)S(1)} %pad_add_fusion.1.info, bf16[2,256,1536]{2,1,0:T(8,128)(2,1)} %bitcast.31, bf16[1536,2304]{1,0:T(8,128)(2,1)} %weights.1, f32[2,768]{1,0:T(2,128)} %gains.1, f32[50,2,1536]{2,1,0:T(2,128)} %modulation.1), custom_call_target="tpu_custom_call" | custom-call | tf_op jit(solution)/shard_map/project/pallas_call | solution.py:78
  10.9 1.9 %copy-done = bf16[16,992,128]{2,1,0:T(8,128)(2,1)} copy-done((bf16[16,992,128]{2,1,0:T(8,128)(2,1)}, bf16[16,992,128]{2,1,0:T(8,128)(2,1)S(1)}, u32[]{:S(2)}) %copy-start) | copy-done | bytes 4063256
  12.8 1.4 collective-permute-start
  14.2 2.5 %collective-permute-done = bf16[6,768,128]{2,1,0:T(8,128)(2,1)S(1)} collective-permute-done((bf16[6,768,128]{2,1,0:T(8,128)(2,1)S(1)}, bf16[6,768,128]{2,1,0:T(8,128)(2,1)S(1)}, u32[]{:S(2)}, u32[]{:S(2)}) %collective-permute-start) | collective-permute-done | bytes 1179680 | tf_op jit(solution)/shard_map/ppermute | solution.py:362
  16.7 1.2 constant_dynamic-update-slice_fusion
  17.9 1.1 fusion.2
  19.0 3.8 %collective-permute-start.1 = (bf16[2,6,2,2,16,128]{5,4,3,1,0,2:T(8,128)(2,1)S(1)}, bf16[2,6,2,2,16,128]{5,4,3,1,0,2:T(8,128)(2,1)S(1)}, u32[]{:S(2)}, u32[]{:S(2)}) collective-permute-start(bf16[2,6,2,2,16,128]{5,4,3,1,0,2:T(8,128)(2,1)S(1)} %pad_maximum_fusion), channel_id=1, source_target_pairs={{0,4},{1,5},{2,6},{3,7},{4,0},{5,1},{6,2},{7,3},{8,12},{9,13},{10,... | collective-permute-start | bytes 589832 | tf_op jit(solution)/shard_map/ppermute | solution.py:366
  22.8 1.7 fusion.3
  24.5 0.8 collective-permute-start.2
  25.4 2.4 %collective-permute-done.1 = bf16[2,6,2,2,16,128]{5,4,3,1,0,2:T(8,128)(2,1)S(1)} collective-permute-done((bf16[2,6,2,2,16,128]{5,4,3,1,0,2:T(8,128)(2,1)S(1)}, bf16[2,6,2,2,16,128]{5,4,3,1,0,2:T(8,128)(2,1)S(1)}, u32[]{:S(2)}, u32[]{:S(2)}) %collective-permute-start.1) | collective-permute-done | bytes 196640 | tf_op jit(solution)/shard_map/ppermute | solution.py:366
  27.9 1.2 collective-permute-done.3
  29.1 1.2 collective-permute-done.2
  31.0 1.0 maximum_dynamic-update-slice_fusion
  31.9 54.5 %all_to_all.10.near = bf16[16,992,128]{2,1,0:T(8,128)(2,1)} all-to-all(bf16[16,992,128]{2,1,0:T(8,128)(2,1)} %bitcast.30), channel_id=1, replica_groups=mesh['tm'=16,'ha'=8] {'tm'}, dimensions={0} | all-to-all | bytes 8126464 | tf_op jit(solution)/shard_map/all_to_all | solution.py:423
  86.4 2.6 %collective-permute-start.4 = (bf16[16,992,128]{2,1,0:T(8,128)(2,1)}, bf16[16,992,128]{2,1,0:T(8,128)(2,1)}, u32[]{:S(2)}, u32[]{:S(2)}) collective-permute-start(bf16[16,992,128]{2,1,0:T(8,128)(2,1)} %all_to_all.10.near), channel_id=1, source_target_pairs={{0,1},{1,0},{2,3},{3,2},{4,5},{5,4},{6,7},{7,6},{8,9},{9,8},{10,11... | collective-permute-start | bytes 12189704 | tf_op jit(solution)/shard_map/ppermute | solution.py:362
  89.2 6.8 %collective-permute-done.4.far = bf16[16,992,128]{2,1,0:T(8,128)(2,1)} collective-permute-done((bf16[16,992,128]{2,1,0:T(8,128)(2,1)}, bf16[16,992,128]{2,1,0:T(8,128)(2,1)}, u32[]{:S(2)}, u32[]{:S(2)}) %collective-permute-start.4) | collective-permute-done | bytes 4063264 | tf_op jit(solution)/shard_map/ppermute | solution.py:362
  96.5 43.9 %attend.1 = (bf16[16,256,128]{2,1,0:T(8,128)(2,1)}, s32[16]{0:T(128)S(1)}) custom-call(s32[33]{0:T(128)S(1)} %pad_add_fusion.info, bf16[16,992,128]{2,1,0:T(8,128)(2,1)} %all_to_all.10.near, bf16[16,992,128]{2,1,0:T(8,128)(2,1)} %collective-permute-done.4.far, f32[3584,128]{1,0:T(8,128)S(1)} %broadcast_in_dim.27.bias), custom_call_target="tpu_custom_call" | custom-call | tf_op jit(solution)/shard_map/attend/pallas_call | solution.py:316
  140.4 3.7 %all-to-all-start.1 = ((bf16[16,256,128]{2,1,0:T(8,128)(2,1)}), bf16[16,256,128]{2,1,0:T(8,128)(2,1)S(1)}, u32[]{:S(2)}, u32[]{:S(2)}) async-start(bf16[16,256,128]{2,1,0:T(8,128)(2,1)} %get-tuple-element.12), calls=%async_computation.1 | async-start | bytes 2097152 | tf_op jit(solution)/shard_map/all_to_all | solution.py:432
  144.1 15.9 %all-to-all-done.1 = bf16[16,256,128]{2,1,0:T(8,128)(2,1)S(1)} async-done(((bf16[16,256,128]{2,1,0:T(8,128)(2,1)}), bf16[16,256,128]{2,1,0:T(8,128)(2,1)S(1)}, u32[]{:S(2)}, u32[]{:S(2)}) %all-to-all-start.1) | async-done | bytes 1048608 | tf_op jit(solution)/shard_map/all_to_all | solution.py:432
  160.0 2.9 %collective-permute-start.5 = (bf16[6,256,128]{2,1,0:T(8,128)(2,1)S(1)}, bf16[6,256,128]{2,1,0:T(8,128)(2,1)S(1)}, u32[]{:S(2)}, u32[]{:S(2)}) collective-permute-start(bf16[6,256,128]{2,1,0:T(8,128)(2,1)S(1)} %get-tuple-element.19), channel_id=1, source_target_pairs={{0,1},{1,0},{2,3},{3,2},{4,5},{5,4},{6,7},{7,6},{8,9},{9,8},{10,11... | collective-permute-start | bytes 1179656 | tf_op jit(solution)/shard_map/ppermute | solution.py:362
  162.9 0.6 dynamic_slice.10
  164.4 0.5 copy.15
  164.9 1.8 %reshape.46 = bf16[2,1,16,16,768]{4,3,2,0,1:T(8,128)(2,1)} reshape(bf16[2,256,6,128]{3,2,1,0:T(8,128)(2,1)S(1)} %copy.15) | data formatting | bytes 1572864 | tf_op jit(solution)/shard_map/reshape | solution.py:437
  (23 shorter events, 1.8 us)
Async XLA Ops:
  10.9 1.9 %copy-start = (bf16[16,992,128]{2,1,0:T(8,128)(2,1)}, bf16[16,992,128]{2,1,0:T(8,128)(2,1)S(1)}, u32[]{:S(2)}) copy-start(bf16[16,992,128]{2,1,0:T(8,128)(2,1)S(1)} %get-tuple-element.9) | copy-start | bytes 12189700
  12.8 3.9 %collective-permute-start = (bf16[6,768,128]{2,1,0:T(8,128)(2,1)S(1)}, bf16[6,768,128]{2,1,0:T(8,128)(2,1)S(1)}, u32[]{:S(2)}, u32[]{:S(2)}) collective-permute-start(bf16[6,768,128]{2,1,0:T(8,128)(2,1)S(1)} %get-tuple-element.10), channel_id=1, source_target_pairs={{0,1},{1,0},{2,3},{3,2},{4,5},{5,4},{6,7},{7,6},{8,9},{9,8},{10,11... | collective-permute-start | bytes 3538952 | tf_op jit(solution)/shard_map/ppermute | solution.py:362
  19.0 8.7 %collective-permute-start.1 = (bf16[2,6,2,2,16,128]{5,4,3,1,0,2:T(8,128)(2,1)S(1)}, bf16[2,6,2,2,16,128]{5,4,3,1,0,2:T(8,128)(2,1)S(1)}, u32[]{:S(2)}, u32[]{:S(2)}) collective-permute-start(bf16[2,6,2,2,16,128]{5,4,3,1,0,2:T(8,128)(2,1)S(1)} %pad_maximum_fusion), channel_id=1, source_target_pairs={{0,4},{1,5},{2,6},{3,7},{4,0},{5,1},{6,2},{7,3},{8,12},{9,13},{10,... | collective-permute-start | bytes 589832 | tf_op jit(solution)/shard_map/ppermute | solution.py:366
  24.5 5.8 %collective-permute-start.2 = (bf16[6,2,16,2,128]{4,3,2,1,0:T(2,128)(2,1)S(1)}, bf16[6,2,16,2,128]{4,3,2,1,0:T(2,128)(2,1)S(1)}, u32[]{:S(2)}, u32[]{:S(2)}) collective-permute-start(bf16[6,2,16,2,128]{4,3,2,1,0:T(2,128)(2,1)S(1)} %bitcast.41), channel_id=1, source_target_pairs={{0,2},{1,3},{2,0},{3,1},{4,6},{5,7},{6,4},{7,5},{8,10},{9,11},{10,... | collective-permute-start | bytes 294920 | tf_op jit(solution)/shard_map/ppermute | solution.py:366
  25.3 3.8 %collective-permute-start.3 = (bf16[6,2,2,2,128]{4,3,2,1,0:T(2,128)(2,1)S(1)}, bf16[6,2,2,2,128]{4,3,2,1,0:T(2,128)(2,1)S(1)}, u32[]{:S(2)}, u32[]{:S(2)}) collective-permute-start(bf16[6,2,2,2,128]{4,3,2,1,0:T(2,128)(2,1)S(1)} %broadcast_select_fusion.1), channel_id=1, source_target_pairs={{0,6},{1,7},{2,4},{3,5},{4,2},{5,3},{6,0},{7,1},{8,14},{9,15},{10,... | collective-permute-start | bytes 36872 | tf_op jit(solution)/shard_map/ppermute | solution.py:366
  31.9 57.2 %copy-start.1 = (s32[32]{0:T(128)S(1)}, s32[32]{0:T(128)}, u32[]{:S(2)}) copy-start(s32[32]{0:T(128)} %param.11) | copy-start | bytes 388
  86.4 9.6 %collective-permute-start.4 = (bf16[16,992,128]{2,1,0:T(8,128)(2,1)}, bf16[16,992,128]{2,1,0:T(8,128)(2,1)}, u32[]{:S(2)}, u32[]{:S(2)}) collective-permute-start(bf16[16,992,128]{2,1,0:T(8,128)(2,1)} %all_to_all.10.near), channel_id=1, source_target_pairs={{0,1},{1,0},{2,3},{3,2},{4,5},{5,4},{6,7},{7,6},{8,9},{9,8},{10,11... | collective-permute-start | bytes 12189704 | tf_op jit(solution)/shard_map/ppermute | solution.py:362
  140.4 19.6 %all-to-all-start.1 = ((bf16[16,256,128]{2,1,0:T(8,128)(2,1)}), bf16[16,256,128]{2,1,0:T(8,128)(2,1)S(1)}, u32[]{:S(2)}, u32[]{:S(2)}) async-start(bf16[16,256,128]{2,1,0:T(8,128)(2,1)} %get-tuple-element.12), calls=%async_computation.1 | async-start | bytes 2097152 | tf_op jit(solution)/shard_map/all_to_all | solution.py:432
  160.0 4.2 %collective-permute-start.5 = (bf16[6,256,128]{2,1,0:T(8,128)(2,1)S(1)}, bf16[6,256,128]{2,1,0:T(8,128)(2,1)S(1)}, u32[]{:S(2)}, u32[]{:S(2)}) collective-permute-start(bf16[6,256,128]{2,1,0:T(8,128)(2,1)S(1)} %get-tuple-element.19), channel_id=1, source_target_pairs={{0,1},{1,0},{2,3},{3,2},{4,5},{5,4},{6,7},{7,6},{8,9},{9,8},{10,11... | collective-permute-start | bytes 1179656 | tf_op jit(solution)/shard_map/ppermute | solution.py:362

commit v6 on v5

--- a/solution.py
+++ b/solution.py
@@ -101,7 +101,7 @@
             jax.ShapeDtypeStruct((CHIPS, LENGTH, HD), jnp.bfloat16),
             jax.ShapeDtypeStruct((HEADS, 3 * TOKENS, HD), jnp.bfloat16),
         ],
-        compiler_params=pltpu.CompilerParams(vmem_limit_bytes=48 * 1024 * 1024),
+        compiler_params=pltpu.CompilerParams(vmem_limit_bytes=60 * 1024 * 1024),
         name="project",
     )(info, in_hbm(tokens), projection, in_hbm(norm_gain), in_hbm(modulation))
 
@@ -408,6 +408,33 @@
     return jnp.broadcast_to(column_of[:, None], (FRAMES * RIM, HD))
 
 
+def finish_kernel(info, back, come, out):
+    core = info[0]
+    frame = jnp.where(core == info[1], 0, 1)
+    for head in range(HEADS):
+        columns = slice(head * HD, (head + 1) * HD)
+        out[frame, :, columns] = back[core * SLOTS + head]
+        out[1 - frame, :, columns] = come[head]
+
+
+def finish(info, back, come):
+    return pl.pallas_call(
+        finish_kernel,
+        grid_spec=pltpu.PrefetchScalarGridSpec(
+            num_scalar_prefetch=1,
+            grid=(1,),
+            in_specs=[
+                pl.BlockSpec((CHIPS, TOKENS, HD), lambda i, info: (0, 0, 0)),
+                pl.BlockSpec((HEADS, TOKENS, HD), lambda i, info: (0, 0, 0)),
+            ],
+            out_specs=pl.BlockSpec((2, TOKENS, QD), lambda i, info: (0, 0, 0)),
+        ),
+        out_shape=jax.ShapeDtypeStruct((2, TOKENS, QD), jnp.bfloat16),
+        compiler_params=pltpu.CompilerParams(vmem_limit_bytes=16 * 1024 * 1024),
+        name="finish",
+    )(info, back, come)
+
+
 def shards(tokens, projection, norm_gain, modulation, levels, frame_order):
     chip = lax.axis_index("tm")
     place = lax.axis_index("ha")
@@ -430,11 +457,9 @@
     turned = lax.dynamic_index_in_dim(bits, chip, 0, keepdims=False)
 
     back = lax.all_to_all(mixed, "tm", 0, 0, tiled=True)
-    stay = lax.dynamic_slice_in_dim(back, core * SLOTS, HEADS, 0)
     leave = lax.dynamic_slice_in_dim(back, (1 - core) * SLOTS, HEADS, 0)
     come = swap_cores(leave)
-    both = jnp.where(core == turned, jnp.stack([stay, come]), jnp.stack([come, stay]))
-    return both.transpose(0, 2, 1, 3).reshape(2, 1, TILE, TILE, QD)
+    return finish(jnp.stack([core, turned]), back, come).reshape(2, 1, TILE, TILE, QD)
 
 
 def solution(mesh):

time: 166 us -> 165 us (level)
  blocking collectives: 54.5 us -> 75 us
  waiting for transfers between devices: 30 us -> 14.3 us
  starting transfers between devices: 15.2 us -> 9.21 us
  local copies, waits for them, and re-layouts: 7.49 us -> 3.21 us
  Pallas kernels: 54 us -> 57.6 us
    all_to_all x0 -> x1, blocking collectives: none -> 20.5 us  [shards(): back = lax.all_to_all(mixed, 'tm', 0, 0, tiled=True)]
    all_to_all x1 -> x0, waiting for transfers between devices: 15.9 us -> none  [shards(): back = lax.all_to_all(mixed, 'tm', 0, 0, tiled=True)]
    all_to_all x1 -> x0, starting transfers between devices: 3.66 us -> none  [shards(): back = lax.all_to_all(mixed, 'tm', 0, 0, tiled=True)]
    ppermute x3, starting transfers between devices: 6.91 us -> 4.55 us  [swap_cores(): return lax.ppermute(value, 'ha', [(i, i ^ 1) for i in range(8)])]
    unnamed x4 -> x2, local copies, waits for them, and re-layouts: 1.92 us -> 0.01 us
    reshape x1 -> x0, local copies, waits for them, and re-layouts: 1.78 us -> none  [shards(): return both.transpose(0, 2, 1, 3).reshape(2, 1, TILE, TILE, QD)]
  transfers between devices with their start and end apart: 7 -> 6, of which waited for: 7 -> 5; matrix products, arithmetic and copies ran while one was open for 2% -> 2% of each run, Pallas kernels for 0% -> 0%
where the time goes in v6:
time: 165 us
  blocking collectives  75 us (45%)
  Pallas kernels  57.6 us (35%)
  waiting for transfers between devices  14.3 us (9%)
  starting transfers between devices  9.21 us (6%)
  other arithmetic  5.81 us (4%)
  local copies, waits for them, and re-layouts  3.21 us (2%)
    all_to_all x1, blocking collectives, shards(): received = lax.all_to_all(sending, 'tm', 0, 0, tiled=True)  54.5 us
    pallas_call x1, Pallas kernels, attend(): pl.pallas_call(attend_kernel, grid_spec=pltpu.PrefetchScalarGridSpec(num_...  45 us
    all_to_all x1, blocking collectives, shards(): back = lax.all_to_all(mixed, 'tm', 0, 0, tiled=True)  20.5 us
    pallas_call x1, Pallas kernels, project(): pl.pallas_call(project_kernel, grid_spec=pltpu.PrefetchScalarGridSpec(num...  11.1 us
    ppermute x3, waiting for transfers between devices, swap_cores(): return lax.ppermute(value, 'ha', [(i, i ^ 1) for i in range(8)])  9.48 us
    ppermute x3, waiting for transfers between devices, swap_depth(): return lax.ppermute(value, 'ha', [(i, i ^ 2 * bits) for i in range(8)])  4.79 us
    ppermute x3, starting transfers between devices, swap_depth(): return lax.ppermute(value, 'ha', [(i, i ^ 2 * bits) for i in range(8)])  4.66 us
    ppermute x3, starting transfers between devices, swap_cores(): return lax.ppermute(value, 'ha', [(i, i ^ 1) for i in range(8)])  4.55 us
  transfers between devices with their start and end apart: 6, of which 5 were waited for; matrix products, arithmetic and copies ran while one was open for 2% of the time, Pallas kernels for 0%

profile of v6, /device:TPU:1, one launch (start us, length us, event | category | flops | bytes accessed | tf_op | source)
XLA Modules:
  0.0 165.3 jit_solution(13403241577209598101)
XLA Ops:
  0.0 1.3 pad_add_fusion.1.info
  1.3 11.1 %project.1 = (bf16[16,992,128]{2,1,0:T(8,128)(2,1)}, bf16[6,768,128]{2,1,0:T(8,128)(2,1)}) custom-call(s32[3]{0:T(128)} %pad_add_fusion.1.info, bf16[2,256,1536]{2,1,0:T(8,128)(2,1)} %bitcast.27, bf16[1536,2304]{1,0:T(8,128)(2,1)} %weights.1, f32[2,768]{1,0:T(2,128)} %gains.1, f32[50,2,1536]{2,1,0:T(2,128)} %modulation.1), custom_call_target="tpu_custom_call" | custom-call | tf_op jit(solution)/shard_map/project/pallas_call | solution.py:78
  12.3 1.5 collective-permute-start
  13.8 2.7 %collective-permute-done = bf16[6,768,128]{2,1,0:T(8,128)(2,1)S(1)} collective-permute-done((bf16[6,768,128]{2,1,0:T(8,128)(2,1)}, bf16[6,768,128]{2,1,0:T(8,128)(2,1)S(1)}, u32[]{:S(2)}, u32[]{:S(2)}) %collective-permute-start) | collective-permute-done | bytes 1179680 | tf_op jit(solution)/shard_map/ppermute | solution.py:362
  16.5 1.2 constant_dynamic-update-slice_fusion
  17.7 1.1 fusion.1
  18.8 3.8 %collective-permute-start.1 = (bf16[2,6,2,2,16,128]{5,4,3,1,0,2:T(8,128)(2,1)S(1)}, bf16[2,6,2,2,16,128]{5,4,3,1,0,2:T(8,128)(2,1)S(1)}, u32[]{:S(2)}, u32[]{:S(2)}) collective-permute-start(bf16[2,6,2,2,16,128]{5,4,3,1,0,2:T(8,128)(2,1)S(1)} %pad_maximum_fusion), channel_id=1, source_target_pairs={{0,4},{1,5},{2,6},{3,7},{4,0},{5,1},{6,2},{7,3},{8,12},{9,13},{10,... | collective-permute-start | bytes 589832 | tf_op jit(solution)/shard_map/ppermute | solution.py:366
  22.6 1.7 %fusion.2 = (bf16[1,6,32,2,128]{4,3,2,1,0:T(2,128)(2,1)S(1)}, bf16[1,6,32,2,128]{4,3,2,1,0:T(2,128)(2,1)S(1)}, bf16[1,6,32,2,128]{4,3,2,1,0:T(2,128)(2,1)S(1)}) fusion(bf16[2,8,62,16,128]{4,3,2,1,0:T(8,128)(2,1)} %bitcast.24, pred[]{:T(512)S(6)} %eq.7), kind=kLoop, calls=%fused_computation.14 | loop fusion | flops 49152 | bytes 688129 | tf_op jit(solution)/shard_map/slice | solution.py:375
  24.2 0.8 collective-permute-start.2
  25.2 2.4 %collective-permute-done.1 = bf16[2,6,2,2,16,128]{5,4,3,1,0,2:T(8,128)(2,1)S(1)} collective-permute-done((bf16[2,6,2,2,16,128]{5,4,3,1,0,2:T(8,128)(2,1)S(1)}, bf16[2,6,2,2,16,128]{5,4,3,1,0,2:T(8,128)(2,1)S(1)}, u32[]{:S(2)}, u32[]{:S(2)}) %collective-permute-start.1) | collective-permute-done | bytes 196640 | tf_op jit(solution)/shard_map/ppermute | solution.py:366
  27.7 1.2 collective-permute-done.3
  28.9 1.2 collective-permute-done.2
  30.4 0.3 concatenate.16
  30.7 1.0 maximum_dynamic-update-slice_fusion
  31.7 54.5 %all_to_all.10.near = bf16[16,992,128]{2,1,0:T(8,128)(2,1)} all-to-all(bf16[16,992,128]{2,1,0:T(8,128)(2,1)} %bitcast.26), channel_id=1, replica_groups=mesh['tm'=16,'ha'=8] {'tm'}, dimensions={0} | all-to-all | bytes 8126464 | tf_op jit(solution)/shard_map/all_to_all | solution.py:450
  86.2 2.6 %collective-permute-start.4 = (bf16[16,992,128]{2,1,0:T(8,128)(2,1)}, bf16[16,992,128]{2,1,0:T(8,128)(2,1)}, u32[]{:S(2)}, u32[]{:S(2)}) collective-permute-start(bf16[16,992,128]{2,1,0:T(8,128)(2,1)} %all_to_all.10.near), channel_id=1, source_target_pairs={{0,1},{1,0},{2,3},{3,2},{4,5},{5,4},{6,7},{7,6},{8,9},{9,8},{10,11... | collective-permute-start | bytes 12189704 | tf_op jit(solution)/shard_map/ppermute | solution.py:362
  89.0 6.8 %collective-permute-done.4.far = bf16[16,992,128]{2,1,0:T(8,128)(2,1)} collective-permute-done((bf16[16,992,128]{2,1,0:T(8,128)(2,1)}, bf16[16,992,128]{2,1,0:T(8,128)(2,1)}, u32[]{:S(2)}, u32[]{:S(2)}) %collective-permute-start.4) | collective-permute-done | bytes 4063264 | tf_op jit(solution)/shard_map/ppermute | solution.py:362
  95.8 0.5 broadcast_in_dim.24.bias
  96.3 45.0 %attend.1 = (bf16[16,256,128]{2,1,0:T(8,128)(2,1)S(1)}, s32[16]{0:T(128)S(1)}) custom-call(s32[33]{0:T(128)S(1)} %pad_add_fusion.info, bf16[16,992,128]{2,1,0:T(8,128)(2,1)} %all_to_all.10.near, bf16[16,992,128]{2,1,0:T(8,128)(2,1)} %collective-permute-done.4.far, f32[3584,128]{1,0:T(8,128)S(1)} %broadcast_in_dim.24.bias), custom_call_target="tpu_custom_call" | custom-call | tf_op jit(solution)/shard_map/attend/pallas_call | solution.py:316
  141.3 20.5 %all_to_all.11.back = bf16[16,256,128]{2,1,0:T(8,128)(2,1)S(1)} all-to-all(bf16[16,256,128]{2,1,0:T(8,128)(2,1)S(1)} %get-tuple-element.12), channel_id=1, replica_groups=mesh['tm'=16,'ha'=8] {'tm'}, dimensions={0} | all-to-all | bytes 2097152 | tf_op jit(solution)/shard_map/all_to_all | solution.py:459
  161.9 0.5 collective-permute-start.5
  162.3 0.6 dynamic_slice.7
  163.0 0.7 pad_add_fusion.2.info
  163.7 1.6 finish.1
  (19 shorter events, 0.8 us)
Async XLA Ops:
  12.3 4.2 %collective-permute-start = (bf16[6,768,128]{2,1,0:T(8,128)(2,1)}, bf16[6,768,128]{2,1,0:T(8,128)(2,1)S(1)}, u32[]{:S(2)}, u32[]{:S(2)}) collective-permute-start(bf16[6,768,128]{2,1,0:T(8,128)(2,1)} %get-tuple-element.10), channel_id=1, source_target_pairs={{0,1},{1,0},{2,3},{3,2},{4,5},{5,4},{6,7},{7,6},{8,9},{9,8},{10,11... | collective-permute-start | bytes 3538952 | tf_op jit(solution)/shard_map/ppermute | solution.py:362
  18.8 8.7 %collective-permute-start.1 = (bf16[2,6,2,2,16,128]{5,4,3,1,0,2:T(8,128)(2,1)S(1)}, bf16[2,6,2,2,16,128]{5,4,3,1,0,2:T(8,128)(2,1)S(1)}, u32[]{:S(2)}, u32[]{:S(2)}) collective-permute-start(bf16[2,6,2,2,16,128]{5,4,3,1,0,2:T(8,128)(2,1)S(1)} %pad_maximum_fusion), channel_id=1, source_target_pairs={{0,4},{1,5},{2,6},{3,7},{4,0},{5,1},{6,2},{7,3},{8,12},{9,13},{10,... | collective-permute-start | bytes 589832 | tf_op jit(solution)/shard_map/ppermute | solution.py:366
  24.2 5.8 %collective-permute-start.2 = (bf16[6,2,16,2,128]{4,3,2,1,0:T(2,128)(2,1)S(1)}, bf16[6,2,16,2,128]{4,3,2,1,0:T(2,128)(2,1)S(1)}, u32[]{:S(2)}, u32[]{:S(2)}) collective-permute-start(bf16[6,2,16,2,128]{4,3,2,1,0:T(2,128)(2,1)S(1)} %bitcast.36), channel_id=1, source_target_pairs={{0,2},{1,3},{2,0},{3,1},{4,6},{5,7},{6,4},{7,5},{8,10},{9,11},{10,... | collective-permute-start | bytes 294920 | tf_op jit(solution)/shard_map/ppermute | solution.py:366
  25.1 3.8 %collective-permute-start.3 = (bf16[6,2,2,2,128]{4,3,2,1,0:T(2,128)(2,1)S(1)}, bf16[6,2,2,2,128]{4,3,2,1,0:T(2,128)(2,1)S(1)}, u32[]{:S(2)}, u32[]{:S(2)}) collective-permute-start(bf16[6,2,2,2,128]{4,3,2,1,0:T(2,128)(2,1)S(1)} %broadcast_select_fusion.1), channel_id=1, source_target_pairs={{0,6},{1,7},{2,4},{3,5},{4,2},{5,3},{6,0},{7,1},{8,14},{9,15},{10,... | collective-permute-start | bytes 36872 | tf_op jit(solution)/shard_map/ppermute | solution.py:366
  31.7 57.2 %copy-start = (s32[32]{0:T(128)S(1)}, s32[32]{0:T(128)}, u32[]{:S(2)}) copy-start(s32[32]{0:T(128)} %param.11) | copy-start | bytes 388
  86.2 9.6 %collective-permute-start.4 = (bf16[16,992,128]{2,1,0:T(8,128)(2,1)}, bf16[16,992,128]{2,1,0:T(8,128)(2,1)}, u32[]{:S(2)}, u32[]{:S(2)}) collective-permute-start(bf16[16,992,128]{2,1,0:T(8,128)(2,1)} %all_to_all.10.near), channel_id=1, source_target_pairs={{0,1},{1,0},{2,3},{3,2},{4,5},{5,4},{6,7},{7,6},{8,9},{9,8},{10,11... | collective-permute-start | bytes 12189704 | tf_op jit(solution)/shard_map/ppermute | solution.py:362
  161.9 1.8 %collective-permute-start.5 = (bf16[6,256,128]{2,1,0:T(8,128)(2,1)S(1)}, bf16[6,256,128]{2,1,0:T(8,128)(2,1)S(1)}, u32[]{:S(2)}, u32[]{:S(2)}) collective-permute-start(bf16[6,256,128]{2,1,0:T(8,128)(2,1)S(1)} %constant_dynamic-slice_fusion), channel_id=1, source_target_pairs={{0,1},{1,0},{2,3},{3,2},{4,5},{5,4},{6,7},{7,6},{8,9},{9,8},{10,11... | collective-permute-start | bytes 1179656 | tf_op jit(solution)/shard_map/ppermute | solution.py:362

commit v7 on v6

--- a/solution.py
+++ b/solution.py
@@ -30,43 +30,49 @@
     part = pl.program_id(0)
     core = info[0]
 
+    def put(target, result):
+        result = result.astype(jnp.bfloat16)
+        for head in range(HEADS):
+            target[head] = result[:, head * HD : (head + 1) * HD]
+
+    def scaled(raw, row):
+        return raw * lax.rsqrt(jnp.mean(raw * raw, axis=-1, keepdims=True) + 1e-06) * row
+
+    def product(values):
+        return jnp.dot(values, weights[...], preferred_element_type=jnp.float32)
+
     @pl.when(part == 0)
     def _():
-        copies = [pltpu.make_async_copy(tokens_hbm, tokens, sem.at[0])]
-        for frame in range(2):
-            copies.append(pltpu.make_async_copy(modulation.at[info[1 + frame]], rows.at[frame], sem.at[1 + frame]))
+        frames = (1 - core, core)
+        copies = []
+        for turn, frame in enumerate(frames):
+            copies.append(pltpu.make_async_copy(modulation.at[info[1 + frame]], rows.at[turn], sem.at[2 + turn]))
+            copies.append(pltpu.make_async_copy(tokens_hbm.at[frame], tokens.at[turn], sem.at[turn]))
         for copy in copies:
             copy.start()
         for copy in copies:
             copy.wait()
-        for turn in range(2):
-            frame = 1 - core if turn == 0 else core
-            values = tokens[frame].astype(jnp.float32)
+        for turn, target in enumerate((away, own)):
+            values = tokens[turn].astype(jnp.float32)
             average = jnp.mean(values, axis=-1, keepdims=True)
             centred = values - average
             spread = jnp.mean(centred * centred, axis=-1, keepdims=True)
             normed = centred * lax.rsqrt(spread + 1e-06)
-            shift = rows[frame, 0:1, :]
-            scale = rows[frame, 1:2, :]
-            inputs[pl.ds(turn * TOKENS, TOKENS)] = (normed * (1.0 + scale) + shift).astype(jnp.bfloat16)
-
-    raw = jnp.dot(inputs[...], weights[...], preferred_element_type=jnp.float32)
-
-    def put(result):
-        result = result.astype(jnp.bfloat16)
-        for head in range(HEADS):
-            columns = slice(head * HD, (head + 1) * HD)
-            away[head] = result[:TOKENS, columns]
-            own[head] = result[TOKENS:, columns]
-
-    @pl.when(part < 2)
+            modulated = (normed * (1.0 + rows[turn, 1:2, :]) + rows[turn, 0:1, :]).astype(jnp.bfloat16)
+            inputs[turn * TOKENS : (turn + 1) * TOKENS] = modulated
+            put(target, scaled(product(modulated), gains[0:1, :]))
+
+    @pl.when(part == 1)
     def _():
-        row = jnp.where(part == 0, gains[0:1, :], gains[1:2, :])
-        put(raw * lax.rsqrt(jnp.mean(raw * raw, axis=-1, keepdims=True) + 1e-06) * row)
+        raw = scaled(product(inputs[...]), gains[1:2, :])
+        put(away, raw[:TOKENS])
+        put(own, raw[TOKENS:])
 
     @pl.when(part == 2)
     def _():
-        put(raw)
+        raw = product(inputs[...])
+        put(away, raw[:TOKENS])
+        put(own, raw[TOKENS:])
 
 
 def in_hbm(value):
@@ -94,7 +100,7 @@
                 pltpu.VMEM((2 * TOKENS, D), jnp.bfloat16),
                 pltpu.VMEM((2, TOKENS, D), jnp.bfloat16),
                 pltpu.VMEM((2, 2, D), jnp.float32),
-                pltpu.SemaphoreType.DMA((3,)),
+                pltpu.SemaphoreType.DMA((4,)),
             ],
         ),
         out_shape=[
@@ -409,8 +415,8 @@
 
 
 def finish_kernel(info, back, come, out):
-    core = info[0]
-    frame = jnp.where(core == info[1], 0, 1)
+    core = lax.axis_index("ha") % 2
+    frame = jnp.where(core == info[lax.axis_index("tm")], 0, 1)
     for head in range(HEADS):
         columns = slice(head * HD, (head + 1) * HD)
         out[frame, :, columns] = back[core * SLOTS + head]
@@ -454,12 +460,11 @@
     odd_tile = chip // SLOTS
     bias = rim_bias(depth % 2 != odd_tile)
     mixed, bits = attend(info, received, far, bias)
-    turned = lax.dynamic_index_in_dim(bits, chip, 0, keepdims=False)
 
     back = lax.all_to_all(mixed, "tm", 0, 0, tiled=True)
     leave = lax.dynamic_slice_in_dim(back, (1 - core) * SLOTS, HEADS, 0)
     come = swap_cores(leave)
-    return finish(jnp.stack([core, turned]), back, come).reshape(2, 1, TILE, TILE, QD)
+    return finish(bits, back, come).reshape(2, 1, TILE, TILE, QD)
 
 
 def solution(mesh):

time: 165 us -> 164 us (level)
  Pallas kernels: 57.6 us -> 55.7 us
  starting transfers between devices: 9.21 us -> 10.9 us
    ppermute x3, starting transfers between devices: 4.55 us -> 6.25 us  [swap_cores(): return lax.ppermute(value, 'ha', [(i, i ^ 1) for i in range(8)])]
  transfers between devices with their start and end apart: 6 -> 6, of which waited for: 5 -> 6; matrix products, arithmetic and copies ran while one was open for 2% -> 1% of each run, Pallas kernels for 0% -> 0%
where the time goes in v7:
time: 164 us
  blocking collectives  73.7 us (45%)
  Pallas kernels  55.7 us (34%)
  waiting for transfers between devices  15.6 us (10%)
  starting transfers between devices  10.9 us (7%)
  other arithmetic  5.1 us (3%)
  local copies, waits for them, and re-layouts  2.61 us (2%)
    all_to_all x1, blocking collectives, shards(): received = lax.all_to_all(sending, 'tm', 0, 0, tiled=True)  54.5 us
    pallas_call x1, Pallas kernels, attend(): pl.pallas_call(attend_kernel, grid_spec=pltpu.PrefetchScalarGridSpec(num_...  43.8 us
    all_to_all x1, blocking collectives, shards(): back = lax.all_to_all(mixed, 'tm', 0, 0, tiled=True)  19.2 us
    ppermute x3, waiting for transfers between devices, swap_cores(): return lax.ppermute(value, 'ha', [(i, i ^ 1) for i in range(8)])  10.8 us
    pallas_call x1, Pallas kernels, project(): pl.pallas_call(project_kernel, grid_spec=pltpu.PrefetchScalarGridSpec(num...  10.4 us
    ppermute x3, starting transfers between devices, swap_cores(): return lax.ppermute(value, 'ha', [(i, i ^ 1) for i in range(8)])  6.25 us
    ppermute x3, waiting for transfers between devices, swap_depth(): return lax.ppermute(value, 'ha', [(i, i ^ 2 * bits) for i in range(8)])  4.79 us
    ppermute x3, starting transfers between devices, swap_depth(): return lax.ppermute(value, 'ha', [(i, i ^ 2 * bits) for i in range(8)])  4.65 us
  transfers between devices with their start and end apart: 6, of which 6 were waited for; matrix products, arithmetic and copies ran while one was open for 1% of the time, Pallas kernels for 0%

profile of v7, /device:TPU:1, one launch (start us, length us, event | category | flops | bytes accessed | tf_op | source)
XLA Modules:
  0.0 163.7 jit_solution(11830550310103950887)
XLA Ops:
  0.0 1.3 pad_add_fusion.1.info
  1.3 10.4 %project.1 = (bf16[16,992,128]{2,1,0:T(8,128)(2,1)}, bf16[6,768,128]{2,1,0:T(8,128)(2,1)}) custom-call(s32[3]{0:T(128)} %pad_add_fusion.1.info, bf16[2,256,1536]{2,1,0:T(8,128)(2,1)} %bitcast.27, bf16[1536,2304]{1,0:T(8,128)(2,1)} %weights.1, f32[2,768]{1,0:T(2,128)} %gains.1, f32[50,2,1536]{2,1,0:T(2,128)} %modulation.1), custom_call_target="tpu_custom_call" | custom-call | tf_op jit(solution)/shard_map/project/pallas_call | solution.py:84
  11.6 1.5 collective-permute-start
  13.1 2.7 %collective-permute-done = bf16[6,768,128]{2,1,0:T(8,128)(2,1)S(1)} collective-permute-done((bf16[6,768,128]{2,1,0:T(8,128)(2,1)}, bf16[6,768,128]{2,1,0:T(8,128)(2,1)S(1)}, u32[]{:S(2)}, u32[]{:S(2)}) %collective-permute-start) | collective-permute-done | bytes 1179680 | tf_op jit(solution)/shard_map/ppermute | solution.py:368
  15.8 1.2 constant_dynamic-update-slice_fusion
  17.0 1.1 fusion.1
  18.1 3.8 %collective-permute-start.1 = (bf16[2,6,2,2,16,128]{5,4,3,1,0,2:T(8,128)(2,1)S(1)}, bf16[2,6,2,2,16,128]{5,4,3,1,0,2:T(8,128)(2,1)S(1)}, u32[]{:S(2)}, u32[]{:S(2)}) collective-permute-start(bf16[2,6,2,2,16,128]{5,4,3,1,0,2:T(8,128)(2,1)S(1)} %pad_maximum_fusion), channel_id=1, source_target_pairs={{0,4},{1,5},{2,6},{3,7},{4,0},{5,1},{6,2},{7,3},{8,12},{9,13},{10,... | collective-permute-start | bytes 589832 | tf_op jit(solution)/shard_map/ppermute | solution.py:372
  21.9 1.7 %fusion.2 = (bf16[1,6,32,2,128]{4,3,2,1,0:T(2,128)(2,1)S(1)}, bf16[1,6,32,2,128]{4,3,2,1,0:T(2,128)(2,1)S(1)}, bf16[1,6,32,2,128]{4,3,2,1,0:T(2,128)(2,1)S(1)}) fusion(bf16[2,8,62,16,128]{4,3,2,1,0:T(8,128)(2,1)} %bitcast.24, pred[]{:T(512)S(6)} %eq.7), kind=kLoop, calls=%fused_computation.13 | loop fusion | flops 49152 | bytes 688129 | tf_op jit(solution)/shard_map/slice | solution.py:381
  23.5 0.8 collective-permute-start.2
  24.5 2.4 %collective-permute-done.1 = bf16[2,6,2,2,16,128]{5,4,3,1,0,2:T(8,128)(2,1)S(1)} collective-permute-done((bf16[2,6,2,2,16,128]{5,4,3,1,0,2:T(8,128)(2,1)S(1)}, bf16[2,6,2,2,16,128]{5,4,3,1,0,2:T(8,128)(2,1)S(1)}, u32[]{:S(2)}, u32[]{:S(2)}) %collective-permute-start.1) | collective-permute-done | bytes 196640 | tf_op jit(solution)/shard_map/ppermute | solution.py:372
  27.0 1.2 collective-permute-done.3
  28.2 1.2 collective-permute-done.2
  29.4 0.3 concatenate.15
  29.7 0.3 concatenate.16
  30.0 1.0 maximum_dynamic-update-slice_fusion
  31.0 54.5 %all_to_all.10.near = bf16[16,992,128]{2,1,0:T(8,128)(2,1)} all-to-all(bf16[16,992,128]{2,1,0:T(8,128)(2,1)} %bitcast.26), channel_id=1, replica_groups=mesh['tm'=16,'ha'=8] {'tm'}, dimensions={0} | all-to-all | bytes 8126464 | tf_op jit(solution)/shard_map/all_to_all | solution.py:456
  85.5 2.6 %collective-permute-start.4 = (bf16[16,992,128]{2,1,0:T(8,128)(2,1)}, bf16[16,992,128]{2,1,0:T(8,128)(2,1)}, u32[]{:S(2)}, u32[]{:S(2)}) collective-permute-start(bf16[16,992,128]{2,1,0:T(8,128)(2,1)} %all_to_all.10.near), channel_id=1, source_target_pairs={{0,1},{1,0},{2,3},{3,2},{4,5},{5,4},{6,7},{7,6},{8,9},{9,8},{10,11... | collective-permute-start | bytes 12189704 | tf_op jit(solution)/shard_map/ppermute | solution.py:368
  88.3 6.8 %collective-permute-done.4.far = bf16[16,992,128]{2,1,0:T(8,128)(2,1)} collective-permute-done((bf16[16,992,128]{2,1,0:T(8,128)(2,1)}, bf16[16,992,128]{2,1,0:T(8,128)(2,1)}, u32[]{:S(2)}, u32[]{:S(2)}) %collective-permute-start.4) | collective-permute-done | bytes 4063264 | tf_op jit(solution)/shard_map/ppermute | solution.py:368
  95.1 0.5 broadcast_in_dim.27.bias
  95.6 43.8 %attend.1 = (bf16[16,256,128]{2,1,0:T(8,128)(2,1)S(1)}, s32[16]{0:T(128)S(1)}) custom-call(s32[33]{0:T(128)S(1)} %pad_add_fusion.info, bf16[16,992,128]{2,1,0:T(8,128)(2,1)} %all_to_all.10.near, bf16[16,992,128]{2,1,0:T(8,128)(2,1)} %collective-permute-done.4.far, f32[3584,128]{1,0:T(8,128)S(1)} %broadcast_in_dim.27.bias), custom_call_target="tpu_custom_call" | custom-call | tf_op jit(solution)/shard_map/attend/pallas_call | solution.py:322
  139.4 19.2 %all_to_all.11.back = bf16[16,256,128]{2,1,0:T(8,128)(2,1)S(1)} all-to-all(bf16[16,256,128]{2,1,0:T(8,128)(2,1)S(1)} %get-tuple-element.12), channel_id=1, replica_groups=mesh['tm'=16,'ha'=8] {'tm'}, dimensions={0} | all-to-all | bytes 2097152 | tf_op jit(solution)/shard_map/all_to_all | solution.py:464
  158.6 2.2 %collective-permute-start.5 = (bf16[6,256,128]{2,1,0:T(8,128)(2,1)S(1)}, bf16[6,256,128]{2,1,0:T(8,128)(2,1)S(1)}, u32[]{:S(2)}, u32[]{:S(2)}) collective-permute-start(bf16[6,256,128]{2,1,0:T(8,128)(2,1)S(1)} %constant_dynamic-slice_fusion), channel_id=1, source_target_pairs={{0,1},{1,0},{2,3},{3,2},{4,5},{5,4},{6,7},{7,6},{8,9},{9,8},{10,11... | collective-permute-start | bytes 1179656 | tf_op jit(solution)/shard_map/ppermute | solution.py:368
  160.8 1.3 collective-permute-done.5.come
  162.2 1.6 finish.1
  (17 shorter events, 0.4 us)
Async XLA Ops:
  11.6 4.2 %collective-permute-start = (bf16[6,768,128]{2,1,0:T(8,128)(2,1)}, bf16[6,768,128]{2,1,0:T(8,128)(2,1)S(1)}, u32[]{:S(2)}, u32[]{:S(2)}) collective-permute-start(bf16[6,768,128]{2,1,0:T(8,128)(2,1)} %get-tuple-element.10), channel_id=1, source_target_pairs={{0,1},{1,0},{2,3},{3,2},{4,5},{5,4},{6,7},{7,6},{8,9},{9,8},{10,11... | collective-permute-start | bytes 3538952 | tf_op jit(solution)/shard_map/ppermute | solution.py:368
  18.1 8.7 %collective-permute-start.1 = (bf16[2,6,2,2,16,128]{5,4,3,1,0,2:T(8,128)(2,1)S(1)}, bf16[2,6,2,2,16,128]{5,4,3,1,0,2:T(8,128)(2,1)S(1)}, u32[]{:S(2)}, u32[]{:S(2)}) collective-permute-start(bf16[2,6,2,2,16,128]{5,4,3,1,0,2:T(8,128)(2,1)S(1)} %pad_maximum_fusion), channel_id=1, source_target_pairs={{0,4},{1,5},{2,6},{3,7},{4,0},{5,1},{6,2},{7,3},{8,12},{9,13},{10,... | collective-permute-start | bytes 589832 | tf_op jit(solution)/shard_map/ppermute | solution.py:372
  23.5 5.8 %collective-permute-start.2 = (bf16[6,2,16,2,128]{4,3,2,1,0:T(2,128)(2,1)S(1)}, bf16[6,2,16,2,128]{4,3,2,1,0:T(2,128)(2,1)S(1)}, u32[]{:S(2)}, u32[]{:S(2)}) collective-permute-start(bf16[6,2,16,2,128]{4,3,2,1,0:T(2,128)(2,1)S(1)} %bitcast.36), channel_id=1, source_target_pairs={{0,2},{1,3},{2,0},{3,1},{4,6},{5,7},{6,4},{7,5},{8,10},{9,11},{10,... | collective-permute-start | bytes 294920 | tf_op jit(solution)/shard_map/ppermute | solution.py:372
  24.4 3.8 %collective-permute-start.3 = (bf16[6,2,2,2,128]{4,3,2,1,0:T(2,128)(2,1)S(1)}, bf16[6,2,2,2,128]{4,3,2,1,0:T(2,128)(2,1)S(1)}, u32[]{:S(2)}, u32[]{:S(2)}) collective-permute-start(bf16[6,2,2,2,128]{4,3,2,1,0:T(2,128)(2,1)S(1)} %broadcast_select_fusion.1), channel_id=1, source_target_pairs={{0,6},{1,7},{2,4},{3,5},{4,2},{5,3},{6,0},{7,1},{8,14},{9,15},{10,... | collective-permute-start | bytes 36872 | tf_op jit(solution)/shard_map/ppermute | solution.py:372
  31.0 57.2 %copy-start = (s32[32]{0:T(128)S(1)}, s32[32]{0:T(128)}, u32[]{:S(2)}) copy-start(s32[32]{0:T(128)} %param.11) | copy-start | bytes 388
  85.5 9.6 %collective-permute-start.4 = (bf16[16,992,128]{2,1,0:T(8,128)(2,1)}, bf16[16,992,128]{2,1,0:T(8,128)(2,1)}, u32[]{:S(2)}, u32[]{:S(2)}) collective-permute-start(bf16[16,992,128]{2,1,0:T(8,128)(2,1)} %all_to_all.10.near), channel_id=1, source_target_pairs={{0,1},{1,0},{2,3},{3,2},{4,5},{5,4},{6,7},{7,6},{8,9},{9,8},{10,11... | collective-permute-start | bytes 12189704 | tf_op jit(solution)/shard_map/ppermute | solution.py:368
  158.6 3.5 %collective-permute-start.5 = (bf16[6,256,128]{2,1,0:T(8,128)(2,1)S(1)}, bf16[6,256,128]{2,1,0:T(8,128)(2,1)S(1)}, u32[]{:S(2)}, u32[]{:S(2)}) collective-permute-start(bf16[6,256,128]{2,1,0:T(8,128)(2,1)S(1)} %constant_dynamic-slice_fusion), channel_id=1, source_target_pairs={{0,1},{1,0},{2,3},{3,2},{4,5},{5,4},{6,7},{7,6},{8,9},{9,8},{10,11... | collective-permute-start | bytes 1179656 | tf_op jit(solution)/shard_map/ppermute | solution.py:368

commit v8 on v7

--- a/solution.py
+++ b/solution.py
@@ -28,7 +28,7 @@
 
 def project_kernel(info, tokens_hbm, weights, gains, modulation, own, away, inputs, tokens, rows, sem):
     part = pl.program_id(0)
-    core = info[0]
+    core = lax.axis_index("ha") % 2
 
     def put(target, result):
         result = result.astype(jnp.bfloat16)
@@ -46,7 +46,7 @@
         frames = (1 - core, core)
         copies = []
         for turn, frame in enumerate(frames):
-            copies.append(pltpu.make_async_copy(modulation.at[info[1 + frame]], rows.at[turn], sem.at[2 + turn]))
+            copies.append(pltpu.make_async_copy(modulation.at[info[frame]], rows.at[turn], sem.at[2 + turn]))
             copies.append(pltpu.make_async_copy(tokens_hbm.at[frame], tokens.at[turn], sem.at[turn]))
         for copy in copies:
             copy.start()
@@ -80,7 +80,6 @@
 
 
 def project(tokens, projection, norm_gain, modulation, levels, core):
-    info = jnp.concatenate([core[None], levels])
     return pl.pallas_call(
         project_kernel,
         grid_spec=pltpu.PrefetchScalarGridSpec(
@@ -93,7 +92,7 @@
                 pl.BlockSpec(memory_space=pltpu.HBM),
             ],
             out_specs=[
-                pl.BlockSpec((SLOTS, TOKENS, HD), lambda p, info: (info[0], p, 0)),
+                pl.BlockSpec((SLOTS, TOKENS, HD), lambda p, levels: (lax.axis_index("ha") % 2, p, 0)),
                 pl.BlockSpec((HEADS, TOKENS, HD), lambda p, info: (0, p, 0)),
             ],
             scratch_shapes=[
@@ -109,7 +108,7 @@
         ],
         compiler_params=pltpu.CompilerParams(vmem_limit_bytes=60 * 1024 * 1024),
         name="project",
-    )(info, in_hbm(tokens), projection, in_hbm(norm_gain), in_hbm(modulation))
+    )(levels, in_hbm(tokens), projection, in_hbm(norm_gain), in_hbm(modulation))
 
 
 STREAMS = 4
@@ -266,7 +265,7 @@
     raws = scratch[17:]
     raws, peaks = raws[: 2 * STREAMS], raws[2 * STREAMS :]
     raws, peaks = [(r[:STREAMS], r[STREAMS:]) for r in (raws, peaks)]
-    core = info[FRAMES]
+    core = lax.axis_index("ha") % 2
     for slot in range(FRAMES):
         slots[info[slot]] = slot
     ahead = jnp.int32(0)
@@ -456,10 +455,9 @@
     received = lax.all_to_all(sending, "tm", 0, 0, tiled=True)
     far = swap_cores(received)
 
-    info = jnp.concatenate([frame_order, core[None]])
     odd_tile = chip // SLOTS
     bias = rim_bias(depth % 2 != odd_tile)
-    mixed, bits = attend(info, received, far, bias)
+    mixed, bits = attend(frame_order, received, far, bias)
 
     back = lax.all_to_all(mixed, "tm", 0, 0, tiled=True)
     leave = lax.dynamic_slice_in_dim(back, (1 - core) * SLOTS, HEADS, 0)

time: 164 us -> 162 us (0.988)
  no operation moved by 1% of the time
where the time goes in v8:
time: 162 us; the launch traced here: 161 us
  blocking collectives  72.6 us (45%)
  Pallas kernels  54.4 us (34%)
  waiting for transfers between devices  15.7 us (10%)
  starting transfers between devices  11.9 us (7%)
  other arithmetic  3.76 us (2%)
  local copies, waits for them, and re-layouts  2.61 us (2%)
    all_to_all x1, blocking collectives, shards(): received = lax.all_to_all(sending, 'tm', 0, 0, tiled=True)  54.5 us
    pallas_call x1, Pallas kernels, attend(): pl.pallas_call(attend_kernel, grid_spec=pltpu.PrefetchScalarGridSpec(num_...  42.5 us
    all_to_all x1, blocking collectives, shards(): back = lax.all_to_all(mixed, 'tm', 0, 0, tiled=True)  18.1 us
    ppermute x3, waiting for transfers between devices, swap_cores(): return lax.ppermute(value, 'ha', [(i, i ^ 1) for i in range(8)])  10.9 us
    pallas_call x1, Pallas kernels, project(): pl.pallas_call(project_kernel, grid_spec=pltpu.PrefetchScalarGridSpec(num...  10.4 us
    ppermute x3, starting transfers between devices, swap_cores(): return lax.ppermute(value, 'ha', [(i, i ^ 1) for i in range(8)])  7.3 us
    ppermute x3, waiting for transfers between devices, swap_depth(): return lax.ppermute(value, 'ha', [(i, i ^ 2 * bits) for i in range(8)])  4.79 us
    ppermute x3, starting transfers between devices, swap_depth(): return lax.ppermute(value, 'ha', [(i, i ^ 2 * bits) for i in range(8)])  4.65 us
  transfers between devices with their start and end apart: 6, of which 6 were waited for; matrix products, arithmetic and copies ran while one was open for 1% of the time, Pallas kernels for 0%

profile of v8, /device:TPU:1, one launch (start us, length us, event | category | flops | bytes accessed | tf_op | source)
XLA Modules:
  0.0 161.2 jit_solution(13993997922678194858)
XLA Ops:
  0.0 10.4 %project.1 = (bf16[16,992,128]{2,1,0:T(8,128)(2,1)}, bf16[6,768,128]{2,1,0:T(8,128)(2,1)}) custom-call(s32[2]{0:T(128)} %info.2, bf16[2,256,1536]{2,1,0:T(8,128)(2,1)} %bitcast.26, bf16[1536,2304]{1,0:T(8,128)(2,1)} %weights.1, f32[2,768]{1,0:T(2,128)} %gains.1, f32[50,2,1536]{2,1,0:T(2,128)} %modulation.1), custom_call_target="tpu_custom_call" | custom-call | tf_op jit(solution)/shard_map/project/pallas_call | solution.py:83
  10.4 1.5 collective-permute-start
  11.9 2.7 %collective-permute-done = bf16[6,768,128]{2,1,0:T(8,128)(2,1)S(1)} collective-permute-done((bf16[6,768,128]{2,1,0:T(8,128)(2,1)}, bf16[6,768,128]{2,1,0:T(8,128)(2,1)S(1)}, u32[]{:S(2)}, u32[]{:S(2)}) %collective-permute-start) | collective-permute-done | bytes 1179680 | tf_op jit(solution)/shard_map/ppermute | solution.py:367
  14.6 1.2 constant_dynamic-update-slice_fusion
  15.8 1.1 fusion.1
  16.9 3.7 %collective-permute-start.1 = (bf16[2,6,2,2,16,128]{5,4,3,1,0,2:T(8,128)(2,1)S(1)}, bf16[2,6,2,2,16,128]{5,4,3,1,0,2:T(8,128)(2,1)S(1)}, u32[]{:S(2)}, u32[]{:S(2)}) collective-permute-start(bf16[2,6,2,2,16,128]{5,4,3,1,0,2:T(8,128)(2,1)S(1)} %pad_maximum_fusion), channel_id=1, source_target_pairs={{0,4},{1,5},{2,6},{3,7},{4,0},{5,1},{6,2},{7,3},{8,12},{9,13},{10,... | collective-permute-start | bytes 589832 | tf_op jit(solution)/shard_map/ppermute | solution.py:371
  20.6 1.7 %fusion.2 = (bf16[1,6,32,2,128]{4,3,2,1,0:T(2,128)(2,1)S(1)}, bf16[1,6,32,2,128]{4,3,2,1,0:T(2,128)(2,1)S(1)}, bf16[1,6,32,2,128]{4,3,2,1,0:T(2,128)(2,1)S(1)}) fusion(bf16[2,8,62,16,128]{4,3,2,1,0:T(8,128)(2,1)} %bitcast.23, pred[]{:T(512)S(6)} %eq.7), kind=kLoop, calls=%fused_computation.11 | loop fusion | flops 49152 | bytes 688129 | tf_op jit(solution)/shard_map/slice | solution.py:380
  22.3 0.8 collective-permute-start.2
  23.1 0.1 collective-permute-start.3
  23.2 2.4 %collective-permute-done.1 = bf16[2,6,2,2,16,128]{5,4,3,1,0,2:T(8,128)(2,1)S(1)} collective-permute-done((bf16[2,6,2,2,16,128]{5,4,3,1,0,2:T(8,128)(2,1)S(1)}, bf16[2,6,2,2,16,128]{5,4,3,1,0,2:T(8,128)(2,1)S(1)}, u32[]{:S(2)}, u32[]{:S(2)}) %collective-permute-start.1) | collective-permute-done | bytes 196640 | tf_op jit(solution)/shard_map/ppermute | solution.py:371
  25.7 1.2 collective-permute-done.3
  27.0 1.2 collective-permute-done.2
  28.1 0.3 concatenate.7
  28.5 0.3 concatenate.8
  28.8 1.0 maximum_dynamic-update-slice_fusion
  29.8 54.5 %all_to_all.10.near = bf16[16,992,128]{2,1,0:T(8,128)(2,1)} all-to-all(bf16[16,992,128]{2,1,0:T(8,128)(2,1)} %bitcast.25), channel_id=1, replica_groups=mesh['tm'=16,'ha'=8] {'tm'}, dimensions={0} | all-to-all | bytes 8126464 | tf_op jit(solution)/shard_map/all_to_all | solution.py:455
  84.3 2.6 %collective-permute-start.4 = (bf16[16,992,128]{2,1,0:T(8,128)(2,1)}, bf16[16,992,128]{2,1,0:T(8,128)(2,1)}, u32[]{:S(2)}, u32[]{:S(2)}) collective-permute-start(bf16[16,992,128]{2,1,0:T(8,128)(2,1)} %all_to_all.10.near), channel_id=1, source_target_pairs={{0,1},{1,0},{2,3},{3,2},{4,5},{5,4},{6,7},{7,6},{8,9},{9,8},{10,11... | collective-permute-start | bytes 12189704 | tf_op jit(solution)/shard_map/ppermute | solution.py:367
  87.0 6.8 %collective-permute-done.4.far = bf16[16,992,128]{2,1,0:T(8,128)(2,1)} collective-permute-done((bf16[16,992,128]{2,1,0:T(8,128)(2,1)}, bf16[16,992,128]{2,1,0:T(8,128)(2,1)}, u32[]{:S(2)}, u32[]{:S(2)}) %collective-permute-start.4) | collective-permute-done | bytes 4063264 | tf_op jit(solution)/shard_map/ppermute | solution.py:367
  93.8 0.5 broadcast_in_dim.22.bias
  94.4 42.5 %attend.1 = (bf16[16,256,128]{2,1,0:T(8,128)(2,1)S(1)}, s32[16]{0:T(128)S(1)}) custom-call(s32[32]{0:T(128)S(1)} %copy-done, bf16[16,992,128]{2,1,0:T(8,128)(2,1)} %all_to_all.10.near, bf16[16,992,128]{2,1,0:T(8,128)(2,1)} %collective-permute-done.4.far, f32[3584,128]{1,0:T(8,128)S(1)} %broadcast_in_dim.22.bias), custom_call_target="tpu_custom_call" | custom-call | tf_op jit(solution)/shard_map/attend/pallas_call | solution.py:321
  136.8 18.1 %all_to_all.11.back = bf16[16,256,128]{2,1,0:T(8,128)(2,1)S(1)} all-to-all(bf16[16,256,128]{2,1,0:T(8,128)(2,1)S(1)} %get-tuple-element.12), channel_id=1, replica_groups=mesh['tm'=16,'ha'=8] {'tm'}, dimensions={0} | all-to-all | bytes 2097152 | tf_op jit(solution)/shard_map/all_to_all | solution.py:462
  155.0 3.2 %collective-permute-start.5 = (bf16[6,256,128]{2,1,0:T(8,128)(2,1)S(1)}, bf16[6,256,128]{2,1,0:T(8,128)(2,1)S(1)}, u32[]{:S(2)}, u32[]{:S(2)}) collective-permute-start(bf16[6,256,128]{2,1,0:T(8,128)(2,1)S(1)} %constant_dynamic-slice_fusion), channel_id=1, source_target_pairs={{0,1},{1,0},{2,3},{3,2},{4,5},{5,4},{6,7},{7,6},{8,9},{9,8},{10,11... | collective-permute-start | bytes 1179656 | tf_op jit(solution)/shard_map/ppermute | solution.py:367
  158.2 1.3 collective-permute-done.5.come
  159.6 1.6 finish.1
  (15 shorter events, 0.2 us)
Async XLA Ops:
  10.4 4.2 %collective-permute-start = (bf16[6,768,128]{2,1,0:T(8,128)(2,1)}, bf16[6,768,128]{2,1,0:T(8,128)(2,1)S(1)}, u32[]{:S(2)}, u32[]{:S(2)}) collective-permute-start(bf16[6,768,128]{2,1,0:T(8,128)(2,1)} %get-tuple-element.10), channel_id=1, source_target_pairs={{0,1},{1,0},{2,3},{3,2},{4,5},{5,4},{6,7},{7,6},{8,9},{9,8},{10,11... | collective-permute-start | bytes 3538952 | tf_op jit(solution)/shard_map/ppermute | solution.py:367
  16.9 8.7 %collective-permute-start.1 = (bf16[2,6,2,2,16,128]{5,4,3,1,0,2:T(8,128)(2,1)S(1)}, bf16[2,6,2,2,16,128]{5,4,3,1,0,2:T(8,128)(2,1)S(1)}, u32[]{:S(2)}, u32[]{:S(2)}) collective-permute-start(bf16[2,6,2,2,16,128]{5,4,3,1,0,2:T(8,128)(2,1)S(1)} %pad_maximum_fusion), channel_id=1, source_target_pairs={{0,4},{1,5},{2,6},{3,7},{4,0},{5,1},{6,2},{7,3},{8,12},{9,13},{10,... | collective-permute-start | bytes 589832 | tf_op jit(solution)/shard_map/ppermute | solution.py:371
  22.3 5.8 %collective-permute-start.2 = (bf16[6,2,16,2,128]{4,3,2,1,0:T(2,128)(2,1)S(1)}, bf16[6,2,16,2,128]{4,3,2,1,0:T(2,128)(2,1)S(1)}, u32[]{:S(2)}, u32[]{:S(2)}) collective-permute-start(bf16[6,2,16,2,128]{4,3,2,1,0:T(2,128)(2,1)S(1)} %bitcast.35), channel_id=1, source_target_pairs={{0,2},{1,3},{2,0},{3,1},{4,6},{5,7},{6,4},{7,5},{8,10},{9,11},{10,... | collective-permute-start | bytes 294920 | tf_op jit(solution)/shard_map/ppermute | solution.py:371
  23.1 3.8 %collective-permute-start.3 = (bf16[6,2,2,2,128]{4,3,2,1,0:T(2,128)(2,1)S(1)}, bf16[6,2,2,2,128]{4,3,2,1,0:T(2,128)(2,1)S(1)}, u32[]{:S(2)}, u32[]{:S(2)}) collective-permute-start(bf16[6,2,2,2,128]{4,3,2,1,0:T(2,128)(2,1)S(1)} %broadcast_select_fusion.1), channel_id=1, source_target_pairs={{0,6},{1,7},{2,4},{3,5},{4,2},{5,3},{6,0},{7,1},{8,14},{9,15},{10,... | collective-permute-start | bytes 36872 | tf_op jit(solution)/shard_map/ppermute | solution.py:371
  29.8 64.6 %copy-start = (s32[32]{0:T(128)S(1)}, s32[32]{0:T(128)}, u32[]{:S(2)}) copy-start(s32[32]{0:T(128)} %info.3) | copy-start | bytes 388
  84.3 9.6 %collective-permute-start.4 = (bf16[16,992,128]{2,1,0:T(8,128)(2,1)}, bf16[16,992,128]{2,1,0:T(8,128)(2,1)}, u32[]{:S(2)}, u32[]{:S(2)}) collective-permute-start(bf16[16,992,128]{2,1,0:T(8,128)(2,1)} %all_to_all.10.near), channel_id=1, source_target_pairs={{0,1},{1,0},{2,3},{3,2},{4,5},{5,4},{6,7},{7,6},{8,9},{9,8},{10,11... | collective-permute-start | bytes 12189704 | tf_op jit(solution)/shard_map/ppermute | solution.py:367
  155.0 4.6 %collective-permute-start.5 = (bf16[6,256,128]{2,1,0:T(8,128)(2,1)S(1)}, bf16[6,256,128]{2,1,0:T(8,128)(2,1)S(1)}, u32[]{:S(2)}, u32[]{:S(2)}) collective-permute-start(bf16[6,256,128]{2,1,0:T(8,128)(2,1)S(1)} %constant_dynamic-slice_fusion), channel_id=1, source_target_pairs={{0,1},{1,0},{2,3},{3,2},{4,5},{5,4},{6,7},{7,6},{8,9},{9,8},{10,11... | collective-permute-start | bytes 1179656 | tf_op jit(solution)/shard_map/ppermute | solution.py:367
